TPU v7x, 512 devices: a whole 4x4x16 slice. The times are simulated.
512 devices in a mesh: gx: 4 (over y), gy: 16 (over z_lo, core), gz: 8 (over x, z_hi).
Axes of the slice: x: 4, y: 4, z: 16 (z_hi: 2, z_lo: 8; z = z_hi * 8 + z_lo), core: 2. Of those that a mesh axis runs over, the one named last changes fastest.
Arguments:
- mixture_fractions: float32 [4, 128, 768, 512], P(None, 'gy', 'gz', 'gx'), may hold values from 0 to 1
- velocity: float32 [3, 128, 768, 512], P(None, 'gy', 'gz', 'gx'), may hold values from -3 to 3
Outputs:
- updated: float32 [4, 128, 768, 512], P(None, 'gy', 'gz', 'gx')
- gram: float32 [512, 512], P('gx')
All inputs are finite; a program needn't handle non-finite values.
Results may differ from a plain program's by a relative error of at most 0.00005.
Values sent between devices are 32-bit elements; how exact they have to be, the bound alone decides.
No kernel may reach another device: no remote copies, remote signals or barrier semaphores. Data moves between devices by JAX's collectives and lax.ppermute only.
A program may use at most 64 MiB of HBM per device.

v0:
```python
import jax
import jax.numpy as jnp
from jax import lax
from jax.sharding import PartitionSpec as P

leading_weight = (4.0 / 5.0, -1.0 / 5.0, 4.0 / 105.0, -1.0 / 280.0)
second_coef = (-205.0 / 72.0, 8.0 / 5.0, -1.0 / 5.0, 8.0 / 315.0, -1.0 / 560.0)


def padded(block, sides, width):
    for axis, dim in sides:
        count = lax.axis_size(axis)
        forward = [(i, i + 1) for i in range(count - 1)]
        forward.append((count - 1, 0))
        backward = [(target, source) for source, target in forward]
        low = lax.ppermute(
            lax.slice_in_dim(block, block.shape[dim] - width, None, axis=dim), axis, forward
        )
        high = lax.ppermute(lax.slice_in_dim(block, 0, width, axis=dim), axis, backward)
        block = jnp.concatenate([low, block, high], axis=dim)
    return block


def shift_amount(padded_field, axis, step, core):
    start = [0, 4, 4, 4]
    start[axis] = start[axis] + step
    limit = [start[index] + core[index] for index in range(4)]
    return lax.slice(padded_field, start, limit)


def derivs(padded_field, axis, core):
    centre = shift_amount(padded_field, axis, 0, core)
    first = jnp.zeros(core, jnp.float32)
    second_factor = second_coef[0] * centre
    for step in range(1, 5):
        ahead = shift_amount(padded_field, axis, step, core)
        behind = shift_amount(padded_field, axis, -step, core)
        first = first + leading_weight[step - 1] * (ahead - behind)
        second_factor = second_factor + second_coef[step] * (ahead + behind)
    return (first, second_factor)


def contract(left, right):
    return lax.dot_general(
        left,
        right,
        (((0,), (0,)), ((), ())),
        precision=lax.Precision.HIGHEST,
        preferred_element_type=jnp.float32,
    )


def shards(mixture_fractions, velocity):
    core = mixture_fractions.shape
    diffusion = jnp.array([0.1, 0.12, 0.08, 0.15], jnp.float32)[:, None, None, None]
    stoichiometry = jnp.array([-1.0, -1.0, 2.0, 0.0], jnp.float32)[:, None, None, None]
    padded_field = padded(mixture_fractions, (("gx", 3), ("gy", 1), ("gz", 2)), 4)
    dx1, dx2 = derivs(padded_field, 3, core)
    dy1, dy2 = derivs(padded_field, 1, core)
    dz1, dz2 = derivs(padded_field, 2, core)
    moved = velocity[0][None] * dx1 + velocity[1][None] * dy1 + velocity[2][None] * dz1
    carried = -moved + diffusion * (dx2 + dy2 + dz2)
    heat_profile = 1.0 + 3.0 * mixture_fractions[2]
    burning_speed = 4.0 * mixture_fractions[0] * mixture_fractions[1] * jnp.exp(-3.0 / heat_profile)
    updated = mixture_fractions + 0.25 * (carried + stoichiometry * burning_speed[None])
    cells_x = core[3]
    unfold = updated.reshape(core[0] * core[1] * core[2], cells_x)
    mode_lines = lax.all_to_all(unfold, "gx", split_axis=0, concat_axis=1, tiled=True)
    whole = contract(mode_lines, mode_lines)
    rows = lax.psum_scatter(whole, "gx", scatter_dimension=0, tiled=True)
    summed = lax.psum(rows, ("gy", "gz"))
    count = core[0] * core[1] * lax.axis_size("gy") * core[2] * lax.axis_size("gz")
    gram = summed * (1.0 / count)
    return (updated, gram)


def solution(mesh):
    in_specs = (P(None, "gy", "gz", "gx"), P(None, "gy", "gz", "gx"))
    out_specs = (P(None, "gy", "gz", "gx"), P("gx", None))
    return jax.shard_map(shards, mesh=mesh, in_specs=in_specs, out_specs=out_specs, check_vma=False)
```

profile of v0, /device:TPU:1, one launch (start us, length us, event | category | flops | bytes accessed | tf_op | source)
XLA Modules:
  0.0 546.4 jit_solution(17917151886975128364)
XLA Ops:
  7.2 0.0 reduce-scatter.2.cloned.1.call-start
  7.2 2.5 fusion.10
  9.7 0.5 copy.22
  10.2 4.0 collective-permute-start.1
  14.3 0.5 copy.21
  14.8 0.0 copy-start
  14.8 3.5 collective-permute-start
  18.3 0.0 collective-permute-done.1
  18.3 0.5 copy.11
  18.8 1.1 collective-permute-done
  19.9 1.7 copy.9
  21.6 0.0 copy-done
  21.6 2.7 pad_maximum_fusion.1
  24.3 1.9 fusion.9
  26.2 3.0 copy.14
  29.1 8.7 %collective-permute-start.2 = (f32[4,4,96,136]{2,3,1,0:T(8,128)}, f32[4,4,96,136]{2,3,1,0:T(8,128)}, u32[]{:S(2)}, u32[]{:S(2)}) collective-permute-start(f32[4,4,96,136]{2,3,1,0:T(8,128)} %copy.14), channel_id=1, source_target_pairs={{8,0},{16,8},{24,16},{32,24},{40,32},{48,40},{56,48},{64,56},{72,6... | collective-permute-start | bytes 2506760 | tf_op jit(solution)/shard_map/ppermute | solution.py:19
  37.8 3.0 copy.16
  40.8 1.9 collective-permute-start.3
  42.7 2.3 slice_bitcast_fusion.2
  45.0 3.2 collective-permute-done.2
  48.1 3.0 copy.15
  51.2 16.1 %collective-permute-done.3 = f32[4,4,96,136]{2,3,1,0:T(8,128)} collective-permute-done((f32[4,4,96,136]{2,3,1,0:T(8,128)}, f32[4,4,96,136]{2,3,1,0:T(8,128)}, u32[]{:S(2)}, u32[]{:S(2)}) %collective-permute-start.3) | collective-permute-done | bytes 835616 | tf_op jit(solution)/shard_map/ppermute | solution.py:16
  67.3 3.0 copy.17
  70.3 0.0 copy-start.1
  70.3 0.0 copy-start.2
  70.3 0.0 copy-start.3
  70.3 1.6 pad_maximum_fusion.20
  71.9 8.1 %collective-permute-start.5 = (f32[4,16,4,136]{3,2,1,0:T(4,128)S(1)}, f32[4,16,4,136]{3,2,1,0:T(4,128)}, u32[]{:S(2)}, u32[]{:S(2)}) collective-permute-start(f32[4,16,4,136]{3,2,1,0:T(4,128)S(1)} %get-tuple-element.2), channel_id=1, source_target_pairs={{0,1},{1,2},{2,3},{3,4},{4,5},{5,6},{6,7},{7,0},{8,9},{9,10},{10,1... | collective-permute-start | bytes 417800 | tf_op jit(solution)/shard_map/ppermute | solution.py:16
  80.0 0.0 copy-start.4
  80.0 0.0 copy-start.5
  80.0 8.2 %collective-permute-start.4 = (f32[4,16,4,136]{3,2,1,0:T(4,128)S(1)}, f32[4,16,4,136]{3,2,1,0:T(4,128)}, u32[]{:S(2)}, u32[]{:S(2)}) collective-permute-start(f32[4,16,4,136]{3,2,1,0:T(4,128)S(1)} %get-tuple-element.3), channel_id=1, source_target_pairs={{1,0},{2,1},{3,2},{4,3},{5,4},{6,5},{7,6},{0,7},{9,8},{10,9},{11,1... | collective-permute-start | bytes 417800 | tf_op jit(solution)/shard_map/ppermute | solution.py:19
  88.2 0.0 copy-done.1
  88.2 0.0 copy-done.2
  88.2 0.0 copy-done.3
  88.3 5.6 %pad_maximum_fusion = (f32[4,12,96,136]{3,2,1,0:T(8,128)}, f32[4,12,96,136]{3,2,1,0:T(8,128)}) fusion(f32[4,4,96,136]{3,2,1,0:T(8,128)S(1)} %copy-done.2, f32[4,8,96,4]{3,2,1,0:T(8,128)S(1)} %copy-done.1, f32[4,8,96,128]{3,2,1,0:T(8,128)S(1)} %copy-done, f32[4,8,96,4]{3,2,1,0:T(8,128)S(1)} %copy.11, f32[4,4,96,136]{3,2,1,0:T(8,128)S(1)} %copy-done.3), kind=kLoop, calls=%fused_computation | loop fusion | flops 3760128 | bytes 8355840 | tf_op jit(solution)/shard_map/concatenate | solution.py:20
  93.9 0.0 collective-permute-done.5
  93.9 16.1 %collective-permute-done.4 = f32[4,16,4,136]{3,2,1,0:T(4,128)} collective-permute-done((f32[4,16,4,136]{3,2,1,0:T(4,128)S(1)}, f32[4,16,4,136]{3,2,1,0:T(4,128)}, u32[]{:S(2)}, u32[]{:S(2)}) %collective-permute-start.4) | collective-permute-done | bytes 139296 | tf_op jit(solution)/shard_map/ppermute | solution.py:19
  110.0 0.0 copy-done.4
  110.0 0.0 copy-done.5
  110.0 20.6 %multiply_add_fusion = f32[4,8,96,128]{3,2,1,0:T(8,128)} fusion(f32[4,8,96,128]{3,2,1,0:T(8,128)S(1)} %copy-done, f32[4,16,4,136]{3,2,1,0:T(4,128)} %collective-permute-done.4, f32[4,4,96,136]{3,2,1,0:T(8,128)} %copy.15, f32[4,8,96,4]{3,2,1,0:T(8,128)} %copy.9, f32[4,8,96,4]{3,2,1,0:T(8,128)S(1)} %copy.11, f32[4,4,96,136]{3,2,1,0:T(8,128)} %copy.17, ...), kind=kLoop, calls=%fused_computation.39 | loop fusion | flops 51904512 | bytes 19349536 | tf_op jit(solution)/shard_map/add | solution.py:65
  130.6 23.0 %all_to_all.19 = f32[4,768,128]{2,1,0:T(8,128)S(1)} all-to-all(f32[4,768,128]{2,1,0:T(8,128)} %bitcast.14), channel_id=1, replica_groups=mesh['gx'=4,'gy'=16,'gz'=8] {'gx'}, dimensions={0} | all-to-all | bytes 3145728 | tf_op jit(solution)/shard_map/all_to_all | solution.py:68
  153.6 0.5 copy.20
  154.1 3.7 fusion.11
  157.8 0.0 reduce-scatter.2.cloned.1.call-update
  157.8 0.0 all-reduce.2.cloned.1.call-start
  157.8 47.2 %reduce-scatter.2.cloned.1.call-done = f32[128,512]{1,0:T(8,128)} async-done(((f32[512,512]{1,0:T(8,128)}), f32[128,512]{1,0:T(8,128)}) %reduce-scatter.2.cloned.1.call-update) | async-done | bytes 262160 | tf_op jit(solution)/shard_map/reduce_scatter | solution.py:70
  205.1 0.0 all-reduce.2.cloned.1.call-update
  205.1 332.8 %all-reduce.2.cloned.1.call-done = f32[128,512]{1,0:T(8,128)} async-done(((f32[128,512]{1,0:T(8,128)}), f32[128,512]{1,0:T(8,128)}) %all-reduce.2.cloned.1.call-update) | async-done | bytes 262160 | tf_op jit(solution)/shard_map/psum | solution.py:71
  537.8 1.7 broadcast_multiply_fusion
Async XLA Ops:
  7.2 197.9 %reduce-scatter.2.cloned.1.call-start = ((), (), s32[]{:S(2)}) async-start(), calls=%async_computation.2 | async-start | bytes 1310720 | tf_op jit(solution)/shard_map/reduce_scatter | solution.py:70
  10.2 8.0 %collective-permute-start.1 = (f32[4,8,96,4]{2,1,3,0:T(8,128)S(1)}, f32[4,8,96,4]{2,1,3,0:T(8,128)S(1)}, u32[]{:S(2)}, u32[]{:S(2)}) collective-permute-start(f32[4,8,96,4]{2,1,3,0:T(8,128)S(1)} %copy.22), channel_id=1, source_target_pairs={{0,128},{128,256},{256,384},{384,0},{1,129},{129,257},{257,385},{3... | collective-permute-start | bytes 147464 | tf_op jit(solution)/shard_map/ppermute | solution.py:16
  14.8 6.8 %copy-start = (f32[4,8,96,128]{3,2,1,0:T(8,128)S(1)}, f32[4,8,96,128]{3,2,1,0:T(8,128)}, u32[]{:S(2)}) copy-start(f32[4,8,96,128]{3,2,1,0:T(8,128)} %param.4) | copy-start | bytes 4718596
  14.8 5.1 collective-permute-start
  29.1 19.0 %collective-permute-start.2 = (f32[4,4,96,136]{2,3,1,0:T(8,128)}, f32[4,4,96,136]{2,3,1,0:T(8,128)}, u32[]{:S(2)}, u32[]{:S(2)}) collective-permute-start(f32[4,4,96,136]{2,3,1,0:T(8,128)} %copy.14), channel_id=1, source_target_pairs={{8,0},{16,8},{24,16},{32,24},{40,32},{48,40},{56,48},{64,56},{72,6... | collective-permute-start | bytes 2506760 | tf_op jit(solution)/shard_map/ppermute | solution.py:19
  40.8 26.5 %collective-permute-start.3 = (f32[4,4,96,136]{2,3,1,0:T(8,128)}, f32[4,4,96,136]{2,3,1,0:T(8,128)}, u32[]{:S(2)}, u32[]{:S(2)}) collective-permute-start(f32[4,4,96,136]{2,3,1,0:T(8,128)} %copy.16), channel_id=1, source_target_pairs={{0,8},{8,16},{16,24},{24,32},{32,40},{40,48},{48,56},{56,64},{64,7... | collective-permute-start | bytes 2506760 | tf_op jit(solution)/shard_map/ppermute | solution.py:16
  70.3 17.9 %copy-start.1 = (f32[4,8,96,4]{3,2,1,0:T(8,128)S(1)}, f32[4,8,96,4]{3,2,1,0:T(8,128)}, u32[]{:S(2)}) copy-start(f32[4,8,96,4]{3,2,1,0:T(8,128)} %copy.9) | copy-start | bytes 147460
  70.3 17.9 %copy-start.2 = (f32[4,4,96,136]{3,2,1,0:T(8,128)S(1)}, f32[4,4,96,136]{3,2,1,0:T(8,128)}, u32[]{:S(2)}) copy-start(f32[4,4,96,136]{3,2,1,0:T(8,128)} %copy.15) | copy-start | bytes 2506756
  70.3 17.9 %copy-start.3 = (f32[4,4,96,136]{3,2,1,0:T(8,128)S(1)}, f32[4,4,96,136]{3,2,1,0:T(8,128)}, u32[]{:S(2)}) copy-start(f32[4,4,96,136]{3,2,1,0:T(8,128)} %copy.17) | copy-start | bytes 2506756
  71.9 22.0 %collective-permute-start.5 = (f32[4,16,4,136]{3,2,1,0:T(4,128)S(1)}, f32[4,16,4,136]{3,2,1,0:T(4,128)}, u32[]{:S(2)}, u32[]{:S(2)}) collective-permute-start(f32[4,16,4,136]{3,2,1,0:T(4,128)S(1)} %get-tuple-element.2), channel_id=1, source_target_pairs={{0,1},{1,2},{2,3},{3,4},{4,5},{5,6},{6,7},{7,0},{8,9},{9,10},{10,1... | collective-permute-start | bytes 417800 | tf_op jit(solution)/shard_map/ppermute | solution.py:16
  80.0 30.0 %copy-start.4 = (f32[4]{0:T(128)S(1)}, f32[4]{0:T(128)}, u32[]{:S(2)}) copy-start(f32[4]{0:T(128)} %constant.33.clone) | copy-start | bytes 52
  80.0 30.0 %copy-start.5 = (f32[4]{0:T(128)S(1)}, f32[4]{0:T(128)}, u32[]{:S(2)}) copy-start(f32[4]{0:T(128)} %constant.32.clone) | copy-start | bytes 52
  80.0 30.0 %collective-permute-start.4 = (f32[4,16,4,136]{3,2,1,0:T(4,128)S(1)}, f32[4,16,4,136]{3,2,1,0:T(4,128)}, u32[]{:S(2)}, u32[]{:S(2)}) collective-permute-start(f32[4,16,4,136]{3,2,1,0:T(4,128)S(1)} %get-tuple-element.3), channel_id=1, source_target_pairs={{1,0},{2,1},{3,2},{4,3},{5,4},{6,5},{7,6},{0,7},{9,8},{10,9},{11,1... | collective-permute-start | bytes 417800 | tf_op jit(solution)/shard_map/ppermute | solution.py:19
  157.8 380.0 %all-reduce.2.cloned.1.call-start = ((), (), s32[]{:S(2)}) async-start(), calls=%async_computation.3 | async-start | bytes 524288 | tf_op jit(solution)/shard_map/psum | solution.py:71
Sparse Core Ops, SparseCore 0:
  157.9 47.0 reduce-scatter.1
  208.9 328.8 all-reduce.1
where the time goes:
time: 547 us; the launch traced here: 546 us
  waiting for transfers between devices  417 us (76%)
  other arithmetic  34.5 us (6%)
  starting transfers between devices  34.4 us (6%)
  blocking collectives  23 us (4%)
  local copies, waits for them, and re-layouts  20 us (4%)
  between operations  14.2 us (3%)
    psum x1, waiting for transfers between devices, shards(): summed = lax.psum(rows, ('gy', 'gz'))  333 us
    reduce_scatter x1, waiting for transfers between devices, shards(): rows = lax.psum_scatter(whole, 'gx', scatter_dimension=0, tiled=True)  47.2 us
    all_to_all x1, blocking collectives, shards(): lax.all_to_all(unfold, 'gx', split_axis=0, concat_axis=1, tiled=True)  23 us
    add x1, other arithmetic, shards(): mixture_fractions + 0.25 * (carried + stoichiometry * burning_speed[None])  20.6 us
    ppermute x3, waiting for transfers between devices, padded(): lax.ppermute(lax.slice_in_dim(block, 0, width, axis=dim), axis, backward)  20.4 us
    ppermute x3, starting transfers between devices, padded(): lax.ppermute(lax.slice_in_dim(block, 0, width, axis=dim), axis, backward)  20.4 us
    ppermute x3, waiting for transfers between devices, padded(): lax.ppermute(lax.slice_in_dim(block, block.shape[dim] - width, None, axis...  16.1 us
    ppermute x3, starting transfers between devices, padded(): lax.ppermute(lax.slice_in_dim(block, block.shape[dim] - width, None, axis...  14 us
  transfers between devices with their start and end apart: 8, of which 6 were waited for; matrix products, arithmetic and copies ran while one was open for 3% of the time, Pallas kernels for 0%

commit v1 on v0

v1 whole, which is shorter than its diff:
```python
import numpy as np
import jax
import jax.numpy as jnp
from jax import lax
from jax.experimental import pallas as pl
from jax.experimental.pallas import tpu as pltpu
from jax.sharding import Mesh, PartitionSpec as P

C1 = (4.0 / 5.0, -1.0 / 5.0, 4.0 / 105.0, -1.0 / 280.0)
C2 = (-205.0 / 72.0, 8.0 / 5.0, -1.0 / 5.0, 8.0 / 315.0, -1.0 / 560.0)
DIFF = (0.10, 0.12, 0.08, 0.15)
NU = (-1.0, -1.0, 2.0, 0.0)
PAIRS = [(a, b) for a in range(4) for b in range(a, 4)]
MIB = 1 << 20


def split(value):
    high = value.astype(jnp.bfloat16)
    return high, (value - high.astype(jnp.float32)).astype(jnp.bfloat16)


def x_matrix(width):
    matrix = np.zeros((2 * width, 2 * width))
    for i in range(width):
        for k in range(-4, 5):
            j = i + k
            row = j if 0 <= j < width else (width + 4 + j if j < 0 else width + 4 + j - width)
            if k:
                matrix[row, i] += np.sign(k) * C1[abs(k) - 1]
            matrix[row, width + i] += C2[abs(k)]
    return jnp.asarray(matrix, jnp.float32)


def dot(left, right):
    return lax.dot_general(
        left, right, (((1,), (0,)), ((), ())), preferred_element_type=jnp.float32
    )


def stencil_body(y, vel, ylow, yhigh, zlow, zhigh, xlow, xhigh, mh, ml, out, rate, side, dx, pad):
    count, rows, depth, width = y.shape
    side[...] = jnp.zeros_like(side)
    for j in range(rows):
        heat = 1.0 + 3.0 * y[2, j]
        rate[j] = y[0, j] * y[1, j] * jnp.exp(-3.0 / heat)

    def species(s, carry):
        diff = jnp.float32(0.25 * DIFF[0])
        nu = jnp.float32(NU[0])
        for q in range(1, count):
            diff = jnp.where(s == q, jnp.float32(0.25 * DIFF[q]), diff)
            nu = jnp.where(s == q, jnp.float32(NU[q]), nu)
        for j in range(rows):
            both = jnp.concatenate([xlow[s, j], xhigh[s, j]], axis=0)
            side[j * depth : (j + 1) * depth, 0:8] = both.T[:depth]
        left = jnp.concatenate([y[s].reshape(rows * depth, width), side[...]], axis=1)
        high, low = split(left)
        dx[...] = dot(high, mh[...]) + (dot(low, mh[...]) + dot(high, ml[...]))
        for j in range(rows):

            def layer(t):
                if t < 0:
                    return ylow[s, 4 + t]
                return y[s, t] if t < rows else yhigh[s, t - rows]

            slot = j % 2
            centre = y[s, j]
            pad[slot, 4:8] = zlow[s, j]
            pad[slot, 8 : 8 + depth] = centre
            pad[slot, 8 + depth : 12 + depth] = zhigh[s, j]
            d1y = d1z = None
            second = (2.0 * C2[0]) * centre + dx[j * depth : (j + 1) * depth, width:]
            for k in range(1, 5):
                ya, yb = layer(j + k), layer(j - k)
                za = pad[slot, 8 + k : 8 + k + depth]
                zb = pad[slot, 8 - k : 8 - k + depth]
                ty, tz = C1[k - 1] * (ya - yb), C1[k - 1] * (za - zb)
                d1y = ty if d1y is None else d1y + ty
                d1z = tz if d1z is None else d1z + tz
                second = second + C2[k] * ((ya + yb) + (za + zb))
            moved = vel[0, j] * dx[j * depth : (j + 1) * depth, :width]
            moved = moved + vel[1, j] * d1y + vel[2, j] * d1z
            out[s, j] = centre + (diff * second - 0.25 * moved + nu * rate[j])
        return carry

    lax.fori_loop(0, count, species, 0)


def stencil(y, vel, *rest):
    _, rows, depth, width = y.shape
    return pl.pallas_call(
        stencil_body,
        out_shape=jax.ShapeDtypeStruct(y.shape, jnp.float32),
        in_specs=[pl.BlockSpec(memory_space=pltpu.VMEM)] * 10,
        out_specs=pl.BlockSpec(memory_space=pltpu.VMEM),
        scratch_shapes=[
            pltpu.VMEM((rows, depth, width), jnp.float32),
            pltpu.VMEM((rows * depth, width), jnp.float32),
            pltpu.VMEM((rows * depth, 2 * width), jnp.float32),
            pltpu.VMEM((2, depth + 16, width), jnp.float32),
        ],
        compiler_params=pltpu.CompilerParams(vmem_limit_bytes=40 * MIB),
        name="stencil",
    )(y, vel, *rest)


def gram_body(lines, out):
    parts = lines.shape[0]
    whole = jnp.concatenate([lines[a] for a in range(parts)], axis=1)
    high, low = split(whole)
    turned_high, turned_low = split(whole.T)
    total = dot(turned_high, high) + (dot(turned_high, low) + dot(turned_low, high))
    for p, (a, b) in enumerate(PAIRS):
        out[p * 128 : (p + 1) * 128] = total[a * 128 : (a + 1) * 128, b * 128 : (b + 1) * 128]


def gram_blocks(lines):
    return pl.pallas_call(
        gram_body,
        out_shape=jax.ShapeDtypeStruct((len(PAIRS) * 128, 128), jnp.float32),
        in_specs=[pl.BlockSpec(memory_space=pltpu.VMEM)],
        out_specs=pl.BlockSpec(memory_space=pltpu.VMEM),
        compiler_params=pltpu.CompilerParams(vmem_limit_bytes=40 * MIB),
        name="gram",
    )(lines)


def rows_body(scale, place, blocks, out):
    mine = place[0]
    for b in range(4):
        low, top = jnp.minimum(mine, b), jnp.maximum(mine, b)
        index = low * 4 - (low * (low - 1)) // 2 + (top - low)
        tile = blocks[pl.ds(pl.multiple_of(index * 128, 128), 128)] * scale
        out[:, b * 128 : (b + 1) * 128] = jnp.where(mine <= b, tile, tile.T)


def gram_rows(blocks, place, scale):
    import functools

    return pl.pallas_call(
        functools.partial(rows_body, scale),
        out_shape=jax.ShapeDtypeStruct((128, 512), jnp.float32),
        in_specs=[
            pl.BlockSpec(memory_space=pltpu.SMEM),
            pl.BlockSpec(memory_space=pltpu.VMEM),
        ],
        out_specs=pl.BlockSpec(memory_space=pltpu.VMEM),
        name="gram_rows",
    )(place, blocks)


def exchange(pieces, axes):
    return lax.all_to_all(pieces, axes, split_axis=0, concat_axis=0, tiled=True)


def shards(y, vel):
    species, rows, depth, width = y.shape
    gy, gz, gx = ("zlo", "core"), ("x", "zhi"), ("gx",)

    def moves(axes, count):
        up = [(i, (i + 1) % count) for i in range(count)]
        return up, [(target, source) for source, target in up]

    up, down = moves(gz, 8)
    zlow = lax.ppermute(y[:, :, depth - 4 :], gz, up)
    zhigh = lax.ppermute(y[:, :, :4], gz, down)
    up, down = moves(gy, 16)
    ylow = lax.ppermute(y[:, rows - 4 :], gy, up)
    yhigh = lax.ppermute(y[:, :4], gy, down)
    up, down = moves(gx, 4)

    def face(part):
        turned = jnp.transpose(part, (0, 1, 3, 2))
        return jnp.pad(turned, ((0, 0), (0, 0), (0, 0), (0, 128 - depth)))

    xlow = lax.ppermute(face(y[..., width - 4 :]), gx, up)
    xhigh = lax.ppermute(face(y[..., :4]), gx, down)
    mh, ml = split(x_matrix(width))
    updated = stencil(y, vel, ylow, yhigh, zlow, zhigh, xlow, xhigh, mh, ml)

    lines = exchange(updated.reshape(4, species * rows * depth // 4, width), gx)
    blocks = gram_blocks(lines)
    plane, column = ("gx", "core", "x"), ("zlo", "zhi")
    part = jnp.sum(exchange(blocks.reshape(32, -1, 128), plane), axis=0)
    part = jnp.sum(exchange(jnp.broadcast_to(part, (16,) + part.shape), column), axis=0)
    blocks = exchange(jnp.broadcast_to(part, (32,) + part.shape), plane)
    place = lax.axis_index("gx").astype(jnp.int32).reshape(1)
    cells = species * rows * 16 * depth * 8
    return updated, gram_rows(blocks.reshape(-1, 128), place, 1.0 / cells)


def solution(mesh):
    fine = Mesh(mesh.devices.reshape(4, 8, 2, 4, 2), ("gx", "zlo", "core", "x", "zhi"))
    grid = P(None, ("zlo", "core"), ("x", "zhi"), "gx")
    return jax.shard_map(
        shards, mesh=fine, in_specs=(grid, grid), out_specs=(grid, P("gx", None)), check_vma=False
    )
```

time: 547 us -> 163 us (0.30)
  waiting for transfers between devices: 417 us -> 21.2 us
  blocking collectives: 23 us -> 70 us
  other arithmetic: 34.5 us -> 0.08 us
  between operations: 14.2 us -> 0.78 us
  Pallas kernels: 0 us -> 10 us
  starting transfers between devices: 34.4 us -> 42.6 us
    psum x1 -> x0, waiting for transfers between devices: 333 us -> none  [shards(): summed = lax.psum(rows, ('gy', 'gz'))]
    reduce_scatter x1 -> x0, waiting for transfers between devices: 47.2 us -> none  [shards(): rows = lax.psum_scatter(whole, 'gx', scatter_dimension=0, tiled=True)]
    all_to_all x1 -> x3, blocking collectives: 23 us -> 70 us  [exchange(): return lax.all_to_all(pieces, axes, split_axis=0, concat_axis=0, tiled=True)]
    ppermute x6, waiting for transfers between devices: 36.5 us -> 8.66 us  [the longest x1 8.65 us: shards(): zhigh = lax.ppermute(y[:, :, :4], gz, down)]
    add x1 -> x0, other arithmetic: 20.6 us -> none  [shards(): mixture_fractions + 0.25 * (carried + stoichiometry * burning_speed[None])]
    all_to_all x0 -> x1, waiting for transfers between devices: none -> 12.5 us  [exchange(): return lax.all_to_all(pieces, axes, split_axis=0, concat_axis=0, tiled=True)]
    pallas_call x0 -> x3, Pallas kernels: none -> 10 us  [the longest x1 6.63 us: stencil(): pl.pallas_call(stencil_body, out_shape=jax.ShapeDtypeStruct(y.shape, jnp....]
    concatenate x3 -> x0, other arithmetic: 9.96 us -> none  [padded(): block = jnp.concatenate([low, block, high], axis=dim)]
  transfers between devices with their start and end apart: 8 -> 7, of which waited for: 6 -> 2; matrix products, arithmetic and copies ran while one was open for 3% -> 6% of each run, Pallas kernels for 0% -> 0%
where the time goes in v1:
time: 163 us; the launch traced here: 161 us
  blocking collectives  70 us (43%)
  starting transfers between devices  42.6 us (26%)
  waiting for transfers between devices  21.2 us (13%)
  local copies, waits for them, and re-layouts  16.1 us (10%)
  Pallas kernels  10 us (6%)
    all_to_all x3, blocking collectives, exchange(): return lax.all_to_all(pieces, axes, split_axis=0, concat_axis=0, tiled=True)  70 us
    all_to_all x1, waiting for transfers between devices, exchange(): return lax.all_to_all(pieces, axes, split_axis=0, concat_axis=0, tiled=True)  12.5 us
    ppermute x1, starting transfers between devices, shards(): zlow = lax.ppermute(y[:, :, depth - 4:], gz, up)  10.8 us
    all_to_all x1, starting transfers between devices, exchange(): return lax.all_to_all(pieces, axes, split_axis=0, concat_axis=0, tiled=True)  9.34 us
    ppermute x1, waiting for transfers between devices, shards(): zhigh = lax.ppermute(y[:, :, :4], gz, down)  8.65 us
    unnamed x12, local copies, waits for them, and re-layouts  7.82 us
    pallas_call x1, Pallas kernels, stencil(): pl.pallas_call(stencil_body, out_shape=jax.ShapeDtypeStruct(y.shape, jnp....  6.63 us
    ppermute x1, starting transfers between devices, shards(): yhigh = lax.ppermute(y[:, :4], gy, down)  5.77 us
  transfers between devices with their start and end apart: 7, of which 2 were waited for; matrix products, arithmetic and copies ran while one was open for 6% of the time, Pallas kernels for 0%

profile of v1, /device:TPU:1, one launch (start us, length us, event | category | flops | bytes accessed | tf_op | source)
XLA Modules:
  0.0 160.8 jit_solution(7271420071489481586)
XLA Ops:
  0.6 0.0 copy-start
  0.6 2.8 %fusion.2 = (f32[4,4,96,128]{3,2,1,0:T(8,128)}, f32[4,4,96,128]{3,2,1,0:T(8,128)}) fusion(f32[4,8,96,128]{3,2,1,0:T(8,128)} %y.5), kind=kLoop, calls=%fused_computation.2 | loop fusion | bytes 3145728 | tf_op jit(solution)/shard_map/slice | solution.py:169
  3.4 4.9 %collective-permute-start = (f32[4,4,96,128]{3,2,1,0:T(8,128)}, f32[4,4,96,128]{3,2,1,0:T(8,128)S(1)}, u32[]{:S(2)}, u32[]{:S(2)}) collective-permute-start(f32[4,4,96,128]{3,2,1,0:T(8,128)} %get-tuple-element.7), channel_id=1, source_target_pairs={{0,8},{8,16},{16,24},{24,32},{32,40},{40,48},{48,56},{56,64},{64,7... | collective-permute-start | bytes 2359304 | tf_op jit(solution)/shard_map/ppermute | solution.py:168
  8.3 5.8 %collective-permute-start.1 = (f32[4,4,96,128]{3,2,1,0:T(8,128)}, f32[4,4,96,128]{3,2,1,0:T(8,128)}, u32[]{:S(2)}, u32[]{:S(2)}) collective-permute-start(f32[4,4,96,128]{3,2,1,0:T(8,128)} %get-tuple-element.6), channel_id=1, source_target_pairs={{8,0},{16,8},{24,16},{32,24},{40,32},{48,40},{56,48},{64,56},{72,6... | collective-permute-start | bytes 2359304 | tf_op jit(solution)/shard_map/ppermute | solution.py:169
  14.1 0.0 copy-done
  14.1 2.2 %fusion = (f32[4,8,96,4]{3,2,1,0:T(8,128)}, f32[4,8,96,4]{3,2,1,0:T(8,128)}) fusion(f32[4,8,96,128]{3,2,1,0:T(8,128)S(1)} %copy-done), kind=kLoop, calls=%fused_computation | loop fusion | bytes 196608 | tf_op jit(solution)/shard_map/slice | solution.py:177
  16.4 0.0 copy-start.1
  16.4 2.6 %copy.9 = f32[4,8,96,4]{2,3,1,0:T(4,128)} copy(f32[4,8,96,4]{3,2,1,0:T(8,128)} %get-tuple-element.3) | data formatting | bytes 98304
  19.0 1.5 pad.7
  20.5 1.9 %collective-permute-start.4 = (f32[4,8,4,128]{3,2,1,0:T(4,128)}, f32[4,8,4,128]{3,2,1,0:T(4,128)}, u32[]{:S(2)}, u32[]{:S(2)}) collective-permute-start(f32[4,8,4,128]{3,2,1,0:T(4,128)} %pad.7), channel_id=1, source_target_pairs={{0,128},{128,256},{256,384},{384,0},{1,129},{129,257},{257,385},{3... | collective-permute-start | bytes 196616 | tf_op jit(solution)/shard_map/ppermute | solution.py:176
  22.4 2.5 %copy.10 = f32[4,8,96,4]{2,3,1,0:T(4,128)} copy(f32[4,8,96,4]{3,2,1,0:T(8,128)} %get-tuple-element.2) | data formatting | bytes 98304
  24.9 0.9 pad.8
  25.8 4.6 %collective-permute-start.5 = (f32[4,8,4,128]{3,2,1,0:T(4,128)S(1)}, f32[4,8,4,128]{3,2,1,0:T(4,128)S(1)}, u32[]{:S(2)}, u32[]{:S(2)}) collective-permute-start(f32[4,8,4,128]{3,2,1,0:T(4,128)S(1)} %pad.8), channel_id=1, source_target_pairs={{128,0},{256,128},{384,256},{0,384},{129,1},{257,129},{385,257},{1... | collective-permute-start | bytes 196616 | tf_op jit(solution)/shard_map/ppermute | solution.py:177
  30.4 10.8 %collective-permute-start.2 = (f32[4,8,4,128]{3,2,1,0:T(4,128)S(1)}, f32[4,8,4,128]{3,2,1,0:T(4,128)S(1)}, u32[]{:S(2)}, u32[]{:S(2)}) collective-permute-start(f32[4,8,4,128]{3,2,1,0:T(4,128)S(1)} %get-tuple-element.5), channel_id=1, source_target_pairs={{0,1},{1,2},{2,3},{3,4},{4,5},{5,6},{6,7},{7,0},{8,9},{9,10},{10,1... | collective-permute-start | bytes 196616 | tf_op jit(solution)/shard_map/ppermute | solution.py:165
  41.1 0.0 collective-permute-done.4.xlow
  41.2 5.3 %collective-permute-start.3 = (f32[4,8,4,128]{3,2,1,0:T(4,128)S(1)}, f32[4,8,4,128]{3,2,1,0:T(4,128)S(1)}, u32[]{:S(2)}, u32[]{:S(2)}) collective-permute-start(f32[4,8,4,128]{3,2,1,0:T(4,128)S(1)} %get-tuple-element.4), channel_id=1, source_target_pairs={{1,0},{2,1},{3,2},{4,3},{5,4},{6,5},{7,6},{0,7},{9,8},{10,9},{11,1... | collective-permute-start | bytes 196616 | tf_op jit(solution)/shard_map/ppermute | solution.py:166
  46.5 0.0 collective-permute-done.5.xhigh
  46.5 0.0 collective-permute-done.2.zlow
  46.5 8.6 %collective-permute-done.3.zhigh = f32[4,8,4,128]{3,2,1,0:T(4,128)S(1)} collective-permute-done((f32[4,8,4,128]{3,2,1,0:T(4,128)S(1)}, f32[4,8,4,128]{3,2,1,0:T(4,128)S(1)}, u32[]{:S(2)}, u32[]{:S(2)}) %collective-permute-start.3) | collective-permute-done | bytes 65568 | tf_op jit(solution)/shard_map/ppermute | solution.py:166
  55.2 0.0 collective-permute-done.ylow
  55.2 0.0 collective-permute-done.1.yhigh
  55.2 0.0 copy-done.1
  55.2 0.0 copy-start.2
  55.2 0.9 copy-done.2
  56.1 0.0 copy-start.3
  56.1 0.9 copy-done.3
  57.0 6.6 %stencil.1 = f32[4,8,96,128]{3,2,1,0:T(8,128)} custom-call(f32[4,8,96,128]{3,2,1,0:T(8,128)S(1)} %copy-done, f32[3,8,96,128]{3,2,1,0:T(8,128)S(1)} %copy-done.1, f32[4,4,96,128]{3,2,1,0:T(8,128)S(1)} %collective-permute-done.ylow, f32[4,4,96,128]{3,2,1,0:T(8,128)} %collective-permute-done.1.yhigh, f32[4,8,4,128]{3,2,1,0:T(4,128)S(1)} %collective-permute-done.2.zlow, ...), custom_call_target="tpu_custom_call" | custom-call | tf_op jit(solution)/shard_map/stencil/pallas_call | solution.py:91
  63.6 16.1 %all_to_all.20.lines = f32[4,768,128]{2,1,0:T(8,128)S(1)} all-to-all(f32[4,768,128]{2,1,0:T(8,128)} %bitcast.7), channel_id=1, replica_groups=mesh['gx'=4,'zlo'=8,'core'=2,'x'=4,'zhi'=2] {'gx'}, dimensions={0} | all-to-all | bytes 3145728 | tf_op jit(solution)/shard_map/all_to_all | solution.py:153
  79.7 1.5 gram.1
  81.2 27.9 %all_to_all.21 = f32[32,40,128]{2,1,0:T(8,128)S(1)} all-to-all(f32[32,40,128]{2,1,0:T(8,128)S(1)} %bitcast.6), channel_id=1, replica_groups=mesh['gx'=4,'zlo'=8,'core'=2,'x'=4,'zhi'=2] {'gx','core','x'}, dimensions={0} | all-to-all | bytes 1310720 | tf_op jit(solution)/shard_map/all_to_all | solution.py:153
  109.0 0.1 reduce_sum.18
  109.1 26.1 %all_to_all.22 = f32[16,40,128]{2,1,0:T(8,128)S(1)} all-to-all(f32[16,40,128]{2,1,0:T(8,128)S(1)} %broadcast_in_dim.6), channel_id=1, replica_groups=mesh['gx'=4,'zlo'=8,'core'=2,'x'=4,'zhi'=2] {'zlo','zhi'}, dimensions={0} | all-to-all | bytes 655360 | tf_op jit(solution)/shard_map/all_to_all | solution.py:153
  135.2 0.9 broadcast_in_dim.7
  136.1 9.3 %all-to-all-start.3 = ((f32[32,40,128]{2,1,0:T(8,128)}), f32[32,40,128]{2,1,0:T(8,128)S(1)}, u32[]{:S(2)}, u32[]{:S(2)}) async-start(f32[32,40,128]{2,1,0:T(8,128)} %broadcast_in_dim.7), calls=%async_computation.3 | async-start | bytes 1310720 | tf_op jit(solution)/shard_map/all_to_all | solution.py:153
  145.5 12.5 %all-to-all-done.3 = f32[32,40,128]{2,1,0:T(8,128)S(1)} async-done(((f32[32,40,128]{2,1,0:T(8,128)}), f32[32,40,128]{2,1,0:T(8,128)S(1)}, u32[]{:S(2)}, u32[]{:S(2)}) %all-to-all-start.3) | async-done | bytes 655392 | tf_op jit(solution)/shard_map/all_to_all | solution.py:153
  158.0 0.0 copy-start.4
  158.0 0.8 copy-done.4
  158.8 1.9 %gram_rows.1 = f32[128,512]{1,0:T(8,128)} custom-call(s32[1]{0:T(128)} %bitcast.2.place, f32[1280,128]{1,0:T(8,128)} %bitcast.8), custom_call_target="tpu_custom_call" | custom-call | tf_op jit(solution)/shard_map/gram_rows/pallas_call | solution.py:140
  (3 shorter events, 0.1 us)
Async XLA Ops:
  0.6 13.5 %copy-start = (f32[4,8,96,128]{3,2,1,0:T(8,128)S(1)}, f32[4,8,96,128]{3,2,1,0:T(8,128)}, u32[]{:S(2)}) copy-start(f32[4,8,96,128]{3,2,1,0:T(8,128)} %y.5) | copy-start | bytes 4718596
  3.4 51.8 %collective-permute-start = (f32[4,4,96,128]{3,2,1,0:T(8,128)}, f32[4,4,96,128]{3,2,1,0:T(8,128)S(1)}, u32[]{:S(2)}, u32[]{:S(2)}) collective-permute-start(f32[4,4,96,128]{3,2,1,0:T(8,128)} %get-tuple-element.7), channel_id=1, source_target_pairs={{0,8},{8,16},{16,24},{24,32},{32,40},{40,48},{48,56},{56,64},{64,7... | collective-permute-start | bytes 2359304 | tf_op jit(solution)/shard_map/ppermute | solution.py:168
  8.3 46.8 %collective-permute-start.1 = (f32[4,4,96,128]{3,2,1,0:T(8,128)}, f32[4,4,96,128]{3,2,1,0:T(8,128)}, u32[]{:S(2)}, u32[]{:S(2)}) collective-permute-start(f32[4,4,96,128]{3,2,1,0:T(8,128)} %get-tuple-element.6), channel_id=1, source_target_pairs={{8,0},{16,8},{24,16},{32,24},{40,32},{48,40},{56,48},{64,56},{72,6... | collective-permute-start | bytes 2359304 | tf_op jit(solution)/shard_map/ppermute | solution.py:169
  16.4 38.8 %copy-start.1 = (f32[3,8,96,128]{3,2,1,0:T(8,128)S(1)}, f32[3,8,96,128]{3,2,1,0:T(8,128)}, u32[]{:S(2)}) copy-start(f32[3,8,96,128]{3,2,1,0:T(8,128)} %vel.1) | copy-start | bytes 3538948
  20.5 20.7 %collective-permute-start.4 = (f32[4,8,4,128]{3,2,1,0:T(4,128)}, f32[4,8,4,128]{3,2,1,0:T(4,128)}, u32[]{:S(2)}, u32[]{:S(2)}) collective-permute-start(f32[4,8,4,128]{3,2,1,0:T(4,128)} %pad.7), channel_id=1, source_target_pairs={{0,128},{128,256},{256,384},{384,0},{1,129},{129,257},{257,385},{3... | collective-permute-start | bytes 196616 | tf_op jit(solution)/shard_map/ppermute | solution.py:176
  25.8 20.7 %collective-permute-start.5 = (f32[4,8,4,128]{3,2,1,0:T(4,128)S(1)}, f32[4,8,4,128]{3,2,1,0:T(4,128)S(1)}, u32[]{:S(2)}, u32[]{:S(2)}) collective-permute-start(f32[4,8,4,128]{3,2,1,0:T(4,128)S(1)} %pad.8), channel_id=1, source_target_pairs={{128,0},{256,128},{384,256},{0,384},{129,1},{257,129},{385,257},{1... | collective-permute-start | bytes 196616 | tf_op jit(solution)/shard_map/ppermute | solution.py:177
  30.4 16.1 %collective-permute-start.2 = (f32[4,8,4,128]{3,2,1,0:T(4,128)S(1)}, f32[4,8,4,128]{3,2,1,0:T(4,128)S(1)}, u32[]{:S(2)}, u32[]{:S(2)}) collective-permute-start(f32[4,8,4,128]{3,2,1,0:T(4,128)S(1)} %get-tuple-element.5), channel_id=1, source_target_pairs={{0,1},{1,2},{2,3},{3,4},{4,5},{5,6},{6,7},{7,0},{8,9},{9,10},{10,1... | collective-permute-start | bytes 196616 | tf_op jit(solution)/shard_map/ppermute | solution.py:165
  41.2 14.0 %collective-permute-start.3 = (f32[4,8,4,128]{3,2,1,0:T(4,128)S(1)}, f32[4,8,4,128]{3,2,1,0:T(4,128)S(1)}, u32[]{:S(2)}, u32[]{:S(2)}) collective-permute-start(f32[4,8,4,128]{3,2,1,0:T(4,128)S(1)} %get-tuple-element.4), channel_id=1, source_target_pairs={{1,0},{2,1},{3,2},{4,3},{5,4},{6,5},{7,6},{0,7},{9,8},{10,9},{11,1... | collective-permute-start | bytes 196616 | tf_op jit(solution)/shard_map/ppermute | solution.py:166
  55.2 0.9 copy-start.2
  56.1 0.9 copy-start.3
  136.1 21.9 %all-to-all-start.3 = ((f32[32,40,128]{2,1,0:T(8,128)}), f32[32,40,128]{2,1,0:T(8,128)S(1)}, u32[]{:S(2)}, u32[]{:S(2)}) async-start(f32[32,40,128]{2,1,0:T(8,128)} %broadcast_in_dim.7), calls=%async_computation.3 | async-start | bytes 1310720 | tf_op jit(solution)/shard_map/all_to_all | solution.py:153
  158.0 0.8 copy-start.4

commit v2 on v1

v2 whole, which is shorter than its diff:
```python
import functools

import ml_dtypes
import numpy as np
import jax
import jax.numpy as jnp
from jax import lax
from jax.experimental import pallas as pl
from jax.experimental.pallas import tpu as pltpu
from jax.sharding import Mesh, PartitionSpec as P

C1 = (4.0 / 5.0, -1.0 / 5.0, 4.0 / 105.0, -1.0 / 280.0)
C2 = (-205.0 / 72.0, 8.0 / 5.0, -1.0 / 5.0, 8.0 / 315.0, -1.0 / 560.0)
DIFF = (0.10, 0.12, 0.08, 0.15)
NU = (-1.0, -1.0, 2.0, 0.0)
PAIRS = [(a, b) for a in range(4) for b in range(a, 4)]
MIB = 1 << 20


def split(value):
    high = value.astype(jnp.bfloat16)
    return high, (value - high.astype(jnp.float32)).astype(jnp.bfloat16)


def x_matrices(width):
    matrix = np.zeros((2 * width, 2 * width))
    for i in range(width):
        for k in range(-4, 5):
            j = i + k
            row = j if 0 <= j < width else (width + 4 + j if j < 0 else width + 4 + j - width)
            if k:
                matrix[row, i] += np.sign(k) * C1[abs(k) - 1]
            matrix[row, width + i] += C2[abs(k)]
    matrix = matrix.astype(np.float32)
    high = matrix.astype(ml_dtypes.bfloat16)
    return high, (matrix - high.astype(np.float32)).astype(ml_dtypes.bfloat16)


def dot(left, right):
    return lax.dot_general(
        left, right, (((1,), (0,)), ((), ())), preferred_element_type=jnp.float32
    )


def lanes():
    return lax.broadcasted_iota(jnp.int32, (8, 128), 1)


def pack_body(place, y, inner, outer, za, zb, xs):
    count, rows, depth, width = y.shape
    core, half = place[1], place[2]
    lane = lanes()

    def species(s, carry):
        inner[s] = y[s, pl.ds(4 * (1 - core), 4)]
        outer[s] = y[s, pl.ds(4 * core, 4)]
        for j in range(rows):
            low, high = y[s, j, 0:4], y[s, j, depth - 4 :]
            at = 4 * (j % 2)
            za[s, j // 2, at : at + 4] = jnp.where(half == 0, high, low)
            zb[s, j // 2, at : at + 4] = jnp.where(half == 0, low, high)
            packed = jnp.zeros((8, width), jnp.float32)
            for g in range(depth // 8):
                turned = pltpu.roll(y[s, j, 8 * g : 8 * g + 8], 8 * g + 4, 1)
                packed = jnp.where(lane // 8 == g, turned, packed)
            xs[s, j] = packed
        return carry

    lax.fori_loop(0, count, species, 0)


SMEM = pl.BlockSpec(memory_space=pltpu.SMEM)
VMEM = pl.BlockSpec(memory_space=pltpu.VMEM)


def pack(place, y):
    count, rows, depth, width = y.shape
    shapes = [(count, 4, depth, width)] * 2 + [(count, rows // 2, 8, width)] * 2
    shapes = shapes + [(count, rows, 8, width)]
    return pl.pallas_call(
        pack_body,
        out_shape=[jax.ShapeDtypeStruct(shape, jnp.float32) for shape in shapes],
        in_specs=[SMEM, VMEM],
        out_specs=[VMEM] * 5,
        compiler_params=pltpu.CompilerParams(vmem_limit_bytes=24 * MIB),
        name="pack",
    )(place, y)


def stencil_body(place, y, vel, inner, outer, za, zb, xlow, xhigh, mh, ml, out, rate, side, dx, pad):
    count, rows, depth, width = y.shape
    core, half = place[1], place[2]
    below = lanes() % 8 < 4
    for j in range(rows):
        heat = 1.0 + 3.0 * y[2, j]
        rate[j] = y[0, j] * y[1, j] * jnp.exp(-3.0 / heat)

    def species(s, carry):
        diff = jnp.float32(0.25 * DIFF[0])
        nu = jnp.float32(NU[0])
        for q in range(1, count):
            diff = jnp.where(s == q, jnp.float32(0.25 * DIFF[q]), diff)
            nu = jnp.where(s == q, jnp.float32(NU[q]), nu)
        pad[pl.ds(12 * (1 - core), 4), 8 : 8 + depth] = inner[s]
        pad[pl.ds(12 * core, 4), 8 : 8 + depth] = outer[s]
        for j in range(rows):
            at = 4 * (j % 2)
            fa, fb = za[s, j // 2, at : at + 4], zb[s, j // 2, at : at + 4]
            pad[4 + j, 4:8] = jnp.where(half == 0, fb, fa)
            pad[4 + j, 8 : 8 + depth] = y[s, j]
            pad[4 + j, 8 + depth : 12 + depth] = jnp.where(half == 0, fa, fb)
            packed = jnp.where(below, xlow[s, j], xhigh[s, j])
            for g in range(depth // 8):
                row = j * depth + 8 * g
                side[row : row + 8] = pltpu.roll(packed, (128 - 8 * g) % 128, 1)
        left = jnp.concatenate([y[s].reshape(rows * depth, width), side[...]], axis=1)
        high, low = split(left)
        dx[...] = dot(high, mh[...]) + (dot(low, mh[...]) + dot(high, ml[...]))
        for j in range(rows):
            centre = y[s, j]
            d1y = d1z = None
            second = (2.0 * C2[0]) * centre + dx[j * depth : (j + 1) * depth, width:]
            for k in range(1, 5):
                ya, yb = pad[4 + j + k, 8 : 8 + depth], pad[4 + j - k, 8 : 8 + depth]
                za_, zb_ = pad[4 + j, 8 + k : 8 + k + depth], pad[4 + j, 8 - k : 8 - k + depth]
                ty, tz = C1[k - 1] * (ya - yb), C1[k - 1] * (za_ - zb_)
                d1y = ty if d1y is None else d1y + ty
                d1z = tz if d1z is None else d1z + tz
                second = second + C2[k] * ((ya + yb) + (za_ + zb_))
            moved = vel[0, j] * dx[j * depth : (j + 1) * depth, :width]
            moved = moved + vel[1, j] * d1y + vel[2, j] * d1z
            out[s, j] = centre + (diff * second - 0.25 * moved + nu * rate[j])
        return carry

    lax.fori_loop(0, count, species, 0)


def stencil(place, y, *rest):
    _, rows, depth, width = y.shape
    return pl.pallas_call(
        stencil_body,
        out_shape=jax.ShapeDtypeStruct(y.shape, jnp.float32),
        in_specs=[SMEM] + [VMEM] * (1 + len(rest)),
        out_specs=VMEM,
        scratch_shapes=[
            pltpu.VMEM((rows, depth, width), jnp.float32),
            pltpu.VMEM((rows * depth, width), jnp.float32),
            pltpu.VMEM((rows * depth, 2 * width), jnp.float32),
            pltpu.VMEM((rows + 8, depth + 16, width), jnp.float32),
        ],
        compiler_params=pltpu.CompilerParams(vmem_limit_bytes=40 * MIB),
        name="stencil",
    )(place, y, *rest)


def gram_body(place, lines, mine, other):
    parts = lines.shape[0]
    whole = jnp.concatenate([lines[a] for a in range(parts)], axis=1)
    high, low = split(whole)
    turned_high, turned_low = split(whole.T)
    total = dot(turned_high, high) + (dot(turned_high, low) + dot(turned_low, high))
    tiles = [total[a * 128 : (a + 1) * 128, b * 128 : (b + 1) * 128] for a, b in PAIRS]
    for q in range(5):
        first, second = tiles[q], tiles[q + 5]
        mine[q * 128 : (q + 1) * 128] = jnp.where(place[1] == 0, first, second)
        other[q * 128 : (q + 1) * 128] = jnp.where(place[1] == 0, second, first)


def gram_blocks(place, lines):
    return pl.pallas_call(
        gram_body,
        out_shape=[jax.ShapeDtypeStruct((len(PAIRS) * 64, 128), jnp.float32)] * 2,
        in_specs=[SMEM, VMEM],
        out_specs=[VMEM] * 2,
        compiler_params=pltpu.CompilerParams(vmem_limit_bytes=40 * MIB),
        name="gram",
    )(place, lines)


def rows_body(scale, place, mine, other, out):
    row, core = place[0], place[1]
    for b in range(4):
        low, top = jnp.minimum(row, b), jnp.maximum(row, b)
        index = low * 4 - (low * (low - 1)) // 2 + (top - low)
        owner = jnp.where(index >= 5, 1, 0)
        at = pl.ds(pl.multiple_of((index - 5 * owner) * 128, 128), 128)
        tile = jnp.where(owner == core, mine[at], other[at]) * scale
        out[:, b * 128 : (b + 1) * 128] = jnp.where(row <= b, tile, tile.T)


def gram_rows(place, mine, other, scale):
    return pl.pallas_call(
        functools.partial(rows_body, scale),
        out_shape=jax.ShapeDtypeStruct((128, 512), jnp.float32),
        in_specs=[SMEM, VMEM, VMEM],
        out_specs=VMEM,
        name="gram_rows",
    )(place, mine, other)


def exchange(pieces, axes):
    return lax.all_to_all(pieces, axes, split_axis=0, concat_axis=0, tiled=True)


def gather_sum(part, axes, count):
    return jnp.sum(exchange(jnp.broadcast_to(part, (count,) + part.shape), axes), axis=0)


def shards(y, vel):
    species, rows, depth, width = y.shape
    gy, gz, gx = ("zpair", "znear", "core"), ("x", "zhi"), ("gx",)
    place = jnp.stack([lax.axis_index("gx"), lax.axis_index("core"), lax.axis_index("zhi")])
    place = place.astype(jnp.int32)
    inner, outer, za, zb, xs = pack(place, y)

    def cross(count):
        return [(i, (i + 1) % count if i % 2 else (i - 1) % count) for i in range(count)]

    up = [(i, (i + 1) % 4) for i in range(4)]
    swap = [(0, 1), (1, 0)]
    za = lax.ppermute(za, "zhi", swap)
    zb = lax.ppermute(zb, gz, cross(8))
    outer = lax.ppermute(outer, gy, cross(16))
    inner = lax.ppermute(inner, "core", swap)
    xlow = lax.ppermute(xs, gx, up)
    xhigh = lax.ppermute(xs, gx, [(target, source) for source, target in up])
    updated = stencil(place, y, vel, inner, outer, za, zb, xlow, xhigh, *x_matrices(width))

    lines = exchange(updated.reshape(4, species * rows * depth // 4, width), gx)
    mine, other = gram_blocks(place, lines)
    mine = mine + lax.ppermute(other, "core", swap)
    plane = ("gx", "x")
    part = jnp.sum(exchange(mine.reshape(16, -1, 128), plane), axis=0)
    part = gather_sum(part, ("znear",), 4)
    part = gather_sum(part, ("zpair", "zhi"), 4)
    mine = exchange(jnp.broadcast_to(part, (16,) + part.shape), plane).reshape(-1, 128)
    other = lax.ppermute(mine, "core", swap)
    cells = species * rows * 16 * depth * 8
    return updated, gram_rows(place, mine, other, 1.0 / cells)


def solution(mesh):
    axes = ("gx", "zpair", "znear", "core", "x", "zhi")
    fine = Mesh(mesh.devices.reshape(4, 2, 4, 2, 4, 2), axes)
    grid = P(None, ("zpair", "znear", "core"), ("x", "zhi"), "gx")
    return jax.shard_map(
        shards, mesh=fine, in_specs=(grid, grid), out_specs=(grid, P("gx", None)), check_vma=False
    )
```

time: 163 us -> 163 us (level); the launches traced: 161 us -> 163 us
  local copies, waits for them, and re-layouts: 16.1 us -> 5.25 us
  starting transfers between devices: 42.6 us -> 49.2 us
  waiting for transfers between devices: 21.2 us -> 26.8 us
  Pallas kernels: 10 us -> 11.7 us
    ppermute x6 -> x8, waiting for transfers between devices: 8.66 us -> 26.8 us  [the longest x1 13.8 us: shards(): zb = lax.ppermute(zb, gz, cross(8))]
    ppermute x6 -> x8, starting transfers between devices: 33.3 us -> 49.2 us  [the longest x1 12 us: shards(): mine = mine + lax.ppermute(other, 'core', swap)]
    all_to_all x1 -> x0, waiting for transfers between devices: 12.5 us -> none  [exchange(): return lax.all_to_all(pieces, axes, split_axis=0, concat_axis=0, tiled=True)]
    all_to_all x1 -> x0, starting transfers between devices: 9.34 us -> none  [exchange(): return lax.all_to_all(pieces, axes, split_axis=0, concat_axis=0, tiled=True)]
    slice x3 -> x0, local copies, waits for them, and re-layouts: 5.02 us -> none  [the longest x1 2.77 us: shards(): yhigh = lax.ppermute(y[:, :4], gy, down)]
    unnamed x12 -> x16, local copies, waits for them, and re-layouts: 7.82 us -> 5.21 us
    pad x2 -> x0, local copies, waits for them, and re-layouts: 2.32 us -> none  [face(): return jnp.pad(turned, ((0, 0), (0, 0), (0, 0), (0, 128 - depth)))]
    pallas_call x1 -> x2, Pallas kernels: 1.45 us -> 3.33 us  [the longest x1 2.01 us: gram_blocks(): pl.pallas_call(gram_body, out_shape=[jax.ShapeDtypeStruct((len(PAIRS) * 6...]
  transfers between devices with their start and end apart: 7 -> 8, of which waited for: 2 -> 4; matrix products, arithmetic and copies ran while one was open for 6% -> 0% of each run, Pallas kernels for 0% -> 0%
where the time goes in v2:
time: 163 us
  blocking collectives  68.7 us (42%)
  starting transfers between devices  49.2 us (30%)
  waiting for transfers between devices  26.8 us (16%)
  Pallas kernels  11.7 us (7%)
  local copies, waits for them, and re-layouts  5.25 us (3%)
    all_to_all x5, blocking collectives, exchange(): return lax.all_to_all(pieces, axes, split_axis=0, concat_axis=0, tiled=True)  68.7 us
    ppermute x1, waiting for transfers between devices, shards(): zb = lax.ppermute(zb, gz, cross(8))  13.8 us
    ppermute x1, starting transfers between devices, shards(): mine = mine + lax.ppermute(other, 'core', swap)  12 us
    ppermute x1, starting transfers between devices, shards(): za = lax.ppermute(za, 'zhi', swap)  10.7 us
    ppermute x1, waiting for transfers between devices, shards(): za = lax.ppermute(za, 'zhi', swap)  10.4 us
    ppermute x1, starting transfers between devices, shards(): inner = lax.ppermute(inner, 'core', swap)  8.79 us
    ppermute x1, starting transfers between devices, shards(): other = lax.ppermute(mine, 'core', swap)  7.3 us
    pallas_call x1, Pallas kernels, stencil(): pl.pallas_call(stencil_body, out_shape=jax.ShapeDtypeStruct(y.shape, jnp....  6.45 us
  transfers between devices with their start and end apart: 8, of which 4 were waited for; matrix products, arithmetic and copies ran while one was open for 0% of the time, Pallas kernels for 0%

profile of v2, /device:TPU:1, one launch (start us, length us, event | category | flops | bytes accessed | tf_op | source)
XLA Modules:
  0.0 162.6 jit_solution(15101925211127621826)
XLA Ops:
  0.6 0.1 pad_add_fusion.place
  0.7 0.0 copy-start
  0.7 1.4 copy-done
  2.1 0.0 copy-start.5
  2.1 0.0 copy-start.1
  2.1 1.3 pack.1
  3.5 8.8 %collective-permute-start = (f32[4,4,96,128]{3,2,1,0:T(8,128)S(1)}, f32[4,4,96,128]{3,2,1,0:T(8,128)S(1)}, u32[]{:S(2)}, u32[]{:S(2)}) collective-permute-start(f32[4,4,96,128]{3,2,1,0:T(8,128)S(1)} %get-tuple-element.9), channel_id=1, source_target_pairs={{0,8},{8,0},{1,9},{9,1},{2,10},{10,2},{3,11},{11,3},{4,12},{12,4},... | collective-permute-start | bytes 2359304 | tf_op jit(solution)/shard_map/ppermute | solution.py:224
  12.2 1.9 %collective-permute-start.1 = (f32[4,4,96,128]{3,2,1,0:T(8,128)S(1)}, f32[4,4,96,128]{3,2,1,0:T(8,128)S(1)}, u32[]{:S(2)}, u32[]{:S(2)}) collective-permute-start(f32[4,4,96,128]{3,2,1,0:T(8,128)S(1)} %get-tuple-element.10), channel_id=1, source_target_pairs={{0,120},{8,16},{16,8},{24,32},{32,24},{40,48},{48,40},{56,64},{64,... | collective-permute-start | bytes 2359304 | tf_op jit(solution)/shard_map/ppermute | solution.py:223
  14.2 10.7 %collective-permute-start.2 = (f32[4,4,8,128]{3,2,1,0:T(8,128)S(1)}, f32[4,4,8,128]{3,2,1,0:T(8,128)S(1)}, u32[]{:S(2)}, u32[]{:S(2)}) collective-permute-start(f32[4,4,8,128]{3,2,1,0:T(8,128)S(1)} %get-tuple-element.11), channel_id=1, source_target_pairs={{0,1},{1,0},{2,3},{3,2},{4,5},{5,4},{6,7},{7,6},{8,9},{9,8},{10,11... | collective-permute-start | bytes 196616 | tf_op jit(solution)/shard_map/ppermute | solution.py:221
  24.9 4.6 %collective-permute-start.5 = (f32[4,8,8,128]{3,2,1,0:T(8,128)S(1)}, f32[4,8,8,128]{3,2,1,0:T(8,128)S(1)}, u32[]{:S(2)}, u32[]{:S(2)}) collective-permute-start(f32[4,8,8,128]{3,2,1,0:T(8,128)S(1)} %get-tuple-element.13), channel_id=1, source_target_pairs={{128,0},{256,128},{384,256},{0,384},{129,1},{257,129},{385,257},{1... | collective-permute-start | bytes 393224 | tf_op jit(solution)/shard_map/ppermute | solution.py:226
  29.5 1.9 %collective-permute-start.4 = (f32[4,8,8,128]{3,2,1,0:T(8,128)S(1)}, f32[4,8,8,128]{3,2,1,0:T(8,128)S(1)}, u32[]{:S(2)}, u32[]{:S(2)}) collective-permute-start(f32[4,8,8,128]{3,2,1,0:T(8,128)S(1)} %get-tuple-element.13), channel_id=1, source_target_pairs={{0,128},{128,256},{256,384},{384,0},{1,129},{129,257},{257,385},{3... | collective-permute-start | bytes 393224 | tf_op jit(solution)/shard_map/ppermute | solution.py:225
  31.5 10.4 %collective-permute-done.2.za = f32[4,4,8,128]{3,2,1,0:T(8,128)S(1)} collective-permute-done((f32[4,4,8,128]{3,2,1,0:T(8,128)S(1)}, f32[4,4,8,128]{3,2,1,0:T(8,128)S(1)}, u32[]{:S(2)}, u32[]{:S(2)}) %collective-permute-start.2) | collective-permute-done | bytes 65568 | tf_op jit(solution)/shard_map/ppermute | solution.py:221
  41.9 2.0 %collective-permute-start.3 = (f32[4,4,8,128]{3,2,1,0:T(8,128)S(1)}, f32[4,4,8,128]{3,2,1,0:T(8,128)S(1)}, u32[]{:S(2)}, u32[]{:S(2)}) collective-permute-start(f32[4,4,8,128]{3,2,1,0:T(8,128)S(1)} %get-tuple-element.12), channel_id=1, source_target_pairs={{0,7},{1,2},{2,1},{3,4},{4,3},{5,6},{6,5},{7,0},{8,15},{9,10},{10,... | collective-permute-start | bytes 196616 | tf_op jit(solution)/shard_map/ppermute | solution.py:222
  43.9 13.8 %collective-permute-done.3.zb = f32[4,4,8,128]{3,2,1,0:T(8,128)S(1)} collective-permute-done((f32[4,4,8,128]{3,2,1,0:T(8,128)S(1)}, f32[4,4,8,128]{3,2,1,0:T(8,128)S(1)}, u32[]{:S(2)}, u32[]{:S(2)}) %collective-permute-start.3) | collective-permute-done | bytes 65568 | tf_op jit(solution)/shard_map/ppermute | solution.py:222
  57.7 0.0 collective-permute-done.5.xhigh
  57.7 0.0 collective-permute-done.4.xlow
  57.7 0.0 collective-permute-done.inner
  57.7 0.0 collective-permute-done.1.outer
  57.8 0.0 copy-done.1
  57.8 0.0 copy-start.2
  57.8 1.3 copy-done.2
  59.0 0.0 copy-start.3
  59.0 0.9 copy-done.3
  59.9 0.0 copy-start.4
  59.9 0.9 copy-done.4
  60.8 6.5 %stencil.1 = f32[4,8,96,128]{3,2,1,0:T(8,128)} custom-call(s32[3]{0:T(128)S(1)} %pad_add_fusion.place, f32[4,8,96,128]{3,2,1,0:T(8,128)S(1)} %copy-done.1, f32[3,8,96,128]{3,2,1,0:T(8,128)S(1)} %copy-done.2, f32[4,4,96,128]{3,2,1,0:T(8,128)S(1)} %collective-permute-done.inner, f32[4,4,96,128]{3,2,1,0:T(8,128)S(1)} %collective-permute-done.1.outer, ...), custom_call_target="tpu_custom_call" | custom-call | tf_op jit(solution)/shard_map/stencil/pallas_call | solution.py:140
  67.3 16.1 %all_to_all.25.lines = f32[4,768,128]{2,1,0:T(8,128)S(1)} all-to-all(f32[4,768,128]{2,1,0:T(8,128)} %bitcast.6), channel_id=1, replica_groups=mesh['gx'=4,'zpair'=2,'znear'=4,'core'=2,'x'=4,'zhi'=2] {'gx'}, dimensions={0} | all-to-all | bytes 3145728 | tf_op jit(solution)/shard_map/all_to_all | solution.py:202
  83.4 0.0 copy-done.5
  83.4 2.0 %gram.1 = (f32[640,128]{1,0:T(8,128)S(1)}, f32[640,128]{1,0:T(8,128)S(1)}) custom-call(s32[3]{0:T(128)S(1)} %pad_add_fusion.place, f32[4,768,128]{2,1,0:T(8,128)S(1)} %all_to_all.25.lines), custom_call_target="tpu_custom_call" | custom-call | tf_op jit(solution)/shard_map/gram/pallas_call | solution.py:170
  85.4 12.0 %collective-permute-start.6 = (f32[640,128]{1,0:T(8,128)S(1)}, f32[640,128]{1,0:T(8,128)S(1)}, u32[]{:S(2)}, u32[]{:S(2)}) collective-permute-start(f32[640,128]{1,0:T(8,128)S(1)} %get-tuple-element.15), channel_id=1, source_target_pairs={{0,8},{8,0},{1,9},{9,1},{2,10},{10,2},{3,11},{11,3},{4,12},{12,4},... | collective-permute-start | bytes 983048 | tf_op jit(solution)/shard_map/ppermute | solution.py:231
  97.4 1.2 collective-permute-done.6
  98.7 11.6 %all_to_all.26 = f32[16,40,128]{2,1,0:T(8,128)S(1)} all-to-all(f32[16,40,128]{2,1,0:T(8,128)S(1)} %bitcast.9), channel_id=1, replica_groups=mesh['gx'=4,'zpair'=2,'znear'=4,'core'=2,'x'=4,'zhi'=2] {'gx','x'}, dimensions={0} | all-to-all | bytes 655360 | tf_op jit(solution)/shard_map/all_to_all | solution.py:202
  110.3 7.0 %all_to_all.27 = f32[4,40,128]{2,1,0:T(8,128)S(1)} all-to-all(f32[4,40,128]{2,1,0:T(8,128)S(1)} %broadcast_in_dim.9), channel_id=1, replica_groups=mesh['gx'=4,'zpair'=2,'znear'=4,'core'=2,'x'=4,'zhi'=2] {'znear'}, dimensions={0} | all-to-all | bytes 163840 | tf_op jit(solution)/shard_map/all_to_all | solution.py:202
  117.3 23.3 %all_to_all.28 = f32[4,40,128]{2,1,0:T(8,128)S(1)} all-to-all(f32[4,40,128]{2,1,0:T(8,128)S(1)} %broadcast_in_dim.10), channel_id=1, replica_groups=mesh['gx'=4,'zpair'=2,'znear'=4,'core'=2,'x'=4,'zhi'=2] {'zpair','zhi'}, dimensions={0} | all-to-all | bytes 163840 | tf_op jit(solution)/shard_map/all_to_all | solution.py:202
  140.7 10.7 %all_to_all.29 = f32[16,40,128]{2,1,0:T(8,128)S(1)} all-to-all(f32[16,40,128]{2,1,0:T(8,128)S(1)} %broadcast_in_dim.11), channel_id=1, replica_groups=mesh['gx'=4,'zpair'=2,'znear'=4,'core'=2,'x'=4,'zhi'=2] {'gx','x'}, dimensions={0} | all-to-all | bytes 655360 | tf_op jit(solution)/shard_map/all_to_all | solution.py:202
  151.4 0.0 copy-start.6
  151.4 7.3 %collective-permute-start.7 = (f32[640,128]{1,0:T(8,128)S(1)}, f32[640,128]{1,0:T(8,128)S(1)}, u32[]{:S(2)}, u32[]{:S(2)}) collective-permute-start(f32[640,128]{1,0:T(8,128)S(1)} %bitcast.7), channel_id=1, source_target_pairs={{0,8},{8,0},{1,9},{9,1},{2,10},{10,2},{3,11},{11,3},{4,12},{12,4},... | collective-permute-start | bytes 983048 | tf_op jit(solution)/shard_map/ppermute | solution.py:237
  158.7 1.2 collective-permute-done.7.other
  159.9 0.0 copy-done.6
  159.9 0.0 copy-start.7
  159.9 0.7 copy-done.7
  160.6 1.9 %gram_rows.1 = f32[128,512]{1,0:T(8,128)} custom-call(s32[3]{0:T(128)} %copy-done.5, f32[640,128]{1,0:T(8,128)} %bitcast.8, f32[640,128]{1,0:T(8,128)} %copy-done.7), custom_call_target="tpu_custom_call" | custom-call | tf_op jit(solution)/shard_map/gram_rows/pallas_call | solution.py:192
  (7 shorter events, 0.1 us)
Async XLA Ops:
  0.7 1.4 copy-start
  2.1 81.3 %copy-start.5 = (s32[3]{0:T(128)}, s32[3]{0:T(128)S(1)}, u32[]{:S(2)}) copy-start(s32[3]{0:T(128)S(1)} %pad_add_fusion.place) | copy-start | bytes 40
  2.1 55.6 %copy-start.1 = (f32[4,8,96,128]{3,2,1,0:T(8,128)S(1)}, f32[4,8,96,128]{3,2,1,0:T(8,128)}, u32[]{:S(2)}) copy-start(f32[4,8,96,128]{3,2,1,0:T(8,128)} %y.3) | copy-start | bytes 4718596
  3.5 54.3 %collective-permute-start = (f32[4,4,96,128]{3,2,1,0:T(8,128)S(1)}, f32[4,4,96,128]{3,2,1,0:T(8,128)S(1)}, u32[]{:S(2)}, u32[]{:S(2)}) collective-permute-start(f32[4,4,96,128]{3,2,1,0:T(8,128)S(1)} %get-tuple-element.9), channel_id=1, source_target_pairs={{0,8},{8,0},{1,9},{9,1},{2,10},{10,2},{3,11},{11,3},{4,12},{12,4},... | collective-permute-start | bytes 2359304 | tf_op jit(solution)/shard_map/ppermute | solution.py:224
  12.2 45.5 %collective-permute-start.1 = (f32[4,4,96,128]{3,2,1,0:T(8,128)S(1)}, f32[4,4,96,128]{3,2,1,0:T(8,128)S(1)}, u32[]{:S(2)}, u32[]{:S(2)}) collective-permute-start(f32[4,4,96,128]{3,2,1,0:T(8,128)S(1)} %get-tuple-element.10), channel_id=1, source_target_pairs={{0,120},{8,16},{16,8},{24,32},{32,24},{40,48},{48,40},{56,64},{64,... | collective-permute-start | bytes 2359304 | tf_op jit(solution)/shard_map/ppermute | solution.py:223
  14.2 27.7 %collective-permute-start.2 = (f32[4,4,8,128]{3,2,1,0:T(8,128)S(1)}, f32[4,4,8,128]{3,2,1,0:T(8,128)S(1)}, u32[]{:S(2)}, u32[]{:S(2)}) collective-permute-start(f32[4,4,8,128]{3,2,1,0:T(8,128)S(1)} %get-tuple-element.11), channel_id=1, source_target_pairs={{0,1},{1,0},{2,3},{3,2},{4,5},{5,4},{6,7},{7,6},{8,9},{9,8},{10,11... | collective-permute-start | bytes 196616 | tf_op jit(solution)/shard_map/ppermute | solution.py:221
  24.9 32.9 %collective-permute-start.5 = (f32[4,8,8,128]{3,2,1,0:T(8,128)S(1)}, f32[4,8,8,128]{3,2,1,0:T(8,128)S(1)}, u32[]{:S(2)}, u32[]{:S(2)}) collective-permute-start(f32[4,8,8,128]{3,2,1,0:T(8,128)S(1)} %get-tuple-element.13), channel_id=1, source_target_pairs={{128,0},{256,128},{384,256},{0,384},{129,1},{257,129},{385,257},{1... | collective-permute-start | bytes 393224 | tf_op jit(solution)/shard_map/ppermute | solution.py:226
  29.5 28.2 %collective-permute-start.4 = (f32[4,8,8,128]{3,2,1,0:T(8,128)S(1)}, f32[4,8,8,128]{3,2,1,0:T(8,128)S(1)}, u32[]{:S(2)}, u32[]{:S(2)}) collective-permute-start(f32[4,8,8,128]{3,2,1,0:T(8,128)S(1)} %get-tuple-element.13), channel_id=1, source_target_pairs={{0,128},{128,256},{256,384},{384,0},{1,129},{129,257},{257,385},{3... | collective-permute-start | bytes 393224 | tf_op jit(solution)/shard_map/ppermute | solution.py:225
  41.9 15.8 %collective-permute-start.3 = (f32[4,4,8,128]{3,2,1,0:T(8,128)S(1)}, f32[4,4,8,128]{3,2,1,0:T(8,128)S(1)}, u32[]{:S(2)}, u32[]{:S(2)}) collective-permute-start(f32[4,4,8,128]{3,2,1,0:T(8,128)S(1)} %get-tuple-element.12), channel_id=1, source_target_pairs={{0,7},{1,2},{2,1},{3,4},{4,3},{5,6},{6,5},{7,0},{8,15},{9,10},{10,... | collective-permute-start | bytes 196616 | tf_op jit(solution)/shard_map/ppermute | solution.py:222
  57.8 1.3 copy-start.2
  59.0 0.9 copy-start.3
  59.9 0.9 copy-start.4
  85.4 13.2 %collective-permute-start.6 = (f32[640,128]{1,0:T(8,128)S(1)}, f32[640,128]{1,0:T(8,128)S(1)}, u32[]{:S(2)}, u32[]{:S(2)}) collective-permute-start(f32[640,128]{1,0:T(8,128)S(1)} %get-tuple-element.15), channel_id=1, source_target_pairs={{0,8},{8,0},{1,9},{9,1},{2,10},{10,2},{3,11},{11,3},{4,12},{12,4},... | collective-permute-start | bytes 983048 | tf_op jit(solution)/shard_map/ppermute | solution.py:231
  151.4 8.5 %copy-start.6 = (f32[16,40,128]{2,1,0:T(8,128)}, f32[16,40,128]{2,1,0:T(8,128)S(1)}, u32[]{:S(2)}) copy-start(f32[16,40,128]{2,1,0:T(8,128)S(1)} %all_to_all.29) | copy-start | bytes 983044
  151.4 8.5 %collective-permute-start.7 = (f32[640,128]{1,0:T(8,128)S(1)}, f32[640,128]{1,0:T(8,128)S(1)}, u32[]{:S(2)}, u32[]{:S(2)}) collective-permute-start(f32[640,128]{1,0:T(8,128)S(1)} %bitcast.7), channel_id=1, source_target_pairs={{0,8},{8,0},{1,9},{9,1},{2,10},{10,2},{3,11},{11,3},{4,12},{12,4},... | collective-permute-start | bytes 983048 | tf_op jit(solution)/shard_map/ppermute | solution.py:237
  159.9 0.7 copy-start.7

commit v3 on v2

--- a/solution.py
+++ b/solution.py
@@ -87,28 +87,75 @@
     )(place, y)
 
 
-def stencil_body(place, y, vel, inner, outer, za, zb, xlow, xhigh, mh, ml, out, rate, side, dx, pad):
-    count, rows, depth, width = y.shape
-    core, half = place[1], place[2]
-    below = lanes() % 8 < 4
+def factors(s, count):
+    diff = jnp.float32(0.25 * DIFF[0])
+    nu = jnp.float32(NU[0])
+    for q in range(1, count):
+        diff = jnp.where(s == q, jnp.float32(0.25 * DIFF[q]), diff)
+        nu = jnp.where(s == q, jnp.float32(NU[q]), nu)
+    return diff, nu
+
+
+def along_z_body(place, y, vel, za, zb, out, rate, pad):
+    count, rows, depth, width = y.shape
+    half = place[2]
     for j in range(rows):
         heat = 1.0 + 3.0 * y[2, j]
         rate[j] = y[0, j] * y[1, j] * jnp.exp(-3.0 / heat)
 
     def species(s, carry):
-        diff = jnp.float32(0.25 * DIFF[0])
-        nu = jnp.float32(NU[0])
-        for q in range(1, count):
-            diff = jnp.where(s == q, jnp.float32(0.25 * DIFF[q]), diff)
-            nu = jnp.where(s == q, jnp.float32(NU[q]), nu)
-        pad[pl.ds(12 * (1 - core), 4), 8 : 8 + depth] = inner[s]
-        pad[pl.ds(12 * core, 4), 8 : 8 + depth] = outer[s]
+        diff, nu = factors(s, count)
         for j in range(rows):
             at = 4 * (j % 2)
             fa, fb = za[s, j // 2, at : at + 4], zb[s, j // 2, at : at + 4]
-            pad[4 + j, 4:8] = jnp.where(half == 0, fb, fa)
-            pad[4 + j, 8 : 8 + depth] = y[s, j]
-            pad[4 + j, 8 + depth : 12 + depth] = jnp.where(half == 0, fa, fb)
+            pad[j, 4:8] = jnp.where(half == 0, fb, fa)
+            pad[j, 8 : 8 + depth] = y[s, j]
+            pad[j, 8 + depth : 12 + depth] = jnp.where(half == 0, fa, fb)
+        for j in range(rows):
+            centre = y[s, j]
+            first = None
+            second = (2.0 * C2[0]) * centre
+            for k in range(1, 5):
+                ahead, behind = pad[j, 8 + k : 8 + k + depth], pad[j, 8 - k : 8 - k + depth]
+                term = (0.25 * C1[k - 1]) * (ahead - behind)
+                first = term if first is None else first + term
+                second = second + C2[k] * (ahead + behind)
+            out[s, j] = centre + (diff * second - vel[2, j] * first + nu * rate[j])
+        return carry
+
+    lax.fori_loop(0, count, species, 0)
+
+
+def along_z(place, y, *rest):
+    _, rows, depth, width = y.shape
+    return pl.pallas_call(
+        along_z_body,
+        out_shape=jax.ShapeDtypeStruct(y.shape, jnp.float32),
+        in_specs=[SMEM] + [VMEM] * (1 + len(rest)),
+        out_specs=VMEM,
+        scratch_shapes=[
+            pltpu.VMEM((rows, depth, width), jnp.float32),
+            pltpu.VMEM((rows, depth + 16, width), jnp.float32),
+        ],
+        compiler_params=pltpu.CompilerParams(vmem_limit_bytes=24 * MIB),
+        cost_estimate=pl.CostEstimate(
+            flops=10**10, bytes_accessed=2 * 10**8, transcendentals=0
+        ),
+        name="along_z",
+    )(place, y, *rest)
+
+
+def along_xy_body(place, y, vel, base, outer, inner, xlow, xhigh, mh, ml, out, side, dx, pad):
+    count, rows, depth, width = y.shape
+    core = place[1]
+    below = lanes() % 8 < 4
+
+    def species(s, carry):
+        diff, _ = factors(s, count)
+        pad[pl.ds(12 * (1 - core), 4)] = inner[s]
+        pad[pl.ds(12 * core, 4)] = outer[s]
+        pad[4 : 4 + rows] = y[s]
+        for j in range(rows):
             packed = jnp.where(below, xlow[s, j], xhigh[s, j])
             for g in range(depth // 8):
                 row = j * depth + 8 * g
@@ -117,39 +164,34 @@
         high, low = split(left)
         dx[...] = dot(high, mh[...]) + (dot(low, mh[...]) + dot(high, ml[...]))
         for j in range(rows):
-            centre = y[s, j]
-            d1y = d1z = None
-            second = (2.0 * C2[0]) * centre + dx[j * depth : (j + 1) * depth, width:]
+            first = None
+            second = dx[j * depth : (j + 1) * depth, width:]
             for k in range(1, 5):
-                ya, yb = pad[4 + j + k, 8 : 8 + depth], pad[4 + j - k, 8 : 8 + depth]
-                za_, zb_ = pad[4 + j, 8 + k : 8 + k + depth], pad[4 + j, 8 - k : 8 - k + depth]
-                ty, tz = C1[k - 1] * (ya - yb), C1[k - 1] * (za_ - zb_)
-                d1y = ty if d1y is None else d1y + ty
-                d1z = tz if d1z is None else d1z + tz
-                second = second + C2[k] * ((ya + yb) + (za_ + zb_))
-            moved = vel[0, j] * dx[j * depth : (j + 1) * depth, :width]
-            moved = moved + vel[1, j] * d1y + vel[2, j] * d1z
-            out[s, j] = centre + (diff * second - 0.25 * moved + nu * rate[j])
+                ahead, behind = pad[4 + j + k], pad[4 + j - k]
+                term = (0.25 * C1[k - 1]) * (ahead - behind)
+                first = term if first is None else first + term
+                second = second + C2[k] * (ahead + behind)
+            moved = (0.25 * vel[0, j]) * dx[j * depth : (j + 1) * depth, :width]
+            out[s, j] = base[s, j] + (diff * second - (moved + vel[1, j] * first))
         return carry
 
     lax.fori_loop(0, count, species, 0)
 
 
-def stencil(place, y, *rest):
+def along_xy(place, y, *rest):
     _, rows, depth, width = y.shape
     return pl.pallas_call(
-        stencil_body,
+        along_xy_body,
         out_shape=jax.ShapeDtypeStruct(y.shape, jnp.float32),
         in_specs=[SMEM] + [VMEM] * (1 + len(rest)),
         out_specs=VMEM,
         scratch_shapes=[
-            pltpu.VMEM((rows, depth, width), jnp.float32),
             pltpu.VMEM((rows * depth, width), jnp.float32),
             pltpu.VMEM((rows * depth, 2 * width), jnp.float32),
-            pltpu.VMEM((rows + 8, depth + 16, width), jnp.float32),
+            pltpu.VMEM((rows + 8, depth, width), jnp.float32),
         ],
-        compiler_params=pltpu.CompilerParams(vmem_limit_bytes=40 * MIB),
-        name="stencil",
+        compiler_params=pltpu.CompilerParams(vmem_limit_bytes=32 * MIB),
+        name="along_xy",
     )(place, y, *rest)
 
 
@@ -220,11 +262,12 @@
     swap = [(0, 1), (1, 0)]
     za = lax.ppermute(za, "zhi", swap)
     zb = lax.ppermute(zb, gz, cross(8))
+    inner = lax.ppermute(inner, "core", swap)
     outer = lax.ppermute(outer, gy, cross(16))
-    inner = lax.ppermute(inner, "core", swap)
     xlow = lax.ppermute(xs, gx, up)
     xhigh = lax.ppermute(xs, gx, [(target, source) for source, target in up])
-    updated = stencil(place, y, vel, inner, outer, za, zb, xlow, xhigh, *x_matrices(width))
+    base = along_z(place, y, vel, za, zb)
+    updated = along_xy(place, y, vel, base, outer, inner, xlow, xhigh, *x_matrices(width))
 
     lines = exchange(updated.reshape(4, species * rows * depth // 4, width), gx)
     mine, other = gram_blocks(place, lines)

time: 163 us -> 151 us (0.926)
  waiting for transfers between devices: 26.8 us -> 3.49 us
  starting transfers between devices: 49.2 us -> 62.6 us
  local copies, waits for them, and re-layouts: 5.25 us -> 2.2 us
    ppermute x1, waiting for transfers between devices: 13.8 us -> 0.01 us  [shards(): zb = lax.ppermute(zb, gz, cross(8))]
    ppermute x1, waiting for transfers between devices: 10.4 us -> 0.01 us  [shards(): za = lax.ppermute(za, 'zhi', swap)]
    ppermute x1, starting transfers between devices: 10.7 us -> 16.3 us  [shards(): za = lax.ppermute(za, 'zhi', swap)]
    ppermute x1, starting transfers between devices: 12 us -> 16.6 us  [shards(): mine = mine + lax.ppermute(other, 'core', swap)]
    unnamed x16, local copies, waits for them, and re-layouts: 5.21 us -> 2.16 us
    ppermute x1, starting transfers between devices: 1.98 us -> 4.12 us  [shards(): zb = lax.ppermute(zb, gz, cross(8))]
    ppermute x1, starting transfers between devices: 1.92 us -> 3.77 us  [shards(): outer = lax.ppermute(outer, gy, cross(16))]
    pallas_call x1 -> x2, Pallas kernels: 6.45 us -> 7.43 us  [the longest x1 4.96 us: along_xy(): pl.pallas_call(along_xy_body, out_shape=jax.ShapeDtypeStruct(y.shape, jnp...]
  transfers between devices with their start and end apart: 8 -> 8, of which waited for: 4 -> 3; matrix products, arithmetic and copies ran while one was open for 0% -> 0% of each run, Pallas kernels for 0% -> 2%
where the time goes in v3:
time: 151 us; the launch traced here: 150 us
  blocking collectives  68 us (45%)
  starting transfers between devices  62.6 us (41%)
  Pallas kernels  12.7 us (8%)
  waiting for transfers between devices  3.49 us (2%)
  local copies, waits for them, and re-layouts  2.2 us (1%)
    all_to_all x5, blocking collectives, exchange(): return lax.all_to_all(pieces, axes, split_axis=0, concat_axis=0, tiled=True)  68 us
    ppermute x1, starting transfers between devices, shards(): mine = mine + lax.ppermute(other, 'core', swap)  16.6 us
    ppermute x1, starting transfers between devices, shards(): za = lax.ppermute(za, 'zhi', swap)  16.3 us
    ppermute x1, starting transfers between devices, shards(): inner = lax.ppermute(inner, 'core', swap)  8.18 us
    ppermute x1, starting transfers between devices, shards(): other = lax.ppermute(mine, 'core', swap)  7.11 us
    pallas_call x1, Pallas kernels, along_xy(): pl.pallas_call(along_xy_body, out_shape=jax.ShapeDtypeStruct(y.shape, jnp...  4.96 us
    ppermute x1, starting transfers between devices, shards(): xhigh = lax.ppermute(xs, gx, [(target, source) for source, target in up])  4.64 us
    ppermute x1, starting transfers between devices, shards(): zb = lax.ppermute(zb, gz, cross(8))  4.12 us
  transfers between devices with their start and end apart: 8, of which 3 were waited for; matrix products, arithmetic and copies ran while one was open for 0% of the time, Pallas kernels for 2%

profile of v3, /device:TPU:1, one launch (start us, length us, event | category | flops | bytes accessed | tf_op | source)
XLA Modules:
  0.0 149.9 jit_solution(10651042834625090647)
XLA Ops:
  0.6 0.1 pad_add_fusion.place
  0.7 0.0 copy-start
  0.7 1.4 copy-done
  2.1 0.0 copy-start.5
  2.1 0.0 copy-start.2
  2.1 1.3 pack.1
  3.5 16.3 %collective-permute-start = (f32[4,4,8,128]{3,2,1,0:T(8,128)S(1)}, f32[4,4,8,128]{3,2,1,0:T(8,128)S(1)}, u32[]{:S(2)}, u32[]{:S(2)}) collective-permute-start(f32[4,4,8,128]{3,2,1,0:T(8,128)S(1)} %get-tuple-element.9), channel_id=1, source_target_pairs={{0,1},{1,0},{2,3},{3,2},{4,5},{5,4},{6,7},{7,6},{8,9},{9,8},{10,11... | collective-permute-start | bytes 196616 | tf_op jit(solution)/shard_map/ppermute | solution.py:263
  19.7 4.1 %collective-permute-start.1 = (f32[4,4,8,128]{3,2,1,0:T(8,128)S(1)}, f32[4,4,8,128]{3,2,1,0:T(8,128)S(1)}, u32[]{:S(2)}, u32[]{:S(2)}) collective-permute-start(f32[4,4,8,128]{3,2,1,0:T(8,128)S(1)} %get-tuple-element.10), channel_id=1, source_target_pairs={{0,7},{1,2},{2,1},{3,4},{4,3},{5,6},{6,5},{7,0},{8,15},{9,10},{10,... | collective-permute-start | bytes 196616 | tf_op jit(solution)/shard_map/ppermute | solution.py:264
  23.9 4.6 %collective-permute-start.5 = (f32[4,8,8,128]{3,2,1,0:T(8,128)S(1)}, f32[4,8,8,128]{3,2,1,0:T(8,128)S(1)}, u32[]{:S(2)}, u32[]{:S(2)}) collective-permute-start(f32[4,8,8,128]{3,2,1,0:T(8,128)S(1)} %get-tuple-element.13), channel_id=1, source_target_pairs={{128,0},{256,128},{384,256},{0,384},{129,1},{257,129},{385,257},{1... | collective-permute-start | bytes 393224 | tf_op jit(solution)/shard_map/ppermute | solution.py:268
  28.5 1.9 %collective-permute-start.4 = (f32[4,8,8,128]{3,2,1,0:T(8,128)S(1)}, f32[4,8,8,128]{3,2,1,0:T(8,128)S(1)}, u32[]{:S(2)}, u32[]{:S(2)}) collective-permute-start(f32[4,8,8,128]{3,2,1,0:T(8,128)S(1)} %get-tuple-element.13), channel_id=1, source_target_pairs={{0,128},{128,256},{256,384},{384,0},{1,129},{129,257},{257,385},{3... | collective-permute-start | bytes 393224 | tf_op jit(solution)/shard_map/ppermute | solution.py:267
  30.4 3.8 %collective-permute-start.2 = (f32[4,4,96,128]{3,2,1,0:T(8,128)S(1)}, f32[4,4,96,128]{3,2,1,0:T(8,128)S(1)}, u32[]{:S(2)}, u32[]{:S(2)}) collective-permute-start(f32[4,4,96,128]{3,2,1,0:T(8,128)S(1)} %get-tuple-element.11), channel_id=1, source_target_pairs={{0,120},{8,16},{16,8},{24,32},{32,24},{40,48},{48,40},{56,64},{64,... | collective-permute-start | bytes 2359304 | tf_op jit(solution)/shard_map/ppermute | solution.py:266
  34.2 0.0 collective-permute-done.za
  34.2 0.0 copy-start.1
  34.2 0.0 copy-start.3
  34.2 0.0 copy-start.4
  34.3 8.2 %collective-permute-start.3 = (f32[4,4,96,128]{3,2,1,0:T(8,128)S(1)}, f32[4,4,96,128]{3,2,1,0:T(8,128)S(1)}, u32[]{:S(2)}, u32[]{:S(2)}) collective-permute-start(f32[4,4,96,128]{3,2,1,0:T(8,128)S(1)} %get-tuple-element.12), channel_id=1, source_target_pairs={{0,8},{8,0},{1,9},{9,1},{2,10},{10,2},{3,11},{11,3},{4,12},{12,4},... | collective-permute-start | bytes 2359304 | tf_op jit(solution)/shard_map/ppermute | solution.py:265
  42.4 0.0 collective-permute-done.1.zb
  42.5 0.0 copy-done.2
  42.5 2.5 %along_z.1.base = f32[4,8,96,128]{3,2,1,0:T(8,128)S(1)} custom-call(s32[3]{0:T(128)S(1)} %pad_add_fusion.place, f32[4,8,96,128]{3,2,1,0:T(8,128)S(1)} %copy-done, f32[3,8,96,128]{3,2,1,0:T(8,128)S(1)} %copy-done.2, f32[4,4,8,128]{3,2,1,0:T(8,128)S(1)} %collective-permute-done.za, f32[4,4,8,128]{3,2,1,0:T(8,128)S(1)} %collective-permute-done.1.zb), custom_call_target="tpu_custom_call" | custom-call | flops 10000000000 | bytes 200000000 | tf_op jit(solution)/shard_map/along_z/pallas_call | solution.py:131
  44.9 0.0 collective-permute-done.5.xhigh
  45.0 0.0 collective-permute-done.4.xlow
  45.0 1.0 collective-permute-done.2.outer
  46.0 0.0 collective-permute-done.3.inner
  46.0 0.0 copy-done.1
  46.0 0.0 copy-done.3
  46.0 0.0 copy-done.4
  46.0 5.0 %along_xy.1 = f32[4,8,96,128]{3,2,1,0:T(8,128)} custom-call(s32[3]{0:T(128)S(1)} %pad_add_fusion.place, f32[4,8,96,128]{3,2,1,0:T(8,128)S(1)} %copy-done.1, f32[3,8,96,128]{3,2,1,0:T(8,128)S(1)} %copy-done.2, f32[4,8,96,128]{3,2,1,0:T(8,128)S(1)} %along_z.1.base, f32[4,4,96,128]{3,2,1,0:T(8,128)S(1)} %collective-permute-done.2.outer, ...), custom_call_target="tpu_custom_call" | custom-call | tf_op jit(solution)/shard_map/along_xy/pallas_call | solution.py:183
  51.0 17.5 %all_to_all.25.lines = f32[4,768,128]{2,1,0:T(8,128)S(1)} all-to-all(f32[4,768,128]{2,1,0:T(8,128)} %bitcast.6), channel_id=1, replica_groups=mesh['gx'=4,'zpair'=2,'znear'=4,'core'=2,'x'=4,'zhi'=2] {'gx'}, dimensions={0} | all-to-all | bytes 3145728 | tf_op jit(solution)/shard_map/all_to_all | solution.py:244
  68.4 0.0 copy-done.5
  68.4 2.0 %gram.1 = (f32[640,128]{1,0:T(8,128)S(1)}, f32[640,128]{1,0:T(8,128)S(1)}) custom-call(s32[3]{0:T(128)S(1)} %pad_add_fusion.place, f32[4,768,128]{2,1,0:T(8,128)S(1)} %all_to_all.25.lines), custom_call_target="tpu_custom_call" | custom-call | tf_op jit(solution)/shard_map/gram/pallas_call | solution.py:212
  70.4 16.6 %collective-permute-start.6 = (f32[640,128]{1,0:T(8,128)S(1)}, f32[640,128]{1,0:T(8,128)S(1)}, u32[]{:S(2)}, u32[]{:S(2)}) collective-permute-start(f32[640,128]{1,0:T(8,128)S(1)} %get-tuple-element.15), channel_id=1, source_target_pairs={{0,8},{8,0},{1,9},{9,1},{2,10},{10,2},{3,11},{11,3},{4,12},{12,4},... | collective-permute-start | bytes 983048 | tf_op jit(solution)/shard_map/ppermute | solution.py:274
  87.0 1.2 collective-permute-done.6
  88.3 11.7 %all_to_all.26 = f32[16,40,128]{2,1,0:T(8,128)S(1)} all-to-all(f32[16,40,128]{2,1,0:T(8,128)S(1)} %bitcast.9), channel_id=1, replica_groups=mesh['gx'=4,'zpair'=2,'znear'=4,'core'=2,'x'=4,'zhi'=2] {'gx','x'}, dimensions={0} | all-to-all | bytes 655360 | tf_op jit(solution)/shard_map/all_to_all | solution.py:244
  100.0 7.1 %all_to_all.27 = f32[4,40,128]{2,1,0:T(8,128)S(1)} all-to-all(f32[4,40,128]{2,1,0:T(8,128)S(1)} %broadcast_in_dim.9), channel_id=1, replica_groups=mesh['gx'=4,'zpair'=2,'znear'=4,'core'=2,'x'=4,'zhi'=2] {'znear'}, dimensions={0} | all-to-all | bytes 163840 | tf_op jit(solution)/shard_map/all_to_all | solution.py:244
  107.1 21.0 %all_to_all.28 = f32[4,40,128]{2,1,0:T(8,128)S(1)} all-to-all(f32[4,40,128]{2,1,0:T(8,128)S(1)} %broadcast_in_dim.10), channel_id=1, replica_groups=mesh['gx'=4,'zpair'=2,'znear'=4,'core'=2,'x'=4,'zhi'=2] {'zpair','zhi'}, dimensions={0} | all-to-all | bytes 163840 | tf_op jit(solution)/shard_map/all_to_all | solution.py:244
  128.1 10.8 %all_to_all.29 = f32[16,40,128]{2,1,0:T(8,128)S(1)} all-to-all(f32[16,40,128]{2,1,0:T(8,128)S(1)} %broadcast_in_dim.11), channel_id=1, replica_groups=mesh['gx'=4,'zpair'=2,'znear'=4,'core'=2,'x'=4,'zhi'=2] {'gx','x'}, dimensions={0} | all-to-all | bytes 655360 | tf_op jit(solution)/shard_map/all_to_all | solution.py:244
  138.9 0.0 copy-start.6
  138.9 7.1 %collective-permute-start.7 = (f32[640,128]{1,0:T(8,128)S(1)}, f32[640,128]{1,0:T(8,128)S(1)}, u32[]{:S(2)}, u32[]{:S(2)}) collective-permute-start(f32[640,128]{1,0:T(8,128)S(1)} %bitcast.7), channel_id=1, source_target_pairs={{0,8},{8,0},{1,9},{9,1},{2,10},{10,2},{3,11},{11,3},{4,12},{12,4},... | collective-permute-start | bytes 983048 | tf_op jit(solution)/shard_map/ppermute | solution.py:280
  146.0 1.2 collective-permute-done.7.other
  147.3 0.0 copy-done.6
  147.3 0.0 copy-start.7
  147.3 0.7 copy-done.7
  148.0 1.9 %gram_rows.1 = f32[128,512]{1,0:T(8,128)} custom-call(s32[3]{0:T(128)} %copy-done.5, f32[640,128]{1,0:T(8,128)} %bitcast.8, f32[640,128]{1,0:T(8,128)} %copy-done.7), custom_call_target="tpu_custom_call" | custom-call | tf_op jit(solution)/shard_map/gram_rows/pallas_call | solution.py:234
  (7 shorter events, 0.1 us)
Async XLA Ops:
  0.7 1.4 copy-start
  2.1 66.3 %copy-start.5 = (s32[3]{0:T(128)}, s32[3]{0:T(128)S(1)}, u32[]{:S(2)}) copy-start(s32[3]{0:T(128)S(1)} %pad_add_fusion.place) | copy-start | bytes 40
  2.1 40.3 %copy-start.2 = (f32[3,8,96,128]{3,2,1,0:T(8,128)S(1)}, f32[3,8,96,128]{3,2,1,0:T(8,128)}, u32[]{:S(2)}) copy-start(f32[3,8,96,128]{3,2,1,0:T(8,128)} %vel.3) | copy-start | bytes 3538948
  3.5 30.8 %collective-permute-start = (f32[4,4,8,128]{3,2,1,0:T(8,128)S(1)}, f32[4,4,8,128]{3,2,1,0:T(8,128)S(1)}, u32[]{:S(2)}, u32[]{:S(2)}) collective-permute-start(f32[4,4,8,128]{3,2,1,0:T(8,128)S(1)} %get-tuple-element.9), channel_id=1, source_target_pairs={{0,1},{1,0},{2,3},{3,2},{4,5},{5,4},{6,7},{7,6},{8,9},{9,8},{10,11... | collective-permute-start | bytes 196616 | tf_op jit(solution)/shard_map/ppermute | solution.py:263
  19.7 22.7 %collective-permute-start.1 = (f32[4,4,8,128]{3,2,1,0:T(8,128)S(1)}, f32[4,4,8,128]{3,2,1,0:T(8,128)S(1)}, u32[]{:S(2)}, u32[]{:S(2)}) collective-permute-start(f32[4,4,8,128]{3,2,1,0:T(8,128)S(1)} %get-tuple-element.10), channel_id=1, source_target_pairs={{0,7},{1,2},{2,1},{3,4},{4,3},{5,6},{6,5},{7,0},{8,15},{9,10},{10,... | collective-permute-start | bytes 196616 | tf_op jit(solution)/shard_map/ppermute | solution.py:264
  23.9 21.1 %collective-permute-start.5 = (f32[4,8,8,128]{3,2,1,0:T(8,128)S(1)}, f32[4,8,8,128]{3,2,1,0:T(8,128)S(1)}, u32[]{:S(2)}, u32[]{:S(2)}) collective-permute-start(f32[4,8,8,128]{3,2,1,0:T(8,128)S(1)} %get-tuple-element.13), channel_id=1, source_target_pairs={{128,0},{256,128},{384,256},{0,384},{129,1},{257,129},{385,257},{1... | collective-permute-start | bytes 393224 | tf_op jit(solution)/shard_map/ppermute | solution.py:268
  28.5 16.4 %collective-permute-start.4 = (f32[4,8,8,128]{3,2,1,0:T(8,128)S(1)}, f32[4,8,8,128]{3,2,1,0:T(8,128)S(1)}, u32[]{:S(2)}, u32[]{:S(2)}) collective-permute-start(f32[4,8,8,128]{3,2,1,0:T(8,128)S(1)} %get-tuple-element.13), channel_id=1, source_target_pairs={{0,128},{128,256},{256,384},{384,0},{1,129},{129,257},{257,385},{3... | collective-permute-start | bytes 393224 | tf_op jit(solution)/shard_map/ppermute | solution.py:267
  30.4 15.5 %collective-permute-start.2 = (f32[4,4,96,128]{3,2,1,0:T(8,128)S(1)}, f32[4,4,96,128]{3,2,1,0:T(8,128)S(1)}, u32[]{:S(2)}, u32[]{:S(2)}) collective-permute-start(f32[4,4,96,128]{3,2,1,0:T(8,128)S(1)} %get-tuple-element.11), channel_id=1, source_target_pairs={{0,120},{8,16},{16,8},{24,32},{32,24},{40,48},{48,40},{56,64},{64,... | collective-permute-start | bytes 2359304 | tf_op jit(solution)/shard_map/ppermute | solution.py:266
  34.2 11.8 %copy-start.1 = (f32[4,8,96,128]{3,2,1,0:T(8,128)S(1)}, f32[4,8,96,128]{3,2,1,0:T(8,128)}, u32[]{:S(2)}) copy-start(f32[4,8,96,128]{3,2,1,0:T(8,128)} %y.5) | copy-start | bytes 4718596
  34.2 11.8 %copy-start.3 = (bf16[256,256]{1,0:T(8,128)(2,1)S(1)}, bf16[256,256]{1,0:T(8,128)(2,1)}, u32[]{:S(2)}) copy-start(bf16[256,256]{1,0:T(8,128)(2,1)} %constant.20.clone.ml) | copy-start | bytes 393220
  34.2 11.7 %copy-start.4 = (bf16[256,256]{1,0:T(8,128)(2,1)S(1)}, bf16[256,256]{1,0:T(8,128)(2,1)}, u32[]{:S(2)}) copy-start(bf16[256,256]{1,0:T(8,128)(2,1)} %constant.19.clone.mh) | copy-start | bytes 393220
  34.3 11.7 %collective-permute-start.3 = (f32[4,4,96,128]{3,2,1,0:T(8,128)S(1)}, f32[4,4,96,128]{3,2,1,0:T(8,128)S(1)}, u32[]{:S(2)}, u32[]{:S(2)}) collective-permute-start(f32[4,4,96,128]{3,2,1,0:T(8,128)S(1)} %get-tuple-element.12), channel_id=1, source_target_pairs={{0,8},{8,0},{1,9},{9,1},{2,10},{10,2},{3,11},{11,3},{4,12},{12,4},... | collective-permute-start | bytes 2359304 | tf_op jit(solution)/shard_map/ppermute | solution.py:265
  70.4 17.8 %collective-permute-start.6 = (f32[640,128]{1,0:T(8,128)S(1)}, f32[640,128]{1,0:T(8,128)S(1)}, u32[]{:S(2)}, u32[]{:S(2)}) collective-permute-start(f32[640,128]{1,0:T(8,128)S(1)} %get-tuple-element.15), channel_id=1, source_target_pairs={{0,8},{8,0},{1,9},{9,1},{2,10},{10,2},{3,11},{11,3},{4,12},{12,4},... | collective-permute-start | bytes 983048 | tf_op jit(solution)/shard_map/ppermute | solution.py:274
  138.9 8.4 %copy-start.6 = (f32[16,40,128]{2,1,0:T(8,128)}, f32[16,40,128]{2,1,0:T(8,128)S(1)}, u32[]{:S(2)}) copy-start(f32[16,40,128]{2,1,0:T(8,128)S(1)} %all_to_all.29) | copy-start | bytes 983044
  138.9 8.3 %collective-permute-start.7 = (f32[640,128]{1,0:T(8,128)S(1)}, f32[640,128]{1,0:T(8,128)S(1)}, u32[]{:S(2)}, u32[]{:S(2)}) collective-permute-start(f32[640,128]{1,0:T(8,128)S(1)} %bitcast.7), channel_id=1, source_target_pairs={{0,8},{8,0},{1,9},{9,1},{2,10},{10,2},{3,11},{11,3},{4,12},{12,4},... | collective-permute-start | bytes 983048 | tf_op jit(solution)/shard_map/ppermute | solution.py:280
  147.3 0.7 copy-start.7

commit v4 on v2

--- a/solution.py
+++ b/solution.py
@@ -87,73 +87,117 @@
     )(place, y)
 
 
-def stencil_body(place, y, vel, inner, outer, za, zb, xlow, xhigh, mh, ml, out, rate, side, dx, pad):
-    count, rows, depth, width = y.shape
-    core, half = place[1], place[2]
+def factors(s, count):
+    diff = jnp.float32(0.25 * DIFF[0])
+    nu = jnp.float32(NU[0])
+    for q in range(1, count):
+        diff = jnp.where(s == q, jnp.float32(0.25 * DIFF[q]), diff)
+        nu = jnp.where(s == q, jnp.float32(NU[q]), nu)
+    return diff, nu
+
+
+def layers_body(front, place, y, vel, face, zs, xlow, xhigh, mh, ml, out, side, dx, pad):
+    count, rows, depth, width = y.shape
+    ahead_of = place[1] == front
+    start = jnp.where(ahead_of, 0, 4)
     below = lanes() % 8 < 4
-    for j in range(rows):
-        heat = 1.0 + 3.0 * y[2, j]
-        rate[j] = y[0, j] * y[1, j] * jnp.exp(-3.0 / heat)
+    spot = pl.ds(8, depth)
 
     def species(s, carry):
-        diff = jnp.float32(0.25 * DIFF[0])
-        nu = jnp.float32(NU[0])
-        for q in range(1, count):
-            diff = jnp.where(s == q, jnp.float32(0.25 * DIFF[q]), diff)
-            nu = jnp.where(s == q, jnp.float32(NU[q]), nu)
-        pad[pl.ds(12 * (1 - core), 4), 8 : 8 + depth] = inner[s]
-        pad[pl.ds(12 * core, 4), 8 : 8 + depth] = outer[s]
-        for j in range(rows):
-            at = 4 * (j % 2)
-            fa, fb = za[s, j // 2, at : at + 4], zb[s, j // 2, at : at + 4]
-            pad[4 + j, 4:8] = jnp.where(half == 0, fb, fa)
-            pad[4 + j, 8 : 8 + depth] = y[s, j]
-            pad[4 + j, 8 + depth : 12 + depth] = jnp.where(half == 0, fa, fb)
-            packed = jnp.where(below, xlow[s, j], xhigh[s, j])
+        diff, nu = factors(s, count)
+        pad[pl.ds(4 - start, rows), spot] = y[s]
+        pad[pl.ds(2 * start, 4), spot] = face[s]
+        for i in range(4):
+            at = 4 * (i % 2)
+            tile = start // 2 + i // 2
+            pad[4 + i, 4:8] = zs[0, s, tile, at : at + 4]
+            pad[4 + i, 8 + depth : 12 + depth] = zs[1, s, tile, at : at + 4]
+            packed = jnp.where(below, xlow[s, start + i], xhigh[s, start + i])
             for g in range(depth // 8):
-                row = j * depth + 8 * g
+                row = i * depth + 8 * g
                 side[row : row + 8] = pltpu.roll(packed, (128 - 8 * g) % 128, 1)
-        left = jnp.concatenate([y[s].reshape(rows * depth, width), side[...]], axis=1)
-        high, low = split(left)
+        own = y[s, pl.ds(start, 4)].reshape(4 * depth, width)
+        high, low = split(jnp.concatenate([own, side[...]], axis=1))
         dx[...] = dot(high, mh[...]) + (dot(low, mh[...]) + dot(high, ml[...]))
-        for j in range(rows):
-            centre = y[s, j]
+        for i in range(4):
+            centre = y[s, start + i]
             d1y = d1z = None
-            second = (2.0 * C2[0]) * centre + dx[j * depth : (j + 1) * depth, width:]
+            second = (2.0 * C2[0]) * centre + dx[i * depth : (i + 1) * depth, width:]
             for k in range(1, 5):
-                ya, yb = pad[4 + j + k, 8 : 8 + depth], pad[4 + j - k, 8 : 8 + depth]
-                za_, zb_ = pad[4 + j, 8 + k : 8 + k + depth], pad[4 + j, 8 - k : 8 - k + depth]
-                ty, tz = C1[k - 1] * (ya - yb), C1[k - 1] * (za_ - zb_)
+                ya, yb = pad[4 + i + k, 8 : 8 + depth], pad[4 + i - k, 8 : 8 + depth]
+                na, nb = pad[4 + i, 8 + k : 8 + k + depth], pad[4 + i, 8 - k : 8 - k + depth]
+                ty, tz = (0.25 * C1[k - 1]) * (ya - yb), (0.25 * C1[k - 1]) * (na - nb)
                 d1y = ty if d1y is None else d1y + ty
                 d1z = tz if d1z is None else d1z + tz
-                second = second + C2[k] * ((ya + yb) + (za_ + zb_))
-            moved = vel[0, j] * dx[j * depth : (j + 1) * depth, :width]
-            moved = moved + vel[1, j] * d1y + vel[2, j] * d1z
-            out[s, j] = centre + (diff * second - 0.25 * moved + nu * rate[j])
+                second = second + C2[k] * ((ya + yb) + (na + nb))
+            moved = (0.25 * vel[0, start + i]) * dx[i * depth : (i + 1) * depth, :width]
+            moved = moved + (vel[1, start + i] * d1y + vel[2, start + i] * d1z)
+            heat = 1.0 + 3.0 * y[2, start + i]
+            rate = y[0, start + i] * y[1, start + i] * jnp.exp(-3.0 / heat)
+            out[s, i] = centre + (diff * second - moved + nu * rate)
         return carry
 
     lax.fori_loop(0, count, species, 0)
 
 
-def stencil(place, y, *rest):
-    _, rows, depth, width = y.shape
-    return pl.pallas_call(
-        stencil_body,
-        out_shape=jax.ShapeDtypeStruct(y.shape, jnp.float32),
+def layers(front, place, y, *rest):
+    count, rows, depth, width = y.shape
+    return pl.pallas_call(
+        functools.partial(layers_body, front),
+        out_shape=jax.ShapeDtypeStruct((count, 4, depth, width), jnp.float32),
         in_specs=[SMEM] + [VMEM] * (1 + len(rest)),
         out_specs=VMEM,
         scratch_shapes=[
-            pltpu.VMEM((rows, depth, width), jnp.float32),
-            pltpu.VMEM((rows * depth, width), jnp.float32),
-            pltpu.VMEM((rows * depth, 2 * width), jnp.float32),
-            pltpu.VMEM((rows + 8, depth + 16, width), jnp.float32),
+            pltpu.VMEM((4 * depth, width), jnp.float32),
+            pltpu.VMEM((4 * depth, 2 * width), jnp.float32),
+            pltpu.VMEM((12, depth + 16, width), jnp.float32),
         ],
-        compiler_params=pltpu.CompilerParams(vmem_limit_bytes=40 * MIB),
-        name="stencil",
+        compiler_params=pltpu.CompilerParams(vmem_limit_bytes=24 * MIB),
+        cost_estimate=pl.CostEstimate(
+            flops=10**8, bytes_accessed=6 * 10**6, transcendentals=0
+        ),
+        name="layers",
     )(place, y, *rest)
 
 
-def gram_body(place, lines, mine, other):
+def z_faces_body(place, za, zb, out):
+    out[0] = jnp.where(place[2] == 0, zb[...], za[...])
+    out[1] = jnp.where(place[2] == 0, za[...], zb[...])
+
+
+def z_faces(place, za, zb):
+    return pl.pallas_call(
+        z_faces_body,
+        out_shape=jax.ShapeDtypeStruct((2,) + za.shape, jnp.float32),
+        in_specs=[SMEM, VMEM, VMEM],
+        out_specs=VMEM,
+        cost_estimate=pl.CostEstimate(
+            flops=18 * 10**8, bytes_accessed=10**7, transcendentals=0
+        ),
+        name="z_faces",
+    )(place, za, zb)
+
+
+def join_body(place, inner, outer, out):
+    core = place[1]
+    out[:, pl.ds(4 - 4 * core, 4)] = inner[...]
+    out[:, pl.ds(4 * core, 4)] = outer[...]
+
+
+def join(place, inner, outer):
+    count, rows, depth, width = inner.shape
+    return pl.pallas_call(
+        join_body,
+        out_shape=jax.ShapeDtypeStruct((count, 2 * rows, depth, width), jnp.float32),
+        in_specs=[SMEM, VMEM, VMEM],
+        out_specs=VMEM,
+        compiler_params=pltpu.CompilerParams(vmem_limit_bytes=24 * MIB),
+        name="join",
+    )(place, inner, outer)
+
+
+def gram_body(place, lines, *rest):
+    *before, mine, other = rest
     parts = lines.shape[0]
     whole = jnp.concatenate([lines[a] for a in range(parts)], axis=1)
     high, low = split(whole)
@@ -161,20 +205,24 @@
     total = dot(turned_high, high) + (dot(turned_high, low) + dot(turned_low, high))
     tiles = [total[a * 128 : (a + 1) * 128, b * 128 : (b + 1) * 128] for a, b in PAIRS]
     for q in range(5):
-        first, second = tiles[q], tiles[q + 5]
-        mine[q * 128 : (q + 1) * 128] = jnp.where(place[1] == 0, first, second)
-        other[q * 128 : (q + 1) * 128] = jnp.where(place[1] == 0, second, first)
-
-
-def gram_blocks(place, lines):
+        at = slice(q * 128, (q + 1) * 128)
+        first = jnp.where(place[1] == 0, tiles[q], tiles[q + 5])
+        second = jnp.where(place[1] == 0, tiles[q + 5], tiles[q])
+        if before:
+            first, second = first + before[0][at], second + before[1][at]
+        mine[at] = first
+        other[at] = second
+
+
+def gram_blocks(place, lines, *before):
     return pl.pallas_call(
         gram_body,
         out_shape=[jax.ShapeDtypeStruct((len(PAIRS) * 64, 128), jnp.float32)] * 2,
-        in_specs=[SMEM, VMEM],
+        in_specs=[SMEM] + [VMEM] * (1 + len(before)),
         out_specs=[VMEM] * 2,
-        compiler_params=pltpu.CompilerParams(vmem_limit_bytes=40 * MIB),
+        compiler_params=pltpu.CompilerParams(vmem_limit_bytes=32 * MIB),
         name="gram",
-    )(place, lines)
+    )(place, lines, *before)
 
 
 def rows_body(scale, place, mine, other, out):
@@ -220,14 +268,17 @@
     swap = [(0, 1), (1, 0)]
     za = lax.ppermute(za, "zhi", swap)
     zb = lax.ppermute(zb, gz, cross(8))
+    inner = lax.ppermute(inner, "core", swap)
     outer = lax.ppermute(outer, gy, cross(16))
-    inner = lax.ppermute(inner, "core", swap)
     xlow = lax.ppermute(xs, gx, up)
     xhigh = lax.ppermute(xs, gx, [(target, source) for source, target in up])
-    updated = stencil(place, y, vel, inner, outer, za, zb, xlow, xhigh, *x_matrices(width))
-
-    lines = exchange(updated.reshape(4, species * rows * depth // 4, width), gx)
-    mine, other = gram_blocks(place, lines)
+    rest = (z_faces(place, za, zb), xlow, xhigh) + x_matrices(width)
+    near = layers(1, place, y, vel, inner, *rest)
+    pieces = (4, species * depth, width)
+    sums = gram_blocks(place, exchange(near.reshape(pieces), gx))
+    far = layers(0, place, y, vel, outer, *rest)
+    mine, other = gram_blocks(place, exchange(far.reshape(pieces), gx), *sums)
+    updated = join(place, near, far)
     mine = mine + lax.ppermute(other, "core", swap)
     plane = ("gx", "x")
     part = jnp.sum(exchange(mine.reshape(16, -1, 128), plane), axis=0)

time: 163 us -> 156 us (0.957)
  blocking collectives: 68.7 us -> 51.3 us
  waiting for transfers between devices: 26.8 us -> 12.9 us
  starting transfers between devices: 49.2 us -> 59.1 us
  Pallas kernels: 11.7 us -> 21.5 us
  local copies, waits for them, and re-layouts: 5.25 us -> 8.9 us
    all_to_all x5 -> x4, blocking collectives: 68.7 us -> 51.3 us  [exchange(): return lax.all_to_all(pieces, axes, split_axis=0, concat_axis=0, tiled=True)]
    ppermute x1, waiting for transfers between devices: 10.4 us -> 0.01 us  [shards(): za = lax.ppermute(za, 'zhi', swap)]
    ppermute x1, waiting for transfers between devices: 13.8 us -> 4.34 us  [shards(): zb = lax.ppermute(zb, gz, cross(8))]
    all_to_all x0 -> x2, starting transfers between devices: none -> 8 us  [exchange(): return lax.all_to_all(pieces, axes, split_axis=0, concat_axis=0, tiled=True)]
    pallas_call x1 -> x4, Pallas kernels: 6.45 us -> 14 us  [the longest x2 9.83 us: layers(): pl.pallas_call(functools.partial(layers_body, front), out_shape=jax.Shape...]
    all_to_all x0 -> x2, waiting for transfers between devices: none -> 7.32 us  [exchange(): return lax.all_to_all(pieces, axes, split_axis=0, concat_axis=0, tiled=True)]
    unnamed x16 -> x30, local copies, waits for them, and re-layouts: 5.21 us -> 8.86 us
    ppermute x1, starting transfers between devices: 1.98 us -> 4.12 us  [shards(): zb = lax.ppermute(zb, gz, cross(8))]
  transfers between devices with their start and end apart: 8 -> 10, of which waited for: 4 -> 4; matrix products, arithmetic and copies ran while one was open for 0% -> 0% of each run, Pallas kernels for 0% -> 10%
where the time goes in v4:
time: 156 us; the launch traced here: 155 us
  starting transfers between devices  59.1 us (38%)
  blocking collectives  51.3 us (33%)
  Pallas kernels  21.5 us (14%)
  waiting for transfers between devices  12.9 us (8%)
  local copies, waits for them, and re-layouts  8.9 us (6%)
    all_to_all x4, blocking collectives, exchange(): return lax.all_to_all(pieces, axes, split_axis=0, concat_axis=0, tiled=True)  51.3 us
    ppermute x1, starting transfers between devices, shards(): mine = mine + lax.ppermute(other, 'core', swap)  11.2 us
    ppermute x1, starting transfers between devices, shards(): za = lax.ppermute(za, 'zhi', swap)  10.1 us
    pallas_call x2, Pallas kernels, layers(): pl.pallas_call(functools.partial(layers_body, front), out_shape=jax.Shape...  9.83 us
    unnamed x30, local copies, waits for them, and re-layouts  8.86 us
    ppermute x1, starting transfers between devices, shards(): inner = lax.ppermute(inner, 'core', swap)  8.77 us
    all_to_all x2, starting transfers between devices, exchange(): return lax.all_to_all(pieces, axes, split_axis=0, concat_axis=0, tiled=True)  8 us
    all_to_all x2, waiting for transfers between devices, exchange(): return lax.all_to_all(pieces, axes, split_axis=0, concat_axis=0, tiled=True)  7.32 us
  transfers between devices with their start and end apart: 10, of which 4 were waited for; matrix products, arithmetic and copies ran while one was open for 0% of the time, Pallas kernels for 10%

profile of v4, /device:TPU:1, one launch (start us, length us, event | category | flops | bytes accessed | tf_op | source)
XLA Modules:
  0.0 154.6 jit_solution(5264883764638122774)
XLA Ops:
  0.6 0.1 pad_add_fusion.place
  0.7 0.0 copy-start
  0.7 1.4 copy-done
  2.1 0.0 copy-start.9
  2.1 2.4 %pack.1 = (f32[4,4,96,128]{3,2,1,0:T(8,128)}, f32[4,4,96,128]{3,2,1,0:T(8,128)}, f32[4,4,8,128]{3,2,1,0:T(8,128)S(1)}, f32[4,4,8,128]{3,2,1,0:T(8,128)S(1)}, f32[4,8,8,128]{3,2,1,0:T(8,128)}) custom-call(s32[3]{0:T(128)S(1)} %pad_add_fusion.place, f32[4,8,96,128]{3,2,1,0:T(8,128)S(1)} %copy-done), custom_call_target="tpu_custom_call" | custom-call | tf_op jit(solution)/shard_map/pack/pallas_call | solution.py:80
  4.5 8.8 %collective-permute-start = (f32[4,4,96,128]{3,2,1,0:T(8,128)}, f32[4,4,96,128]{3,2,1,0:T(8,128)S(1)}, u32[]{:S(2)}, u32[]{:S(2)}) collective-permute-start(f32[4,4,96,128]{3,2,1,0:T(8,128)} %get-tuple-element.11), channel_id=1, source_target_pairs={{0,8},{8,0},{1,9},{9,1},{2,10},{10,2},{3,11},{11,3},{4,12},{12,4},... | collective-permute-start | bytes 2359304 | tf_op jit(solution)/shard_map/ppermute | solution.py:271
  13.3 10.1 %collective-permute-start.1 = (f32[4,4,8,128]{3,2,1,0:T(8,128)S(1)}, f32[4,4,8,128]{3,2,1,0:T(8,128)S(1)}, u32[]{:S(2)}, u32[]{:S(2)}) collective-permute-start(f32[4,4,8,128]{3,2,1,0:T(8,128)S(1)} %get-tuple-element.12), channel_id=1, source_target_pairs={{0,1},{1,0},{2,3},{3,2},{4,5},{5,4},{6,7},{7,6},{8,9},{9,8},{10,11... | collective-permute-start | bytes 196616 | tf_op jit(solution)/shard_map/ppermute | solution.py:269
  23.4 4.1 %collective-permute-start.2 = (f32[4,4,8,128]{3,2,1,0:T(8,128)S(1)}, f32[4,4,8,128]{3,2,1,0:T(8,128)}, u32[]{:S(2)}, u32[]{:S(2)}) collective-permute-start(f32[4,4,8,128]{3,2,1,0:T(8,128)S(1)} %get-tuple-element.13), channel_id=1, source_target_pairs={{0,7},{1,2},{2,1},{3,4},{4,3},{5,6},{6,5},{7,0},{8,15},{9,10},{10,... | collective-permute-start | bytes 196616 | tf_op jit(solution)/shard_map/ppermute | solution.py:270
  27.5 2.8 %collective-permute-start.5 = (f32[4,4,96,128]{3,2,1,0:T(8,128)}, f32[4,4,96,128]{3,2,1,0:T(8,128)}, u32[]{:S(2)}, u32[]{:S(2)}) collective-permute-start(f32[4,4,96,128]{3,2,1,0:T(8,128)} %get-tuple-element.15), channel_id=1, source_target_pairs={{0,120},{8,16},{16,8},{24,32},{32,24},{40,48},{48,40},{56,64},{64,... | collective-permute-start | bytes 2359304 | tf_op jit(solution)/shard_map/ppermute | solution.py:272
  30.3 0.0 copy-start.1
  30.4 0.0 copy-start.2
  30.4 4.9 %collective-permute-start.4 = (f32[4,8,8,128]{3,2,1,0:T(8,128)}, f32[4,8,8,128]{3,2,1,0:T(8,128)}, u32[]{:S(2)}, u32[]{:S(2)}) collective-permute-start(f32[4,8,8,128]{3,2,1,0:T(8,128)} %get-tuple-element.14), channel_id=1, source_target_pairs={{128,0},{256,128},{384,256},{0,384},{129,1},{257,129},{385,257},{1... | collective-permute-start | bytes 393224 | tf_op jit(solution)/shard_map/ppermute | solution.py:274
  35.3 0.0 collective-permute-done.1.za
  35.3 0.0 copy-start.14
  35.3 0.6 copy-done.14
  35.9 1.9 %collective-permute-start.3 = (f32[4,8,8,128]{3,2,1,0:T(8,128)}, f32[4,8,8,128]{3,2,1,0:T(8,128)}, u32[]{:S(2)}, u32[]{:S(2)}) collective-permute-start(f32[4,8,8,128]{3,2,1,0:T(8,128)} %get-tuple-element.14), channel_id=1, source_target_pairs={{0,128},{128,256},{256,384},{384,0},{1,129},{129,257},{257,385},{3... | collective-permute-start | bytes 393224 | tf_op jit(solution)/shard_map/ppermute | solution.py:273
  37.8 4.3 %collective-permute-done.2.zb = f32[4,4,8,128]{3,2,1,0:T(8,128)} collective-permute-done((f32[4,4,8,128]{3,2,1,0:T(8,128)S(1)}, f32[4,4,8,128]{3,2,1,0:T(8,128)}, u32[]{:S(2)}, u32[]{:S(2)}) %collective-permute-start.2) | collective-permute-done | bytes 65568 | tf_op jit(solution)/shard_map/ppermute | solution.py:270
  42.2 0.0 copy-done.9
  42.2 1.6 %z_faces.1.zs = f32[2,4,4,8,128]{4,3,2,1,0:T(8,128)} custom-call(s32[3]{0:T(128)} %copy-done.9, f32[4,4,8,128]{3,2,1,0:T(8,128)} %copy-done.14, f32[4,4,8,128]{3,2,1,0:T(8,128)} %collective-permute-done.2.zb), custom_call_target="tpu_custom_call" | custom-call | flops 1800000000 | bytes 10000000 | tf_op jit(solution)/shard_map/z_faces/pallas_call | solution.py:169
  43.7 0.0 collective-permute-done.4.xhigh
  43.7 0.0 collective-permute-done.3.xlow
  43.7 0.0 collective-permute-done.face
  43.7 0.0 copy-done.1
  43.7 0.0 copy-done.2
  43.8 0.0 copy-start.3
  43.8 0.9 copy-done.3
  44.7 0.0 copy-start.5
  44.7 0.9 copy-done.5
  45.6 0.0 copy-start.7
  45.6 0.9 copy-done.7
  46.5 0.0 copy-start.10
  46.5 0.7 copy-done.10
  47.1 4.8 %layers.2.inner = f32[4,4,96,128]{3,2,1,0:T(8,128)} custom-call(s32[3]{0:T(128)S(1)} %copy-done.10, f32[4,8,96,128]{3,2,1,0:T(8,128)S(1)} %copy-done.1, f32[3,8,96,128]{3,2,1,0:T(8,128)S(1)} %copy-done.2, f32[4,4,96,128]{3,2,1,0:T(8,128)S(1)} %collective-permute-done.face, f32[2,4,4,8,128]{4,3,2,1,0:T(8,128)S(1)} %copy-done.7, ...), custom_call_target="tpu_custom_call" | custom-call | flops 100000000 | bytes 6000000 | tf_op jit(solution)/shard_map/layers/pallas_call | solution.py:145
  51.9 0.0 copy-start.11
  51.9 4.3 %all-to-all-start.1 = ((f32[4,384,128]{2,1,0:T(8,128)}), f32[4,384,128]{2,1,0:T(8,128)S(1)}, u32[]{:S(2)}, u32[]{:S(2)}) async-start(f32[4,384,128]{2,1,0:T(8,128)} %bitcast.4), calls=%async_computation.1 | async-start | bytes 1572864 | tf_op jit(solution)/shard_map/all_to_all | solution.py:250
  56.2 0.0 collective-permute-done.5.face
  56.2 0.0 copy-done.11
  56.2 0.0 copy-start.4
  56.3 0.9 copy-done.4
  57.2 0.0 copy-start.6
  57.2 0.9 copy-done.6
  58.1 0.0 copy-start.8
  58.1 0.9 copy-done.8
  59.0 5.1 %layers.3.outer = f32[4,4,96,128]{3,2,1,0:T(8,128)} custom-call(s32[3]{0:T(128)S(1)} %copy-done.11, f32[4,8,96,128]{3,2,1,0:T(8,128)S(1)} %copy-done.1, f32[3,8,96,128]{3,2,1,0:T(8,128)S(1)} %copy-done.2, f32[4,4,96,128]{3,2,1,0:T(8,128)} %collective-permute-done.5.face, f32[2,4,4,8,128]{4,3,2,1,0:T(8,128)S(1)} %copy-done.8, ...), custom_call_target="tpu_custom_call" | custom-call | flops 100000000 | bytes 6000000 | tf_op jit(solution)/shard_map/layers/pallas_call | solution.py:145
  64.0 0.6 all-to-all-done.1.lines
  64.6 3.7 %all-to-all-start = ((f32[4,384,128]{2,1,0:T(8,128)}), f32[4,384,128]{2,1,0:T(8,128)S(1)}, u32[]{:S(2)}, u32[]{:S(2)}) async-start(f32[4,384,128]{2,1,0:T(8,128)} %bitcast.3), calls=%async_computation | async-start | bytes 1572864 | tf_op jit(solution)/shard_map/all_to_all | solution.py:250
  68.3 1.6 %gram.2 = (f32[640,128]{1,0:T(8,128)S(1)}, f32[640,128]{1,0:T(8,128)S(1)}) custom-call(s32[3]{0:T(128)S(1)} %copy-done.11, f32[4,384,128]{2,1,0:T(8,128)S(1)} %all-to-all-done.1.lines), custom_call_target="tpu_custom_call" | custom-call | tf_op jit(solution)/shard_map/gram/pallas_call | solution.py:218
  69.8 6.8 %all-to-all-done.lines = f32[4,384,128]{2,1,0:T(8,128)S(1)} async-done(((f32[4,384,128]{2,1,0:T(8,128)}), f32[4,384,128]{2,1,0:T(8,128)S(1)}, u32[]{:S(2)}, u32[]{:S(2)}) %all-to-all-start) | async-done | bytes 786464 | tf_op jit(solution)/shard_map/all_to_all | solution.py:250
  76.6 1.6 %gram.3 = (f32[640,128]{1,0:T(8,128)S(1)}, f32[640,128]{1,0:T(8,128)S(1)}) custom-call(s32[3]{0:T(128)S(1)} %copy-done.11, f32[4,384,128]{2,1,0:T(8,128)S(1)} %all-to-all-done.lines, f32[640,128]{1,0:T(8,128)S(1)} %get-tuple-element.16.rest_0_, f32[640,128]{1,0:T(8,128)S(1)} %get-tuple-element.17.rest_1_), custom_call_target="tpu_custom_call" | custom-call | tf_op jit(solution)/shard_map/gram/pallas_call | solution.py:218
  78.2 11.2 %collective-permute-start.6 = (f32[640,128]{1,0:T(8,128)S(1)}, f32[640,128]{1,0:T(8,128)S(1)}, u32[]{:S(2)}, u32[]{:S(2)}) collective-permute-start(f32[640,128]{1,0:T(8,128)S(1)} %get-tuple-element.19), channel_id=1, source_target_pairs={{0,8},{8,0},{1,9},{9,1},{2,10},{10,2},{3,11},{11,3},{4,12},{12,4},... | collective-permute-start | bytes 983048 | tf_op jit(solution)/shard_map/ppermute | solution.py:282
  89.4 1.2 collective-permute-done.6
  90.6 11.6 %all_to_all.30 = f32[16,40,128]{2,1,0:T(8,128)S(1)} all-to-all(f32[16,40,128]{2,1,0:T(8,128)S(1)} %bitcast.9), channel_id=1, replica_groups=mesh['gx'=4,'zpair'=2,'znear'=4,'core'=2,'x'=4,'zhi'=2] {'gx','x'}, dimensions={0} | all-to-all | bytes 655360 | tf_op jit(solution)/shard_map/all_to_all | solution.py:250
  102.3 8.0 %all_to_all.31 = f32[4,40,128]{2,1,0:T(8,128)S(1)} all-to-all(f32[4,40,128]{2,1,0:T(8,128)S(1)} %broadcast_in_dim.9), channel_id=1, replica_groups=mesh['gx'=4,'zpair'=2,'znear'=4,'core'=2,'x'=4,'zhi'=2] {'znear'}, dimensions={0} | all-to-all | bytes 163840 | tf_op jit(solution)/shard_map/all_to_all | solution.py:250
  110.3 21.0 %all_to_all.32 = f32[4,40,128]{2,1,0:T(8,128)S(1)} all-to-all(f32[4,40,128]{2,1,0:T(8,128)S(1)} %broadcast_in_dim.10), channel_id=1, replica_groups=mesh['gx'=4,'zpair'=2,'znear'=4,'core'=2,'x'=4,'zhi'=2] {'zpair','zhi'}, dimensions={0} | all-to-all | bytes 163840 | tf_op jit(solution)/shard_map/all_to_all | solution.py:250
  131.3 10.7 %all_to_all.33 = f32[16,40,128]{2,1,0:T(8,128)S(1)} all-to-all(f32[16,40,128]{2,1,0:T(8,128)S(1)} %broadcast_in_dim.11), channel_id=1, replica_groups=mesh['gx'=4,'zpair'=2,'znear'=4,'core'=2,'x'=4,'zhi'=2] {'gx','x'}, dimensions={0} | all-to-all | bytes 655360 | tf_op jit(solution)/shard_map/all_to_all | solution.py:250
  142.0 0.0 copy-start.12
  142.0 7.3 %collective-permute-start.7 = (f32[640,128]{1,0:T(8,128)S(1)}, f32[640,128]{1,0:T(8,128)S(1)}, u32[]{:S(2)}, u32[]{:S(2)}) collective-permute-start(f32[640,128]{1,0:T(8,128)S(1)} %bitcast.7), channel_id=1, source_target_pairs={{0,8},{8,0},{1,9},{9,1},{2,10},{10,2},{3,11},{11,3},{4,12},{12,4},... | collective-permute-start | bytes 983048 | tf_op jit(solution)/shard_map/ppermute | solution.py:288
  149.3 2.6 %join.1 = f32[4,8,96,128]{3,2,1,0:T(8,128)} custom-call(s32[3]{0:T(128)S(1)} %copy-done.11, f32[4,4,96,128]{3,2,1,0:T(8,128)} %layers.2.inner, f32[4,4,96,128]{3,2,1,0:T(8,128)} %layers.3.outer), custom_call_target="tpu_custom_call" | custom-call | tf_op jit(solution)/shard_map/join/pallas_call | solution.py:189
  152.0 0.0 copy-done.12
  152.0 0.0 collective-permute-done.7.other
  152.0 0.0 copy-start.13
  152.0 0.7 copy-done.13
  152.7 1.9 %gram_rows.1 = f32[128,512]{1,0:T(8,128)} custom-call(s32[3]{0:T(128)} %copy-done.9, f32[640,128]{1,0:T(8,128)} %bitcast.8, f32[640,128]{1,0:T(8,128)} %copy-done.13), custom_call_target="tpu_custom_call" | custom-call | tf_op jit(solution)/shard_map/gram_rows/pallas_call | solution.py:240
  (7 shorter events, 0.1 us)
Async XLA Ops:
  0.7 1.4 copy-start
  2.1 40.0 %copy-start.9 = (s32[3]{0:T(128)}, s32[3]{0:T(128)S(1)}, u32[]{:S(2)}) copy-start(s32[3]{0:T(128)S(1)} %pad_add_fusion.place) | copy-start | bytes 40
  4.5 39.2 %collective-permute-start = (f32[4,4,96,128]{3,2,1,0:T(8,128)}, f32[4,4,96,128]{3,2,1,0:T(8,128)S(1)}, u32[]{:S(2)}, u32[]{:S(2)}) collective-permute-start(f32[4,4,96,128]{3,2,1,0:T(8,128)} %get-tuple-element.11), channel_id=1, source_target_pairs={{0,8},{8,0},{1,9},{9,1},{2,10},{10,2},{3,11},{11,3},{4,12},{12,4},... | collective-permute-start | bytes 2359304 | tf_op jit(solution)/shard_map/ppermute | solution.py:271
  13.3 22.0 %collective-permute-start.1 = (f32[4,4,8,128]{3,2,1,0:T(8,128)S(1)}, f32[4,4,8,128]{3,2,1,0:T(8,128)S(1)}, u32[]{:S(2)}, u32[]{:S(2)}) collective-permute-start(f32[4,4,8,128]{3,2,1,0:T(8,128)S(1)} %get-tuple-element.12), channel_id=1, source_target_pairs={{0,1},{1,0},{2,3},{3,2},{4,5},{5,4},{6,7},{7,6},{8,9},{9,8},{10,11... | collective-permute-start | bytes 196616 | tf_op jit(solution)/shard_map/ppermute | solution.py:269
  23.4 18.8 %collective-permute-start.2 = (f32[4,4,8,128]{3,2,1,0:T(8,128)S(1)}, f32[4,4,8,128]{3,2,1,0:T(8,128)}, u32[]{:S(2)}, u32[]{:S(2)}) collective-permute-start(f32[4,4,8,128]{3,2,1,0:T(8,128)S(1)} %get-tuple-element.13), channel_id=1, source_target_pairs={{0,7},{1,2},{2,1},{3,4},{4,3},{5,6},{6,5},{7,0},{8,15},{9,10},{10,... | collective-permute-start | bytes 196616 | tf_op jit(solution)/shard_map/ppermute | solution.py:270
  27.5 28.7 %collective-permute-start.5 = (f32[4,4,96,128]{3,2,1,0:T(8,128)}, f32[4,4,96,128]{3,2,1,0:T(8,128)}, u32[]{:S(2)}, u32[]{:S(2)}) collective-permute-start(f32[4,4,96,128]{3,2,1,0:T(8,128)} %get-tuple-element.15), channel_id=1, source_target_pairs={{0,120},{8,16},{16,8},{24,32},{32,24},{40,48},{48,40},{56,64},{64,... | collective-permute-start | bytes 2359304 | tf_op jit(solution)/shard_map/ppermute | solution.py:272
  30.3 13.4 %copy-start.1 = (f32[4,8,96,128]{3,2,1,0:T(8,128)S(1)}, f32[4,8,96,128]{3,2,1,0:T(8,128)}, u32[]{:S(2)}) copy-start(f32[4,8,96,128]{3,2,1,0:T(8,128)} %y.5) | copy-start | bytes 4718596
  30.4 13.4 %copy-start.2 = (f32[3,8,96,128]{3,2,1,0:T(8,128)S(1)}, f32[3,8,96,128]{3,2,1,0:T(8,128)}, u32[]{:S(2)}) copy-start(f32[3,8,96,128]{3,2,1,0:T(8,128)} %vel.3) | copy-start | bytes 3538948
  30.4 13.4 %collective-permute-start.4 = (f32[4,8,8,128]{3,2,1,0:T(8,128)}, f32[4,8,8,128]{3,2,1,0:T(8,128)}, u32[]{:S(2)}, u32[]{:S(2)}) collective-permute-start(f32[4,8,8,128]{3,2,1,0:T(8,128)} %get-tuple-element.14), channel_id=1, source_target_pairs={{128,0},{256,128},{384,256},{0,384},{129,1},{257,129},{385,257},{1... | collective-permute-start | bytes 393224 | tf_op jit(solution)/shard_map/ppermute | solution.py:274
  35.3 0.6 copy-start.14
  35.9 7.8 %collective-permute-start.3 = (f32[4,8,8,128]{3,2,1,0:T(8,128)}, f32[4,8,8,128]{3,2,1,0:T(8,128)}, u32[]{:S(2)}, u32[]{:S(2)}) collective-permute-start(f32[4,8,8,128]{3,2,1,0:T(8,128)} %get-tuple-element.14), channel_id=1, source_target_pairs={{0,128},{128,256},{256,384},{384,0},{1,129},{129,257},{257,385},{3... | collective-permute-start | bytes 393224 | tf_op jit(solution)/shard_map/ppermute | solution.py:273
  43.8 0.9 copy-start.3
  44.7 0.9 copy-start.5
  45.6 0.9 copy-start.7
  46.5 0.7 copy-start.10
  51.9 4.3 %copy-start.11 = (s32[3]{0:T(128)S(1)}, s32[3]{0:T(128)}, u32[]{:S(2)}) copy-start(s32[3]{0:T(128)} %copy-done.9) | copy-start | bytes 40
  51.9 12.7 %all-to-all-start.1 = ((f32[4,384,128]{2,1,0:T(8,128)}), f32[4,384,128]{2,1,0:T(8,128)S(1)}, u32[]{:S(2)}, u32[]{:S(2)}) async-start(f32[4,384,128]{2,1,0:T(8,128)} %bitcast.4), calls=%async_computation.1 | async-start | bytes 1572864 | tf_op jit(solution)/shard_map/all_to_all | solution.py:250
  56.2 0.9 copy-start.4
  57.2 0.9 copy-start.6
  58.1 0.9 copy-start.8
  64.6 12.0 %all-to-all-start = ((f32[4,384,128]{2,1,0:T(8,128)}), f32[4,384,128]{2,1,0:T(8,128)S(1)}, u32[]{:S(2)}, u32[]{:S(2)}) async-start(f32[4,384,128]{2,1,0:T(8,128)} %bitcast.3), calls=%async_computation | async-start | bytes 1572864 | tf_op jit(solution)/shard_map/all_to_all | solution.py:250
  78.2 12.4 %collective-permute-start.6 = (f32[640,128]{1,0:T(8,128)S(1)}, f32[640,128]{1,0:T(8,128)S(1)}, u32[]{:S(2)}, u32[]{:S(2)}) collective-permute-start(f32[640,128]{1,0:T(8,128)S(1)} %get-tuple-element.19), channel_id=1, source_target_pairs={{0,8},{8,0},{1,9},{9,1},{2,10},{10,2},{3,11},{11,3},{4,12},{12,4},... | collective-permute-start | bytes 983048 | tf_op jit(solution)/shard_map/ppermute | solution.py:282
  142.0 9.9 %copy-start.12 = (f32[16,40,128]{2,1,0:T(8,128)}, f32[16,40,128]{2,1,0:T(8,128)S(1)}, u32[]{:S(2)}) copy-start(f32[16,40,128]{2,1,0:T(8,128)S(1)} %all_to_all.33) | copy-start | bytes 983044
  142.0 9.9 %collective-permute-start.7 = (f32[640,128]{1,0:T(8,128)S(1)}, f32[640,128]{1,0:T(8,128)S(1)}, u32[]{:S(2)}, u32[]{:S(2)}) collective-permute-start(f32[640,128]{1,0:T(8,128)S(1)} %bitcast.7), channel_id=1, source_target_pairs={{0,8},{8,0},{1,9},{9,1},{2,10},{10,2},{3,11},{11,3},{4,12},{12,4},... | collective-permute-start | bytes 983048 | tf_op jit(solution)/shard_map/ppermute | solution.py:288
  152.0 0.7 copy-start.13

commit v5 on v4

v5 whole, which is shorter than its diff:
```python
import functools

import jax
import jax.numpy as jnp
from jax import lax
from jax.experimental import pallas as pl
from jax.experimental.pallas import tpu as pltpu
from jax.sharding import Mesh, PartitionSpec as P

C1 = (4.0 / 5.0, -1.0 / 5.0, 4.0 / 105.0, -1.0 / 280.0)
C2 = (-205.0 / 72.0, 8.0 / 5.0, -1.0 / 5.0, 8.0 / 315.0, -1.0 / 560.0)
DIFF = (0.10, 0.12, 0.08, 0.15)
NU = (-1.0, -1.0, 2.0, 0.0)
PAIRS = [(a, b) for a in range(4) for b in range(a, 4)]
MIB = 1 << 20


def split(value):
    high = value.astype(jnp.bfloat16)
    return high, (value - high.astype(jnp.float32)).astype(jnp.bfloat16)


def x_matrices(width):
    row = lax.broadcasted_iota(jnp.int32, (2 * width, width), 0)
    cell = jnp.where(row < width, row, jnp.where(row < width + 4, row - width - 4, row - 4))
    cell = jnp.where(row < width + 8, cell, 4 * width)
    step = cell - lax.broadcasted_iota(jnp.int32, (2 * width, width), 1)
    first = jnp.zeros((2 * width, width), jnp.float32)
    second = jnp.where(step == 0, jnp.float32(C2[0]), first)
    for k in range(1, 5):
        first = jnp.where(step == k, jnp.float32(C1[k - 1]), first)
        first = jnp.where(step == -k, jnp.float32(-C1[k - 1]), first)
        second = jnp.where(jnp.abs(step) == k, jnp.float32(C2[k]), second)
    return jnp.concatenate([first, second], axis=1)


def dot(left, right):
    return lax.dot_general(
        left, right, (((1,), (0,)), ((), ())), preferred_element_type=jnp.float32
    )


def lanes():
    return lax.broadcasted_iota(jnp.int32, (8, 128), 1)


def pack_body(y, inner, outer, za, zb, xs):
    count, rows, depth, width = y.shape
    core, half = lax.axis_index("core"), lax.axis_index("zhi")
    lane = lanes()

    def species(s, carry):
        inner[s] = y[s, pl.ds(4 * (1 - core), 4)]
        outer[s] = y[s, pl.ds(4 * core, 4)]
        for j in range(rows):
            low, high = y[s, j, 0:4], y[s, j, depth - 4 :]
            at = 4 * (j % 2)
            za[s, j // 2, at : at + 4] = jnp.where(half == 0, high, low)
            zb[s, j // 2, at : at + 4] = jnp.where(half == 0, low, high)
            packed = jnp.zeros((8, width), jnp.float32)
            for g in range(depth // 8):
                turned = pltpu.roll(y[s, j, 8 * g : 8 * g + 8], 8 * g + 4, 1)
                packed = jnp.where(lane // 8 == g, turned, packed)
            xs[s, j] = packed
        return carry

    lax.fori_loop(0, count, species, 0)


VMEM = pl.BlockSpec(memory_space=pltpu.VMEM)


def pack(y):
    count, rows, depth, width = y.shape
    shapes = [(count, 4, depth, width)] * 2 + [(count, rows // 2, 8, width)] * 2
    shapes = shapes + [(count, rows, 8, width)]
    return pl.pallas_call(
        pack_body,
        out_shape=[jax.ShapeDtypeStruct(shape, jnp.float32) for shape in shapes],
        in_specs=[VMEM],
        out_specs=[VMEM] * 5,
        compiler_params=pltpu.CompilerParams(vmem_limit_bytes=24 * MIB),
        name="pack",
    )(y)


def factors(s, count):
    diff = jnp.float32(0.25 * DIFF[0])
    nu = jnp.float32(NU[0])
    for q in range(1, count):
        diff = jnp.where(s == q, jnp.float32(0.25 * DIFF[q]), diff)
        nu = jnp.where(s == q, jnp.float32(NU[q]), nu)
    return diff, nu


def layers_body(front, y, vel, face, zs, xlow, xhigh, out, side, dx, pad, rate, zbuf, mh, ml, sem):
    count, rows, depth, width = y.shape
    load = pltpu.make_async_copy(zs, zbuf, sem)
    load.start()
    start = jnp.where(lax.axis_index("core") == front, 0, 4)
    below = lanes() % 8 < 4
    spot = pl.ds(8, depth)
    mh[...], ml[...] = split(x_matrices(width))
    for i in range(4):
        heat = 1.0 + 3.0 * y[2, start + i]
        rate[i] = y[0, start + i] * y[1, start + i] * jnp.exp(-3.0 / heat)
    load.wait()

    def species(s, carry):
        diff, nu = factors(s, count)
        pad[pl.ds(4 - start, rows), spot] = y[s]
        pad[pl.ds(2 * start, 4), spot] = face[s]
        for i in range(4):
            at = 4 * (i % 2)
            tile = start // 2 + i // 2
            pad[4 + i, 4:8] = zbuf[0, s, tile, at : at + 4]
            pad[4 + i, 8 + depth : 12 + depth] = zbuf[1, s, tile, at : at + 4]
            packed = jnp.where(below, xlow[s, start + i], xhigh[s, start + i])
            for g in range(depth // 8):
                row = i * depth + 8 * g
                side[row : row + 8] = pltpu.roll(packed, (128 - 8 * g) % 128, 1)
        own = y[s, pl.ds(start, 4)].reshape(4 * depth, width)
        high, low = split(jnp.concatenate([own, side[...]], axis=1))
        dx[...] = dot(high, mh[...]) + (dot(low, mh[...]) + dot(high, ml[...]))
        for i in range(4):
            centre = y[s, start + i]
            d1y = d1z = None
            second = (2.0 * C2[0]) * centre + dx[i * depth : (i + 1) * depth, width:]
            for k in range(1, 5):
                ya, yb = pad[4 + i + k, 8 : 8 + depth], pad[4 + i - k, 8 : 8 + depth]
                na, nb = pad[4 + i, 8 + k : 8 + k + depth], pad[4 + i, 8 - k : 8 - k + depth]
                ty, tz = (0.25 * C1[k - 1]) * (ya - yb), (0.25 * C1[k - 1]) * (na - nb)
                d1y = ty if d1y is None else d1y + ty
                d1z = tz if d1z is None else d1z + tz
                second = second + C2[k] * ((ya + yb) + (na + nb))
            moved = (0.25 * vel[0, start + i]) * dx[i * depth : (i + 1) * depth, :width]
            moved = moved + (vel[1, start + i] * d1y + vel[2, start + i] * d1z)
            out[s, i] = centre + (diff * second - moved + nu * rate[i])
        return carry

    lax.fori_loop(0, count, species, 0)


def layers(front, y, vel, face, zs, *rest):
    count, rows, depth, width = y.shape
    return pl.pallas_call(
        functools.partial(layers_body, front),
        out_shape=jax.ShapeDtypeStruct((count, 4, depth, width), jnp.float32),
        in_specs=[VMEM] * 3 + [pl.BlockSpec(memory_space=pltpu.HBM)] + [VMEM] * len(rest),
        out_specs=VMEM,
        scratch_shapes=[
            pltpu.VMEM((4 * depth, width), jnp.float32),
            pltpu.VMEM((4 * depth, 2 * width), jnp.float32),
            pltpu.VMEM((12, depth + 16, width), jnp.float32),
            pltpu.VMEM((4, depth, width), jnp.float32),
            pltpu.VMEM(zs.shape, jnp.float32),
            pltpu.VMEM((2 * width, 2 * width), jnp.bfloat16),
            pltpu.VMEM((2 * width, 2 * width), jnp.bfloat16),
            pltpu.SemaphoreType.DMA,
        ],
        compiler_params=pltpu.CompilerParams(vmem_limit_bytes=24 * MIB),
        cost_estimate=pl.CostEstimate(
            flops=10**8, bytes_accessed=6 * 10**6, transcendentals=0
        ),
        name="layers",
    )(y, vel, face, zs, *rest)


def z_faces_body(za, zb, out):
    half = lax.axis_index("zhi")
    out[0] = jnp.where(half == 0, zb[...], za[...])
    out[1] = jnp.where(half == 0, za[...], zb[...])


def z_faces(za, zb):
    return pl.pallas_call(
        z_faces_body,
        out_shape=jax.ShapeDtypeStruct((2,) + za.shape, jnp.float32),
        in_specs=[VMEM, VMEM],
        out_specs=VMEM,
        cost_estimate=pl.CostEstimate(
            flops=18 * 10**8, bytes_accessed=10**7, transcendentals=0
        ),
        name="z_faces",
    )(za, zb)


def products(lines):
    whole = jnp.concatenate([lines[a] for a in range(lines.shape[0])], axis=1)
    high, low = split(whole)
    turned_high, turned_low = split(whole.T)
    total = dot(turned_high, high) + (dot(turned_high, low) + dot(turned_low, high))
    return [total[a * 128 : (a + 1) * 128, b * 128 : (b + 1) * 128] for a, b in PAIRS]


def first_body(lines, inner, outer, sums, updated):
    core = lax.axis_index("core")
    for q, tile in enumerate(products(lines)):
        sums[q * 128 : (q + 1) * 128] = tile
    updated[:, pl.ds(4 - 4 * core, 4)] = inner[...]
    updated[:, pl.ds(4 * core, 4)] = outer[...]


def first_half(lines, inner, outer):
    count, rows, depth, width = inner.shape
    return pl.pallas_call(
        first_body,
        out_shape=[
            jax.ShapeDtypeStruct((len(PAIRS) * 128, 128), jnp.float32),
            jax.ShapeDtypeStruct((count, 2 * rows, depth, width), jnp.float32),
        ],
        in_specs=[VMEM] * 3,
        out_specs=[VMEM] * 2,
        compiler_params=pltpu.CompilerParams(vmem_limit_bytes=32 * MIB),
        name="first_half",
    )(lines, inner, outer)


def second_body(lines, sums, mine, other):
    core = lax.axis_index("core")
    tiles = products(lines)
    for q in range(5):
        at = slice(q * 128, (q + 1) * 128)
        low = tiles[q] + sums[at]
        high = tiles[q + 5] + sums[(q + 5) * 128 : (q + 6) * 128]
        mine[at] = jnp.where(core == 0, low, high)
        other[at] = jnp.where(core == 0, high, low)


def second_half(lines, sums):
    return pl.pallas_call(
        second_body,
        out_shape=[jax.ShapeDtypeStruct((len(PAIRS) * 64, 128), jnp.float32)] * 2,
        in_specs=[VMEM] * 2,
        out_specs=[VMEM] * 2,
        compiler_params=pltpu.CompilerParams(vmem_limit_bytes=32 * MIB),
        name="second_half",
    )(lines, sums)


def rows_body(scale, mine, other, out):
    row, core = lax.axis_index("gx"), lax.axis_index("core")
    for b in range(4):
        low, top = jnp.minimum(row, b), jnp.maximum(row, b)
        index = low * 4 - (low * (low - 1)) // 2 + (top - low)
        owner = jnp.where(index >= 5, 1, 0)
        at = pl.ds(pl.multiple_of((index - 5 * owner) * 128, 128), 128)
        tile = jnp.where(owner == core, mine[at], other[at]) * scale
        out[:, b * 128 : (b + 1) * 128] = jnp.where(row <= b, tile, tile.T)


def gram_rows(mine, other, scale):
    return pl.pallas_call(
        functools.partial(rows_body, scale),
        out_shape=jax.ShapeDtypeStruct((128, 512), jnp.float32),
        in_specs=[VMEM, VMEM],
        out_specs=VMEM,
        name="gram_rows",
    )(mine, other)


def exchange(pieces, axes):
    return lax.all_to_all(pieces, axes, split_axis=0, concat_axis=0, tiled=True)


def gather_sum(part, axes, count):
    return jnp.sum(exchange(jnp.broadcast_to(part, (count,) + part.shape), axes), axis=0)


def shards(y, vel):
    species, rows, depth, width = y.shape
    gy, gz, gx = ("zpair", "znear", "core"), ("x", "zhi"), ("gx",)
    inner, outer, za, zb, xs = pack(y)

    def cross(count):
        return [(i, (i + 1) % count if i % 2 else (i - 1) % count) for i in range(count)]

    up = [(i, (i + 1) % 4) for i in range(4)]
    swap = [(0, 1), (1, 0)]
    za = lax.ppermute(za, "zhi", swap)
    zb = lax.ppermute(zb, gz, cross(8))
    inner = lax.ppermute(inner, "core", swap)
    outer = lax.ppermute(outer, gy, cross(16))
    xlow = lax.ppermute(xs, gx, up)
    xhigh = lax.ppermute(xs, gx, [(target, source) for source, target in up])
    rest = (z_faces(za, zb), xlow, xhigh)
    pieces = (4, species * depth, width)
    near = layers(1, y, vel, inner, *rest)
    far = layers(0, y, vel, outer, *rest)
    sums, updated = first_half(exchange(near.reshape(pieces), gx), near, far)
    mine, other = second_half(exchange(far.reshape(pieces), gx), sums)
    mine = mine + lax.ppermute(other, "core", swap)
    plane = ("gx", "x")
    part = jnp.sum(exchange(mine.reshape(16, -1, 128), plane), axis=0)
    part = gather_sum(part, ("znear",), 4)
    part = gather_sum(part, ("zpair", "zhi"), 4)
    mine = exchange(jnp.broadcast_to(part, (16,) + part.shape), plane).reshape(-1, 128)
    other = lax.ppermute(mine, "core", swap)
    cells = species * rows * 16 * depth * 8
    return updated, gram_rows(mine, other, 1.0 / cells)


def solution(mesh):
    axes = ("gx", "zpair", "znear", "core", "x", "zhi")
    fine = Mesh(mesh.devices.reshape(4, 2, 4, 2, 4, 2), axes)
    grid = P(None, ("zpair", "znear", "core"), ("x", "zhi"), "gx")
    return jax.shard_map(
        shards, mesh=fine, in_specs=(grid, grid), out_specs=(grid, P("gx", None)), check_vma=False
    )
```

time: 156 us -> 148 us (0.949)
  local copies, waits for them, and re-layouts: 8.9 us -> 4.61 us
  starting transfers between devices: 59.1 us -> 57.1 us
    unnamed x30 -> x16, local copies, waits for them, and re-layouts: 8.86 us -> 4.57 us
    ppermute x1, starting transfers between devices: 11.2 us -> 9.47 us  [shards(): mine = mine + lax.ppermute(other, 'core', swap)]
    pallas_call x3 -> x2, Pallas kernels: 5.77 us -> 4.61 us  [the longest x1 3.57 us: first_half(): pl.pallas_call(first_body, out_shape=[jax.ShapeDtypeStruct((len(PAIRS) *...]
  transfers between devices with their start and end apart: 10 -> 10, of which waited for: 4 -> 5; matrix products, arithmetic and copies ran while one was open for 0% -> 0% of each run, Pallas kernels for 10% -> 10%
where the time goes in v5:
time: 148 us; the launch traced here: 147 us
  starting transfers between devices  57.1 us (39%)
  blocking collectives  50.8 us (34%)
  Pallas kernels  20 us (14%)
  waiting for transfers between devices  13.8 us (9%)
  local copies, waits for them, and re-layouts  4.61 us (3%)
    all_to_all x4, blocking collectives, exchange(): return lax.all_to_all(pieces, axes, split_axis=0, concat_axis=0, tiled=True)  50.8 us
    pallas_call x2, Pallas kernels, layers(): pl.pallas_call(functools.partial(layers_body, front), out_shape=jax.Shape...  10.1 us
    ppermute x1, starting transfers between devices, shards(): za = lax.ppermute(za, 'zhi', swap)  10.1 us
    ppermute x1, starting transfers between devices, shards(): mine = mine + lax.ppermute(other, 'core', swap)  9.47 us
    ppermute x1, starting transfers between devices, shards(): inner = lax.ppermute(inner, 'core', swap)  8.77 us
    all_to_all x2, starting transfers between devices, exchange(): return lax.all_to_all(pieces, axes, split_axis=0, concat_axis=0, tiled=True)  7.7 us
    ppermute x1, starting transfers between devices, shards(): other = lax.ppermute(mine, 'core', swap)  7.3 us
    all_to_all x2, waiting for transfers between devices, exchange(): return lax.all_to_all(pieces, axes, split_axis=0, concat_axis=0, tiled=True)  6.96 us
  transfers between devices with their start and end apart: 10, of which 5 were waited for; matrix products, arithmetic and copies ran while one was open for 0% of the time, Pallas kernels for 10%

profile of v5, /device:TPU:1, one launch (start us, length us, event | category | flops | bytes accessed | tf_op | source)
XLA Modules:
  0.0 147.2 jit_solution(5420971486853931461)
XLA Ops:
  0.6 0.0 copy-start
  0.6 1.4 copy-done
  2.0 1.9 %pack.1 = (f32[4,4,96,128]{3,2,1,0:T(8,128)}, f32[4,4,96,128]{3,2,1,0:T(8,128)}, f32[4,4,8,128]{3,2,1,0:T(8,128)S(1)}, f32[4,4,8,128]{3,2,1,0:T(8,128)S(1)}, f32[4,8,8,128]{3,2,1,0:T(8,128)}) custom-call(f32[4,8,96,128]{3,2,1,0:T(8,128)S(1)} %copy-done), custom_call_target="tpu_custom_call" | custom-call | tf_op jit(solution)/shard_map/pack/pallas_call | solution.py:77
  3.9 8.8 %collective-permute-start = (f32[4,4,96,128]{3,2,1,0:T(8,128)}, f32[4,4,96,128]{3,2,1,0:T(8,128)S(1)}, u32[]{:S(2)}, u32[]{:S(2)}) collective-permute-start(f32[4,4,96,128]{3,2,1,0:T(8,128)} %get-tuple-element.11), channel_id=1, source_target_pairs={{0,8},{8,0},{1,9},{9,1},{2,10},{10,2},{3,11},{11,3},{4,12},{12,4},... | collective-permute-start | bytes 2359304 | tf_op jit(solution)/shard_map/ppermute | solution.py:282
  12.7 10.1 %collective-permute-start.1 = (f32[4,4,8,128]{3,2,1,0:T(8,128)S(1)}, f32[4,4,8,128]{3,2,1,0:T(8,128)S(1)}, u32[]{:S(2)}, u32[]{:S(2)}) collective-permute-start(f32[4,4,8,128]{3,2,1,0:T(8,128)S(1)} %get-tuple-element.12), channel_id=1, source_target_pairs={{0,1},{1,0},{2,3},{3,2},{4,5},{5,4},{6,7},{7,6},{8,9},{9,8},{10,11... | collective-permute-start | bytes 196616 | tf_op jit(solution)/shard_map/ppermute | solution.py:280
  22.8 4.1 %collective-permute-start.2 = (f32[4,4,8,128]{3,2,1,0:T(8,128)S(1)}, f32[4,4,8,128]{3,2,1,0:T(8,128)}, u32[]{:S(2)}, u32[]{:S(2)}) collective-permute-start(f32[4,4,8,128]{3,2,1,0:T(8,128)S(1)} %get-tuple-element.13), channel_id=1, source_target_pairs={{0,7},{1,2},{2,1},{3,4},{4,3},{5,6},{6,5},{7,0},{8,15},{9,10},{10,... | collective-permute-start | bytes 196616 | tf_op jit(solution)/shard_map/ppermute | solution.py:281
  26.9 2.8 %collective-permute-start.5 = (f32[4,4,96,128]{3,2,1,0:T(8,128)}, f32[4,4,96,128]{3,2,1,0:T(8,128)}, u32[]{:S(2)}, u32[]{:S(2)}) collective-permute-start(f32[4,4,96,128]{3,2,1,0:T(8,128)} %get-tuple-element.15), channel_id=1, source_target_pairs={{0,120},{8,16},{16,8},{24,32},{32,24},{40,48},{48,40},{56,64},{64,... | collective-permute-start | bytes 2359304 | tf_op jit(solution)/shard_map/ppermute | solution.py:283
  29.7 0.0 copy-start.1
  29.7 0.0 copy-start.2
  29.8 3.5 %collective-permute-start.3 = (f32[4,8,8,128]{3,2,1,0:T(8,128)}, f32[4,8,8,128]{3,2,1,0:T(8,128)}, u32[]{:S(2)}, u32[]{:S(2)}) collective-permute-start(f32[4,8,8,128]{3,2,1,0:T(8,128)} %get-tuple-element.14), channel_id=1, source_target_pairs={{0,128},{128,256},{256,384},{384,0},{1,129},{129,257},{257,385},{3... | collective-permute-start | bytes 393224 | tf_op jit(solution)/shard_map/ppermute | solution.py:284
  33.2 0.0 collective-permute-done.1.za
  33.2 0.0 copy-start.7
  33.3 0.6 copy-done.7
  33.9 3.3 %collective-permute-start.4 = (f32[4,8,8,128]{3,2,1,0:T(8,128)}, f32[4,8,8,128]{3,2,1,0:T(8,128)}, u32[]{:S(2)}, u32[]{:S(2)}) collective-permute-start(f32[4,8,8,128]{3,2,1,0:T(8,128)} %get-tuple-element.14), channel_id=1, source_target_pairs={{128,0},{256,128},{384,256},{0,384},{129,1},{257,129},{385,257},{1... | collective-permute-start | bytes 393224 | tf_op jit(solution)/shard_map/ppermute | solution.py:285
  37.2 4.3 %collective-permute-done.2.zb = f32[4,4,8,128]{3,2,1,0:T(8,128)} collective-permute-done((f32[4,4,8,128]{3,2,1,0:T(8,128)S(1)}, f32[4,4,8,128]{3,2,1,0:T(8,128)}, u32[]{:S(2)}, u32[]{:S(2)}) %collective-permute-start.2) | collective-permute-done | bytes 65568 | tf_op jit(solution)/shard_map/ppermute | solution.py:281
  41.6 1.5 %z_faces.1.zs = f32[2,4,4,8,128]{4,3,2,1,0:T(8,128)} custom-call(f32[4,4,8,128]{3,2,1,0:T(8,128)} %copy-done.7, f32[4,4,8,128]{3,2,1,0:T(8,128)} %collective-permute-done.2.zb), custom_call_target="tpu_custom_call" | custom-call | flops 1800000000 | bytes 10000000 | tf_op jit(solution)/shard_map/z_faces/pallas_call | solution.py:176
  43.1 0.0 collective-permute-done.3.xlow
  43.1 0.0 collective-permute-done.4.xhigh
  43.1 0.0 collective-permute-done.face
  43.1 0.0 copy-done.1
  43.1 0.0 copy-done.2
  43.1 0.0 copy-start.3
  43.1 0.9 copy-done.3
  44.0 4.9 %layers.2.inner = f32[4,4,96,128]{3,2,1,0:T(8,128)} custom-call(f32[4,8,96,128]{3,2,1,0:T(8,128)S(1)} %copy-done.1, f32[3,8,96,128]{3,2,1,0:T(8,128)S(1)} %copy-done.2, f32[4,4,96,128]{3,2,1,0:T(8,128)S(1)} %collective-permute-done.face, f32[2,4,4,8,128]{4,3,2,1,0:T(8,128)S(1)} %copy-done.3, f32[4,8,8,128]{3,2,1,0:T(8,128)} %collective-permute-done.3.xlow, ...), custom_call_target="tpu_custom_call" | custom-call | flops 100000000 | bytes 6000000 | tf_op jit(solution)/shard_map/layers/pallas_call | solution.py:146
  48.9 4.2 %all-to-all-start = ((f32[4,384,128]{2,1,0:T(8,128)}), f32[4,384,128]{2,1,0:T(8,128)S(1)}, u32[]{:S(2)}, u32[]{:S(2)}) async-start(f32[4,384,128]{2,1,0:T(8,128)} %bitcast), calls=%async_computation | async-start | bytes 1572864 | tf_op jit(solution)/shard_map/all_to_all | solution.py:263
  53.1 0.0 collective-permute-done.5.face
  53.1 0.0 copy-start.4
  53.1 0.9 copy-done.4
  54.0 5.2 %layers.3.outer = f32[4,4,96,128]{3,2,1,0:T(8,128)} custom-call(f32[4,8,96,128]{3,2,1,0:T(8,128)S(1)} %copy-done.1, f32[3,8,96,128]{3,2,1,0:T(8,128)S(1)} %copy-done.2, f32[4,4,96,128]{3,2,1,0:T(8,128)} %collective-permute-done.5.face, f32[2,4,4,8,128]{4,3,2,1,0:T(8,128)S(1)} %copy-done.4, f32[4,8,8,128]{3,2,1,0:T(8,128)} %collective-permute-done.3.xlow, ...), custom_call_target="tpu_custom_call" | custom-call | flops 100000000 | bytes 6000000 | tf_op jit(solution)/shard_map/layers/pallas_call | solution.py:146
  59.2 2.2 %all-to-all-done.lines = f32[4,384,128]{2,1,0:T(8,128)S(1)} async-done(((f32[4,384,128]{2,1,0:T(8,128)}), f32[4,384,128]{2,1,0:T(8,128)S(1)}, u32[]{:S(2)}, u32[]{:S(2)}) %all-to-all-start) | async-done | bytes 786464 | tf_op jit(solution)/shard_map/all_to_all | solution.py:263
  61.5 3.5 %all-to-all-start.1 = ((f32[4,384,128]{2,1,0:T(8,128)}), f32[4,384,128]{2,1,0:T(8,128)S(1)}, u32[]{:S(2)}, u32[]{:S(2)}) async-start(f32[4,384,128]{2,1,0:T(8,128)} %bitcast.1), calls=%async_computation.1 | async-start | bytes 1572864 | tf_op jit(solution)/shard_map/all_to_all | solution.py:263
  65.0 3.6 %first_half.1 = (f32[1280,128]{1,0:T(8,128)S(1)}, f32[4,8,96,128]{3,2,1,0:T(8,128)}) custom-call(f32[4,384,128]{2,1,0:T(8,128)S(1)} %all-to-all-done.lines, f32[4,4,96,128]{3,2,1,0:T(8,128)} %layers.2.inner, f32[4,4,96,128]{3,2,1,0:T(8,128)} %layers.3.outer), custom_call_target="tpu_custom_call" | custom-call | tf_op jit(solution)/shard_map/first_half/pallas_call | solution.py:206
  68.5 4.7 %all-to-all-done.1.lines = f32[4,384,128]{2,1,0:T(8,128)S(1)} async-done(((f32[4,384,128]{2,1,0:T(8,128)}), f32[4,384,128]{2,1,0:T(8,128)S(1)}, u32[]{:S(2)}, u32[]{:S(2)}) %all-to-all-start.1) | async-done | bytes 786464 | tf_op jit(solution)/shard_map/all_to_all | solution.py:263
  73.3 1.0 second_half.1
  74.3 9.5 %collective-permute-start.6 = (f32[640,128]{1,0:T(8,128)S(1)}, f32[640,128]{1,0:T(8,128)S(1)}, u32[]{:S(2)}, u32[]{:S(2)}) collective-permute-start(f32[640,128]{1,0:T(8,128)S(1)} %get-tuple-element.19), channel_id=1, source_target_pairs={{0,8},{8,0},{1,9},{9,1},{2,10},{10,2},{3,11},{11,3},{4,12},{12,4},... | collective-permute-start | bytes 983048 | tf_op jit(solution)/shard_map/ppermute | solution.py:292
  83.8 1.2 collective-permute-done.6
  85.1 11.6 %all_to_all.30 = f32[16,40,128]{2,1,0:T(8,128)S(1)} all-to-all(f32[16,40,128]{2,1,0:T(8,128)S(1)} %bitcast.6), channel_id=1, replica_groups=mesh['gx'=4,'zpair'=2,'znear'=4,'core'=2,'x'=4,'zhi'=2] {'gx','x'}, dimensions={0} | all-to-all | bytes 655360 | tf_op jit(solution)/shard_map/all_to_all | solution.py:263
  96.7 9.0 %all_to_all.31 = f32[4,40,128]{2,1,0:T(8,128)S(1)} all-to-all(f32[4,40,128]{2,1,0:T(8,128)S(1)} %broadcast_in_dim.9), channel_id=1, replica_groups=mesh['gx'=4,'zpair'=2,'znear'=4,'core'=2,'x'=4,'zhi'=2] {'znear'}, dimensions={0} | all-to-all | bytes 163840 | tf_op jit(solution)/shard_map/all_to_all | solution.py:263
  105.7 19.6 %all_to_all.32 = f32[4,40,128]{2,1,0:T(8,128)S(1)} all-to-all(f32[4,40,128]{2,1,0:T(8,128)S(1)} %broadcast_in_dim.10), channel_id=1, replica_groups=mesh['gx'=4,'zpair'=2,'znear'=4,'core'=2,'x'=4,'zhi'=2] {'zpair','zhi'}, dimensions={0} | all-to-all | bytes 163840 | tf_op jit(solution)/shard_map/all_to_all | solution.py:263
  125.3 10.7 %all_to_all.33 = f32[16,40,128]{2,1,0:T(8,128)S(1)} all-to-all(f32[16,40,128]{2,1,0:T(8,128)S(1)} %broadcast_in_dim.11), channel_id=1, replica_groups=mesh['gx'=4,'zpair'=2,'znear'=4,'core'=2,'x'=4,'zhi'=2] {'gx','x'}, dimensions={0} | all-to-all | bytes 655360 | tf_op jit(solution)/shard_map/all_to_all | solution.py:263
  136.0 0.0 copy-start.5
  136.0 7.3 %collective-permute-start.7 = (f32[640,128]{1,0:T(8,128)S(1)}, f32[640,128]{1,0:T(8,128)S(1)}, u32[]{:S(2)}, u32[]{:S(2)}) collective-permute-start(f32[640,128]{1,0:T(8,128)S(1)} %bitcast.4), channel_id=1, source_target_pairs={{0,8},{8,0},{1,9},{9,1},{2,10},{10,2},{3,11},{11,3},{4,12},{12,4},... | collective-permute-start | bytes 983048 | tf_op jit(solution)/shard_map/ppermute | solution.py:298
  143.3 1.2 collective-permute-done.7.other
  144.6 0.0 copy-done.5
  144.6 0.0 copy-start.6
  144.6 0.7 copy-done.6
  145.3 1.9 %gram_rows.1 = f32[128,512]{1,0:T(8,128)} custom-call(f32[640,128]{1,0:T(8,128)} %bitcast.5, f32[640,128]{1,0:T(8,128)} %copy-done.6), custom_call_target="tpu_custom_call" | custom-call | tf_op jit(solution)/shard_map/gram_rows/pallas_call | solution.py:253
  (7 shorter events, 0.1 us)
Async XLA Ops:
  0.6 1.4 copy-start
  3.9 39.2 %collective-permute-start = (f32[4,4,96,128]{3,2,1,0:T(8,128)}, f32[4,4,96,128]{3,2,1,0:T(8,128)S(1)}, u32[]{:S(2)}, u32[]{:S(2)}) collective-permute-start(f32[4,4,96,128]{3,2,1,0:T(8,128)} %get-tuple-element.11), channel_id=1, source_target_pairs={{0,8},{8,0},{1,9},{9,1},{2,10},{10,2},{3,11},{11,3},{4,12},{12,4},... | collective-permute-start | bytes 2359304 | tf_op jit(solution)/shard_map/ppermute | solution.py:282
  12.7 20.5 %collective-permute-start.1 = (f32[4,4,8,128]{3,2,1,0:T(8,128)S(1)}, f32[4,4,8,128]{3,2,1,0:T(8,128)S(1)}, u32[]{:S(2)}, u32[]{:S(2)}) collective-permute-start(f32[4,4,8,128]{3,2,1,0:T(8,128)S(1)} %get-tuple-element.12), channel_id=1, source_target_pairs={{0,1},{1,0},{2,3},{3,2},{4,5},{5,4},{6,7},{7,6},{8,9},{9,8},{10,11... | collective-permute-start | bytes 196616 | tf_op jit(solution)/shard_map/ppermute | solution.py:280
  22.8 18.8 %collective-permute-start.2 = (f32[4,4,8,128]{3,2,1,0:T(8,128)S(1)}, f32[4,4,8,128]{3,2,1,0:T(8,128)}, u32[]{:S(2)}, u32[]{:S(2)}) collective-permute-start(f32[4,4,8,128]{3,2,1,0:T(8,128)S(1)} %get-tuple-element.13), channel_id=1, source_target_pairs={{0,7},{1,2},{2,1},{3,4},{4,3},{5,6},{6,5},{7,0},{8,15},{9,10},{10,... | collective-permute-start | bytes 196616 | tf_op jit(solution)/shard_map/ppermute | solution.py:281
  26.9 26.2 %collective-permute-start.5 = (f32[4,4,96,128]{3,2,1,0:T(8,128)}, f32[4,4,96,128]{3,2,1,0:T(8,128)}, u32[]{:S(2)}, u32[]{:S(2)}) collective-permute-start(f32[4,4,96,128]{3,2,1,0:T(8,128)} %get-tuple-element.15), channel_id=1, source_target_pairs={{0,120},{8,16},{16,8},{24,32},{32,24},{40,48},{48,40},{56,64},{64,... | collective-permute-start | bytes 2359304 | tf_op jit(solution)/shard_map/ppermute | solution.py:283
  29.7 13.4 %copy-start.1 = (f32[4,8,96,128]{3,2,1,0:T(8,128)S(1)}, f32[4,8,96,128]{3,2,1,0:T(8,128)}, u32[]{:S(2)}) copy-start(f32[4,8,96,128]{3,2,1,0:T(8,128)} %y.5) | copy-start | bytes 4718596
  29.7 13.4 %copy-start.2 = (f32[3,8,96,128]{3,2,1,0:T(8,128)S(1)}, f32[3,8,96,128]{3,2,1,0:T(8,128)}, u32[]{:S(2)}) copy-start(f32[3,8,96,128]{3,2,1,0:T(8,128)} %vel.3) | copy-start | bytes 3538948
  29.8 13.3 %collective-permute-start.3 = (f32[4,8,8,128]{3,2,1,0:T(8,128)}, f32[4,8,8,128]{3,2,1,0:T(8,128)}, u32[]{:S(2)}, u32[]{:S(2)}) collective-permute-start(f32[4,8,8,128]{3,2,1,0:T(8,128)} %get-tuple-element.14), channel_id=1, source_target_pairs={{0,128},{128,256},{256,384},{384,0},{1,129},{129,257},{257,385},{3... | collective-permute-start | bytes 393224 | tf_op jit(solution)/shard_map/ppermute | solution.py:284
  33.2 0.6 copy-start.7
  33.9 9.2 %collective-permute-start.4 = (f32[4,8,8,128]{3,2,1,0:T(8,128)}, f32[4,8,8,128]{3,2,1,0:T(8,128)}, u32[]{:S(2)}, u32[]{:S(2)}) collective-permute-start(f32[4,8,8,128]{3,2,1,0:T(8,128)} %get-tuple-element.14), channel_id=1, source_target_pairs={{128,0},{256,128},{384,256},{0,384},{129,1},{257,129},{385,257},{1... | collective-permute-start | bytes 393224 | tf_op jit(solution)/shard_map/ppermute | solution.py:285
  43.1 0.9 copy-start.3
  48.9 12.5 %all-to-all-start = ((f32[4,384,128]{2,1,0:T(8,128)}), f32[4,384,128]{2,1,0:T(8,128)S(1)}, u32[]{:S(2)}, u32[]{:S(2)}) async-start(f32[4,384,128]{2,1,0:T(8,128)} %bitcast), calls=%async_computation | async-start | bytes 1572864 | tf_op jit(solution)/shard_map/all_to_all | solution.py:263
  53.1 0.9 copy-start.4
  61.5 11.8 %all-to-all-start.1 = ((f32[4,384,128]{2,1,0:T(8,128)}), f32[4,384,128]{2,1,0:T(8,128)S(1)}, u32[]{:S(2)}, u32[]{:S(2)}) async-start(f32[4,384,128]{2,1,0:T(8,128)} %bitcast.1), calls=%async_computation.1 | async-start | bytes 1572864 | tf_op jit(solution)/shard_map/all_to_all | solution.py:263
  74.3 10.7 %collective-permute-start.6 = (f32[640,128]{1,0:T(8,128)S(1)}, f32[640,128]{1,0:T(8,128)S(1)}, u32[]{:S(2)}, u32[]{:S(2)}) collective-permute-start(f32[640,128]{1,0:T(8,128)S(1)} %get-tuple-element.19), channel_id=1, source_target_pairs={{0,8},{8,0},{1,9},{9,1},{2,10},{10,2},{3,11},{11,3},{4,12},{12,4},... | collective-permute-start | bytes 983048 | tf_op jit(solution)/shard_map/ppermute | solution.py:292
  136.0 8.5 %copy-start.5 = (f32[16,40,128]{2,1,0:T(8,128)}, f32[16,40,128]{2,1,0:T(8,128)S(1)}, u32[]{:S(2)}) copy-start(f32[16,40,128]{2,1,0:T(8,128)S(1)} %all_to_all.33) | copy-start | bytes 983044
  136.0 8.5 %collective-permute-start.7 = (f32[640,128]{1,0:T(8,128)S(1)}, f32[640,128]{1,0:T(8,128)S(1)}, u32[]{:S(2)}, u32[]{:S(2)}) collective-permute-start(f32[640,128]{1,0:T(8,128)S(1)} %bitcast.4), channel_id=1, source_target_pairs={{0,8},{8,0},{1,9},{9,1},{2,10},{10,2},{3,11},{11,3},{4,12},{12,4},... | collective-permute-start | bytes 983048 | tf_op jit(solution)/shard_map/ppermute | solution.py:298
  144.6 0.7 copy-start.6

commit v6 on v3

--- a/solution.py
+++ b/solution.py
@@ -1,7 +1,5 @@
 import functools
 
-import ml_dtypes
-import numpy as np
 import jax
 import jax.numpy as jnp
 from jax import lax
@@ -23,17 +21,17 @@
 
 
 def x_matrices(width):
-    matrix = np.zeros((2 * width, 2 * width))
-    for i in range(width):
-        for k in range(-4, 5):
-            j = i + k
-            row = j if 0 <= j < width else (width + 4 + j if j < 0 else width + 4 + j - width)
-            if k:
-                matrix[row, i] += np.sign(k) * C1[abs(k) - 1]
-            matrix[row, width + i] += C2[abs(k)]
-    matrix = matrix.astype(np.float32)
-    high = matrix.astype(ml_dtypes.bfloat16)
-    return high, (matrix - high.astype(np.float32)).astype(ml_dtypes.bfloat16)
+    row = lax.broadcasted_iota(jnp.int32, (2 * width, width), 0)
+    cell = jnp.where(row < width, row, jnp.where(row < width + 4, row - width - 4, row - 4))
+    cell = jnp.where(row < width + 8, cell, 4 * width)
+    step = cell - lax.broadcasted_iota(jnp.int32, (2 * width, width), 1)
+    first = jnp.zeros((2 * width, width), jnp.float32)
+    second = jnp.where(step == 0, jnp.float32(C2[0]), first)
+    for k in range(1, 5):
+        first = jnp.where(step == k, jnp.float32(C1[k - 1]), first)
+        first = jnp.where(step == -k, jnp.float32(-C1[k - 1]), first)
+        second = jnp.where(jnp.abs(step) == k, jnp.float32(C2[k]), second)
+    return jnp.concatenate([first, second], axis=1)
 
 
 def dot(left, right):
@@ -46,9 +44,9 @@
     return lax.broadcasted_iota(jnp.int32, (8, 128), 1)
 
 
-def pack_body(place, y, inner, outer, za, zb, xs):
+def pack_body(y, inner, outer, za, zb, xs):
     count, rows, depth, width = y.shape
-    core, half = place[1], place[2]
+    core, half = lax.axis_index("core"), lax.axis_index("zhi")
     lane = lanes()
 
     def species(s, carry):
@@ -69,22 +67,21 @@
     lax.fori_loop(0, count, species, 0)
 
 
-SMEM = pl.BlockSpec(memory_space=pltpu.SMEM)
 VMEM = pl.BlockSpec(memory_space=pltpu.VMEM)
 
 
-def pack(place, y):
+def pack(y):
     count, rows, depth, width = y.shape
     shapes = [(count, 4, depth, width)] * 2 + [(count, rows // 2, 8, width)] * 2
     shapes = shapes + [(count, rows, 8, width)]
     return pl.pallas_call(
         pack_body,
         out_shape=[jax.ShapeDtypeStruct(shape, jnp.float32) for shape in shapes],
-        in_specs=[SMEM, VMEM],
+        in_specs=[VMEM],
         out_specs=[VMEM] * 5,
         compiler_params=pltpu.CompilerParams(vmem_limit_bytes=24 * MIB),
         name="pack",
-    )(place, y)
+    )(y)
 
 
 def factors(s, count):
@@ -96,9 +93,9 @@
     return diff, nu
 
 
-def along_z_body(place, y, vel, za, zb, out, rate, pad):
+def along_z_body(y, vel, za, zb, out, rate, pad):
     count, rows, depth, width = y.shape
-    half = place[2]
+    half = lax.axis_index("zhi")
     for j in range(rows):
         heat = 1.0 + 3.0 * y[2, j]
         rate[j] = y[0, j] * y[1, j] * jnp.exp(-3.0 / heat)
@@ -126,12 +123,12 @@
     lax.fori_loop(0, count, species, 0)
 
 
-def along_z(place, y, *rest):
+def along_z(y, *rest):
     _, rows, depth, width = y.shape
     return pl.pallas_call(
         along_z_body,
         out_shape=jax.ShapeDtypeStruct(y.shape, jnp.float32),
-        in_specs=[SMEM] + [VMEM] * (1 + len(rest)),
+        in_specs=[VMEM] * (1 + len(rest)),
         out_specs=VMEM,
         scratch_shapes=[
             pltpu.VMEM((rows, depth, width), jnp.float32),
@@ -139,16 +136,17 @@
         ],
         compiler_params=pltpu.CompilerParams(vmem_limit_bytes=24 * MIB),
         cost_estimate=pl.CostEstimate(
-            flops=10**10, bytes_accessed=2 * 10**8, transcendentals=0
+            flops=10**9, bytes_accessed=10**7, transcendentals=0
         ),
         name="along_z",
-    )(place, y, *rest)
-
-
-def along_xy_body(place, y, vel, base, outer, inner, xlow, xhigh, mh, ml, out, side, dx, pad):
+    )(y, *rest)
+
+
+def along_xy_body(y, vel, base, outer, inner, xlow, xhigh, out, side, dx, pad):
     count, rows, depth, width = y.shape
-    core = place[1]
+    core = lax.axis_index("core")
     below = lanes() % 8 < 4
+    mh, ml = split(x_matrices(width))
 
     def species(s, carry):
         diff, _ = factors(s, count)
@@ -162,7 +160,7 @@
                 side[row : row + 8] = pltpu.roll(packed, (128 - 8 * g) % 128, 1)
         left = jnp.concatenate([y[s].reshape(rows * depth, width), side[...]], axis=1)
         high, low = split(left)
-        dx[...] = dot(high, mh[...]) + (dot(low, mh[...]) + dot(high, ml[...]))
+        dx[...] = dot(high, mh) + (dot(low, mh) + dot(high, ml))
         for j in range(rows):
             first = None
             second = dx[j * depth : (j + 1) * depth, width:]
@@ -178,12 +176,12 @@
     lax.fori_loop(0, count, species, 0)
 
 
-def along_xy(place, y, *rest):
+def along_xy(y, *rest):
     _, rows, depth, width = y.shape
     return pl.pallas_call(
         along_xy_body,
         out_shape=jax.ShapeDtypeStruct(y.shape, jnp.float32),
-        in_specs=[SMEM] + [VMEM] * (1 + len(rest)),
+        in_specs=[VMEM] * (1 + len(rest)),
         out_specs=VMEM,
         scratch_shapes=[
             pltpu.VMEM((rows * depth, width), jnp.float32),
@@ -192,52 +190,76 @@
         ],
         compiler_params=pltpu.CompilerParams(vmem_limit_bytes=32 * MIB),
         name="along_xy",
-    )(place, y, *rest)
-
-
-def gram_body(place, lines, mine, other):
-    parts = lines.shape[0]
-    whole = jnp.concatenate([lines[a] for a in range(parts)], axis=1)
+    )(y, *rest)
+
+
+def products(lines):
+    whole = jnp.concatenate([lines[a] for a in range(lines.shape[0])], axis=1)
     high, low = split(whole)
     turned_high, turned_low = split(whole.T)
     total = dot(turned_high, high) + (dot(turned_high, low) + dot(turned_low, high))
-    tiles = [total[a * 128 : (a + 1) * 128, b * 128 : (b + 1) * 128] for a, b in PAIRS]
+    return [total[a * 128 : (a + 1) * 128, b * 128 : (b + 1) * 128] for a, b in PAIRS]
+
+
+def gram_body(lines, mine, other):
+    core = lax.axis_index("core")
+    tiles = products(lines)
     for q in range(5):
-        first, second = tiles[q], tiles[q + 5]
-        mine[q * 128 : (q + 1) * 128] = jnp.where(place[1] == 0, first, second)
-        other[q * 128 : (q + 1) * 128] = jnp.where(place[1] == 0, second, first)
-
-
-def gram_blocks(place, lines):
+        at = slice(q * 128, (q + 1) * 128)
+        mine[at] = jnp.where(core == 0, tiles[q], tiles[q + 5])
+        other[at] = jnp.where(core == 0, tiles[q + 5], tiles[q])
+
+
+def gram_blocks(lines):
     return pl.pallas_call(
         gram_body,
         out_shape=[jax.ShapeDtypeStruct((len(PAIRS) * 64, 128), jnp.float32)] * 2,
-        in_specs=[SMEM, VMEM],
+        in_specs=[VMEM],
         out_specs=[VMEM] * 2,
         compiler_params=pltpu.CompilerParams(vmem_limit_bytes=40 * MIB),
         name="gram",
-    )(place, lines)
-
-
-def rows_body(scale, place, mine, other, out):
-    row, core = place[0], place[1]
-    for b in range(4):
+    )(lines)
+
+
+def rows_body(scale, mine, other, out, tiles, sems):
+    row, core = lax.axis_index("gx"), lax.axis_index("core")
+
+    def tile(b):
         low, top = jnp.minimum(row, b), jnp.maximum(row, b)
         index = low * 4 - (low * (low - 1)) // 2 + (top - low)
         owner = jnp.where(index >= 5, 1, 0)
         at = pl.ds(pl.multiple_of((index - 5 * owner) * 128, 128), 128)
-        tile = jnp.where(owner == core, mine[at], other[at]) * scale
-        out[:, b * 128 : (b + 1) * 128] = jnp.where(row <= b, tile, tile.T)
-
-
-def gram_rows(place, mine, other, scale):
+        return owner == core, at
+
+    for b in range(4):
+        here, at = tile(b)
+
+        @pl.when(here)
+        def _():
+            pltpu.make_async_copy(mine.at[at], tiles.at[b], sems.at[b]).start()
+
+        @pl.when(jnp.logical_not(here))
+        def _():
+            pltpu.make_async_copy(other.at[at], tiles.at[b], sems.at[b]).start()
+
+    for b in range(4):
+        pltpu.make_async_copy(mine.at[pl.ds(0, 128)], tiles.at[b], sems.at[b]).wait()
+        block = tiles[b] * scale
+        out[:, b * 128 : (b + 1) * 128] = jnp.where(row <= b, block, block.T)
+
+
+def gram_rows(mine, other, scale):
     return pl.pallas_call(
         functools.partial(rows_body, scale),
         out_shape=jax.ShapeDtypeStruct((128, 512), jnp.float32),
-        in_specs=[SMEM, VMEM, VMEM],
+        in_specs=[pl.BlockSpec(memory_space=pl.ANY)] * 2,
         out_specs=VMEM,
+        scratch_shapes=[
+            pltpu.VMEM((4, 128, 128), jnp.float32),
+            pltpu.SemaphoreType.DMA((4,)),
+        ],
         name="gram_rows",
-    )(place, mine, other)
+    )(mine, other)
 
 
 def exchange(pieces, axes):
@@ -251,9 +273,7 @@
 def shards(y, vel):
     species, rows, depth, width = y.shape
     gy, gz, gx = ("zpair", "znear", "core"), ("x", "zhi"), ("gx",)
-    place = jnp.stack([lax.axis_index("gx"), lax.axis_index("core"), lax.axis_index("zhi")])
-    place = place.astype(jnp.int32)
-    inner, outer, za, zb, xs = pack(place, y)
+    inner, outer, za, zb, xs = pack(y)
 
     def cross(count):
         return [(i, (i + 1) % count if i % 2 else (i - 1) % count) for i in range(count)]
@@ -266,11 +286,9 @@
     outer = lax.ppermute(outer, gy, cross(16))
     xlow = lax.ppermute(xs, gx, up)
     xhigh = lax.ppermute(xs, gx, [(target, source) for source, target in up])
-    base = along_z(place, y, vel, za, zb)
-    updated = along_xy(place, y, vel, base, outer, inner, xlow, xhigh, *x_matrices(width))
-
-    lines = exchange(updated.reshape(4, species * rows * depth // 4, width), gx)
-    mine, other = gram_blocks(place, lines)
+    base = along_z(y, vel, za, zb)
+    updated = along_xy(y, vel, base, outer, inner, xlow, xhigh)
+    mine, other = gram_blocks(exchange(updated.reshape(4, species * rows * depth // 4, width), gx))
     mine = mine + lax.ppermute(other, "core", swap)
     plane = ("gx", "x")
     part = jnp.sum(exchange(mine.reshape(16, -1, 128), plane), axis=0)
@@ -279,7 +297,7 @@
     mine = exchange(jnp.broadcast_to(part, (16,) + part.shape), plane).reshape(-1, 128)
     other = lax.ppermute(mine, "core", swap)
     cells = species * rows * 16 * depth * 8
-    return updated, gram_rows(place, mine, other, 1.0 / cells)
+    return updated, gram_rows(mine, other, 1.0 / cells)
 
 
 def solution(mesh):

time: 151 us -> 144 us (0.954)
  starting transfers between devices: 62.6 us -> 55.3 us
  waiting for transfers between devices: 3.49 us -> 8.07 us
  Pallas kernels: 12.7 us -> 10.4 us
    ppermute x1, starting transfers between devices: 16.3 us -> 7.94 us  [shards(): za = lax.ppermute(za, 'zhi', swap)]
    ppermute x1, starting transfers between devices: 16.6 us -> 9.28 us  [shards(): mine = mine + lax.ppermute(other, 'core', swap)]
    ppermute x1, waiting for transfers between devices: 0.01 us -> 5.59 us  [shards(): zb = lax.ppermute(zb, gz, cross(8))]
    ppermute x1, starting transfers between devices: 4.12 us -> 8.25 us  [shards(): zb = lax.ppermute(zb, gz, cross(8))]
    ppermute x1, starting transfers between devices: 8.18 us -> 11.1 us  [shards(): inner = lax.ppermute(inner, 'core', swap)]
  transfers between devices with their start and end apart: 8 -> 8, of which waited for: 3 -> 3; matrix products, arithmetic and copies ran while one was open for 0% -> 0% of each run, Pallas kernels for 2% -> 1%
where the time goes in v6:
time: 144 us; the launch traced here: 143 us
  blocking collectives  66.6 us (46%)
  starting transfers between devices  55.3 us (38%)
  Pallas kernels  10.4 us (7%)
  waiting for transfers between devices  8.07 us (6%)
  local copies, waits for them, and re-layouts  2.19 us (2%)
    all_to_all x5, blocking collectives, exchange(): return lax.all_to_all(pieces, axes, split_axis=0, concat_axis=0, tiled=True)  66.6 us
    ppermute x1, starting transfers between devices, shards(): inner = lax.ppermute(inner, 'core', swap)  11.1 us
    ppermute x1, starting transfers between devices, shards(): mine = mine + lax.ppermute(other, 'core', swap)  9.28 us
    ppermute x1, starting transfers between devices, shards(): zb = lax.ppermute(zb, gz, cross(8))  8.25 us
    ppermute x1, starting transfers between devices, shards(): za = lax.ppermute(za, 'zhi', swap)  7.94 us
    ppermute x1, starting transfers between devices, shards(): other = lax.ppermute(mine, 'core', swap)  7.08 us
    ppermute x1, waiting for transfers between devices, shards(): zb = lax.ppermute(zb, gz, cross(8))  5.59 us
    ppermute x1, starting transfers between devices, shards(): outer = lax.ppermute(outer, gy, cross(16))  4.94 us
  transfers between devices with their start and end apart: 8, of which 3 were waited for; matrix products, arithmetic and copies ran while one was open for 0% of the time, Pallas kernels for 1%

profile of v6, /device:TPU:1, one launch (start us, length us, event | category | flops | bytes accessed | tf_op | source)
XLA Modules:
  0.0 143.4 jit_solution(3131731084992249029)
XLA Ops:
  0.6 0.0 copy-start
  0.6 1.4 copy-done
  2.0 0.0 copy-start.2
  2.0 0.8 pack.1
  2.8 4.9 %collective-permute-start.2 = (f32[4,4,96,128]{3,2,1,0:T(8,128)S(1)}, f32[4,4,96,128]{3,2,1,0:T(8,128)S(1)}, u32[]{:S(2)}, u32[]{:S(2)}) collective-permute-start(f32[4,4,96,128]{3,2,1,0:T(8,128)S(1)} %get-tuple-element.11), channel_id=1, source_target_pairs={{0,120},{8,16},{16,8},{24,32},{32,24},{40,48},{48,40},{56,64},{64,... | collective-permute-start | bytes 2359304 | tf_op jit(solution)/shard_map/ppermute | solution.py:286
  7.8 11.1 %collective-permute-start.3 = (f32[4,4,96,128]{3,2,1,0:T(8,128)S(1)}, f32[4,4,96,128]{3,2,1,0:T(8,128)S(1)}, u32[]{:S(2)}, u32[]{:S(2)}) collective-permute-start(f32[4,4,96,128]{3,2,1,0:T(8,128)S(1)} %get-tuple-element.12), channel_id=1, source_target_pairs={{0,8},{8,0},{1,9},{9,1},{2,10},{10,2},{3,11},{11,3},{4,12},{12,4},... | collective-permute-start | bytes 2359304 | tf_op jit(solution)/shard_map/ppermute | solution.py:285
  18.9 7.9 %collective-permute-start = (f32[4,4,8,128]{3,2,1,0:T(8,128)S(1)}, f32[4,4,8,128]{3,2,1,0:T(8,128)S(1)}, u32[]{:S(2)}, u32[]{:S(2)}) collective-permute-start(f32[4,4,8,128]{3,2,1,0:T(8,128)S(1)} %get-tuple-element.9), channel_id=1, source_target_pairs={{0,1},{1,0},{2,3},{3,2},{4,5},{5,4},{6,7},{7,6},{8,9},{9,8},{10,11... | collective-permute-start | bytes 196616 | tf_op jit(solution)/shard_map/ppermute | solution.py:283
  26.8 8.3 %collective-permute-start.1 = (f32[4,4,8,128]{3,2,1,0:T(8,128)S(1)}, f32[4,4,8,128]{3,2,1,0:T(8,128)S(1)}, u32[]{:S(2)}, u32[]{:S(2)}) collective-permute-start(f32[4,4,8,128]{3,2,1,0:T(8,128)S(1)} %get-tuple-element.10), channel_id=1, source_target_pairs={{0,7},{1,2},{2,1},{3,4},{4,3},{5,6},{6,5},{7,0},{8,15},{9,10},{10,... | collective-permute-start | bytes 196616 | tf_op jit(solution)/shard_map/ppermute | solution.py:284
  35.1 0.0 copy-start.1
  35.1 4.8 %collective-permute-start.5 = (f32[4,8,8,128]{3,2,1,0:T(8,128)S(1)}, f32[4,8,8,128]{3,2,1,0:T(8,128)S(1)}, u32[]{:S(2)}, u32[]{:S(2)}) collective-permute-start(f32[4,8,8,128]{3,2,1,0:T(8,128)S(1)} %get-tuple-element.13), channel_id=1, source_target_pairs={{128,0},{256,128},{384,256},{0,384},{129,1},{257,129},{385,257},{1... | collective-permute-start | bytes 393224 | tf_op jit(solution)/shard_map/ppermute | solution.py:288
  39.9 0.0 collective-permute-done.za
  39.9 1.9 %collective-permute-start.4 = (f32[4,8,8,128]{3,2,1,0:T(8,128)S(1)}, f32[4,8,8,128]{3,2,1,0:T(8,128)S(1)}, u32[]{:S(2)}, u32[]{:S(2)}) collective-permute-start(f32[4,8,8,128]{3,2,1,0:T(8,128)S(1)} %get-tuple-element.13), channel_id=1, source_target_pairs={{0,128},{128,256},{256,384},{384,0},{1,129},{129,257},{257,385},{3... | collective-permute-start | bytes 393224 | tf_op jit(solution)/shard_map/ppermute | solution.py:287
  41.8 5.6 %collective-permute-done.1.zb = f32[4,4,8,128]{3,2,1,0:T(8,128)S(1)} collective-permute-done((f32[4,4,8,128]{3,2,1,0:T(8,128)S(1)}, f32[4,4,8,128]{3,2,1,0:T(8,128)S(1)}, u32[]{:S(2)}, u32[]{:S(2)}) %collective-permute-start.1) | collective-permute-done | bytes 65568 | tf_op jit(solution)/shard_map/ppermute | solution.py:284
  47.4 0.0 copy-done.2
  47.4 1.9 %along_z.1.base = f32[4,8,96,128]{3,2,1,0:T(8,128)S(1)} custom-call(f32[4,8,96,128]{3,2,1,0:T(8,128)S(1)} %copy-done, f32[3,8,96,128]{3,2,1,0:T(8,128)S(1)} %copy-done.2, f32[4,4,8,128]{3,2,1,0:T(8,128)S(1)} %collective-permute-done.za, f32[4,4,8,128]{3,2,1,0:T(8,128)S(1)} %collective-permute-done.1.zb), custom_call_target="tpu_custom_call" | custom-call | flops 1000000000 | bytes 10000000 | tf_op jit(solution)/shard_map/along_z/pallas_call | solution.py:128
  49.3 0.0 collective-permute-done.5.xhigh
  49.3 0.0 collective-permute-done.4.xlow
  49.3 0.0 collective-permute-done.2.outer
  49.3 0.0 collective-permute-done.3.inner
  49.3 0.0 copy-done.1
  49.3 4.4 %along_xy.1 = f32[4,8,96,128]{3,2,1,0:T(8,128)} custom-call(f32[4,8,96,128]{3,2,1,0:T(8,128)S(1)} %copy-done.1, f32[3,8,96,128]{3,2,1,0:T(8,128)S(1)} %copy-done.2, f32[4,8,96,128]{3,2,1,0:T(8,128)S(1)} %along_z.1.base, f32[4,4,96,128]{3,2,1,0:T(8,128)S(1)} %collective-permute-done.2.outer, f32[4,4,96,128]{3,2,1,0:T(8,128)S(1)} %collective-permute-done.3.inner, ...), custom_call_target="tpu_custom_call" | custom-call | tf_op jit(solution)/shard_map/along_xy/pallas_call | solution.py:181
  53.7 18.5 %all_to_all.25.lines = f32[4,768,128]{2,1,0:T(8,128)S(1)} all-to-all(f32[4,768,128]{2,1,0:T(8,128)} %bitcast.3), channel_id=1, replica_groups=mesh['gx'=4,'zpair'=2,'znear'=4,'core'=2,'x'=4,'zhi'=2] {'gx'}, dimensions={0} | all-to-all | bytes 3145728 | tf_op jit(solution)/shard_map/all_to_all | solution.py:266
  72.2 1.5 %gram.1 = (f32[640,128]{1,0:T(8,128)S(1)}, f32[640,128]{1,0:T(8,128)S(1)}) custom-call(f32[4,768,128]{2,1,0:T(8,128)S(1)} %all_to_all.25.lines), custom_call_target="tpu_custom_call" | custom-call | tf_op jit(solution)/shard_map/gram/pallas_call | solution.py:214
  73.7 9.3 %collective-permute-start.6 = (f32[640,128]{1,0:T(8,128)S(1)}, f32[640,128]{1,0:T(8,128)S(1)}, u32[]{:S(2)}, u32[]{:S(2)}) collective-permute-start(f32[640,128]{1,0:T(8,128)S(1)} %get-tuple-element.15), channel_id=1, source_target_pairs={{0,8},{8,0},{1,9},{9,1},{2,10},{10,2},{3,11},{11,3},{4,12},{12,4},... | collective-permute-start | bytes 983048 | tf_op jit(solution)/shard_map/ppermute | solution.py:292
  83.0 1.2 collective-permute-done.6
  84.2 11.6 %all_to_all.26 = f32[16,40,128]{2,1,0:T(8,128)S(1)} all-to-all(f32[16,40,128]{2,1,0:T(8,128)S(1)} %bitcast.6), channel_id=1, replica_groups=mesh['gx'=4,'zpair'=2,'znear'=4,'core'=2,'x'=4,'zhi'=2] {'gx','x'}, dimensions={0} | all-to-all | bytes 655360 | tf_op jit(solution)/shard_map/all_to_all | solution.py:266
  95.9 7.1 %all_to_all.27 = f32[4,40,128]{2,1,0:T(8,128)S(1)} all-to-all(f32[4,40,128]{2,1,0:T(8,128)S(1)} %broadcast_in_dim.9), channel_id=1, replica_groups=mesh['gx'=4,'zpair'=2,'znear'=4,'core'=2,'x'=4,'zhi'=2] {'znear'}, dimensions={0} | all-to-all | bytes 163840 | tf_op jit(solution)/shard_map/all_to_all | solution.py:266
  103.0 18.4 %all_to_all.28 = f32[4,40,128]{2,1,0:T(8,128)S(1)} all-to-all(f32[4,40,128]{2,1,0:T(8,128)S(1)} %broadcast_in_dim.10), channel_id=1, replica_groups=mesh['gx'=4,'zpair'=2,'znear'=4,'core'=2,'x'=4,'zhi'=2] {'zpair','zhi'}, dimensions={0} | all-to-all | bytes 163840 | tf_op jit(solution)/shard_map/all_to_all | solution.py:266
  121.5 10.9 %all_to_all.29 = f32[16,40,128]{2,1,0:T(8,128)S(1)} all-to-all(f32[16,40,128]{2,1,0:T(8,128)S(1)} %broadcast_in_dim.11), channel_id=1, replica_groups=mesh['gx'=4,'zpair'=2,'znear'=4,'core'=2,'x'=4,'zhi'=2] {'gx','x'}, dimensions={0} | all-to-all | bytes 655360 | tf_op jit(solution)/shard_map/all_to_all | solution.py:266
  132.4 0.0 copy-start.3
  132.4 7.1 %collective-permute-start.7 = (f32[640,128]{1,0:T(8,128)S(1)}, f32[640,128]{1,0:T(8,128)S(1)}, u32[]{:S(2)}, u32[]{:S(2)}) collective-permute-start(f32[640,128]{1,0:T(8,128)S(1)} %bitcast.4), channel_id=1, source_target_pairs={{0,8},{8,0},{1,9},{9,1},{2,10},{10,2},{3,11},{11,3},{4,12},{12,4},... | collective-permute-start | bytes 983048 | tf_op jit(solution)/shard_map/ppermute | solution.py:298
  139.5 1.2 collective-permute-done.7.other
  140.7 0.0 copy-done.3
  140.7 0.0 copy-start.4
  140.8 0.7 copy-done.4
  141.5 1.9 %gram_rows.1 = f32[128,512]{1,0:T(8,128)} custom-call(f32[640,128]{1,0:T(8,128)} %bitcast.5, f32[640,128]{1,0:T(8,128)} %copy-done.4), custom_call_target="tpu_custom_call" | custom-call | tf_op jit(solution)/shard_map/gram_rows/pallas_call | solution.py:252
  (7 shorter events, 0.1 us)
Async XLA Ops:
  0.6 1.4 copy-start
  2.0 45.3 %copy-start.2 = (f32[3,8,96,128]{3,2,1,0:T(8,128)S(1)}, f32[3,8,96,128]{3,2,1,0:T(8,128)}, u32[]{:S(2)}) copy-start(f32[3,8,96,128]{3,2,1,0:T(8,128)} %vel.3) | copy-start | bytes 3538948
  2.8 46.4 %collective-permute-start.2 = (f32[4,4,96,128]{3,2,1,0:T(8,128)S(1)}, f32[4,4,96,128]{3,2,1,0:T(8,128)S(1)}, u32[]{:S(2)}, u32[]{:S(2)}) collective-permute-start(f32[4,4,96,128]{3,2,1,0:T(8,128)S(1)} %get-tuple-element.11), channel_id=1, source_target_pairs={{0,120},{8,16},{16,8},{24,32},{32,24},{40,48},{48,40},{56,64},{64,... | collective-permute-start | bytes 2359304 | tf_op jit(solution)/shard_map/ppermute | solution.py:286
  7.8 41.5 %collective-permute-start.3 = (f32[4,4,96,128]{3,2,1,0:T(8,128)S(1)}, f32[4,4,96,128]{3,2,1,0:T(8,128)S(1)}, u32[]{:S(2)}, u32[]{:S(2)}) collective-permute-start(f32[4,4,96,128]{3,2,1,0:T(8,128)S(1)} %get-tuple-element.12), channel_id=1, source_target_pairs={{0,8},{8,0},{1,9},{9,1},{2,10},{10,2},{3,11},{11,3},{4,12},{12,4},... | collective-permute-start | bytes 2359304 | tf_op jit(solution)/shard_map/ppermute | solution.py:285
  18.9 21.0 %collective-permute-start = (f32[4,4,8,128]{3,2,1,0:T(8,128)S(1)}, f32[4,4,8,128]{3,2,1,0:T(8,128)S(1)}, u32[]{:S(2)}, u32[]{:S(2)}) collective-permute-start(f32[4,4,8,128]{3,2,1,0:T(8,128)S(1)} %get-tuple-element.9), channel_id=1, source_target_pairs={{0,1},{1,0},{2,3},{3,2},{4,5},{5,4},{6,7},{7,6},{8,9},{9,8},{10,11... | collective-permute-start | bytes 196616 | tf_op jit(solution)/shard_map/ppermute | solution.py:283
  26.8 20.6 %collective-permute-start.1 = (f32[4,4,8,128]{3,2,1,0:T(8,128)S(1)}, f32[4,4,8,128]{3,2,1,0:T(8,128)S(1)}, u32[]{:S(2)}, u32[]{:S(2)}) collective-permute-start(f32[4,4,8,128]{3,2,1,0:T(8,128)S(1)} %get-tuple-element.10), channel_id=1, source_target_pairs={{0,7},{1,2},{2,1},{3,4},{4,3},{5,6},{6,5},{7,0},{8,15},{9,10},{10,... | collective-permute-start | bytes 196616 | tf_op jit(solution)/shard_map/ppermute | solution.py:284
  35.1 14.2 %copy-start.1 = (f32[4,8,96,128]{3,2,1,0:T(8,128)S(1)}, f32[4,8,96,128]{3,2,1,0:T(8,128)}, u32[]{:S(2)}) copy-start(f32[4,8,96,128]{3,2,1,0:T(8,128)} %y.5) | copy-start | bytes 4718596
  35.1 14.2 %collective-permute-start.5 = (f32[4,8,8,128]{3,2,1,0:T(8,128)S(1)}, f32[4,8,8,128]{3,2,1,0:T(8,128)S(1)}, u32[]{:S(2)}, u32[]{:S(2)}) collective-permute-start(f32[4,8,8,128]{3,2,1,0:T(8,128)S(1)} %get-tuple-element.13), channel_id=1, source_target_pairs={{128,0},{256,128},{384,256},{0,384},{129,1},{257,129},{385,257},{1... | collective-permute-start | bytes 393224 | tf_op jit(solution)/shard_map/ppermute | solution.py:288
  39.9 9.4 %collective-permute-start.4 = (f32[4,8,8,128]{3,2,1,0:T(8,128)S(1)}, f32[4,8,8,128]{3,2,1,0:T(8,128)S(1)}, u32[]{:S(2)}, u32[]{:S(2)}) collective-permute-start(f32[4,8,8,128]{3,2,1,0:T(8,128)S(1)} %get-tuple-element.13), channel_id=1, source_target_pairs={{0,128},{128,256},{256,384},{384,0},{1,129},{129,257},{257,385},{3... | collective-permute-start | bytes 393224 | tf_op jit(solution)/shard_map/ppermute | solution.py:287
  73.7 10.5 %collective-permute-start.6 = (f32[640,128]{1,0:T(8,128)S(1)}, f32[640,128]{1,0:T(8,128)S(1)}, u32[]{:S(2)}, u32[]{:S(2)}) collective-permute-start(f32[640,128]{1,0:T(8,128)S(1)} %get-tuple-element.15), channel_id=1, source_target_pairs={{0,8},{8,0},{1,9},{9,1},{2,10},{10,2},{3,11},{11,3},{4,12},{12,4},... | collective-permute-start | bytes 983048 | tf_op jit(solution)/shard_map/ppermute | solution.py:292
  132.4 8.3 %copy-start.3 = (f32[16,40,128]{2,1,0:T(8,128)}, f32[16,40,128]{2,1,0:T(8,128)S(1)}, u32[]{:S(2)}) copy-start(f32[16,40,128]{2,1,0:T(8,128)S(1)} %all_to_all.29) | copy-start | bytes 983044
  132.4 8.3 %collective-permute-start.7 = (f32[640,128]{1,0:T(8,128)S(1)}, f32[640,128]{1,0:T(8,128)S(1)}, u32[]{:S(2)}, u32[]{:S(2)}) collective-permute-start(f32[640,128]{1,0:T(8,128)S(1)} %bitcast.4), channel_id=1, source_target_pairs={{0,8},{8,0},{1,9},{9,1},{2,10},{10,2},{3,11},{11,3},{4,12},{12,4},... | collective-permute-start | bytes 983048 | tf_op jit(solution)/shard_map/ppermute | solution.py:298
  140.7 0.7 copy-start.4

commit v7 on v6

--- a/solution.py
+++ b/solution.py
@@ -93,7 +93,7 @@
     return diff, nu
 
 
-def along_z_body(y, vel, za, zb, out, rate, pad):
+def along_z_body(y, vel, base, za, zb, out, rate, pad):
     count, rows, depth, width = y.shape
     half = lax.axis_index("zhi")
     for j in range(rows):
@@ -117,7 +117,7 @@
                 term = (0.25 * C1[k - 1]) * (ahead - behind)
                 first = term if first is None else first + term
                 second = second + C2[k] * (ahead + behind)
-            out[s, j] = centre + (diff * second - vel[2, j] * first + nu * rate[j])
+            out[s, j] = (centre + base[s, j]) + (diff * second - vel[2, j] * first + nu * rate[j])
         return carry
 
     lax.fori_loop(0, count, species, 0)
@@ -135,14 +135,11 @@
             pltpu.VMEM((rows, depth + 16, width), jnp.float32),
         ],
         compiler_params=pltpu.CompilerParams(vmem_limit_bytes=24 * MIB),
-        cost_estimate=pl.CostEstimate(
-            flops=10**9, bytes_accessed=10**7, transcendentals=0
-        ),
         name="along_z",
     )(y, *rest)
 
 
-def along_xy_body(y, vel, base, outer, inner, xlow, xhigh, out, side, dx, pad):
+def along_xy_body(y, vel, outer, inner, xlow, xhigh, out, side, dx, pad):
     count, rows, depth, width = y.shape
     core = lax.axis_index("core")
     below = lanes() % 8 < 4
@@ -170,7 +167,7 @@
                 first = term if first is None else first + term
                 second = second + C2[k] * (ahead + behind)
             moved = (0.25 * vel[0, j]) * dx[j * depth : (j + 1) * depth, :width]
-            out[s, j] = base[s, j] + (diff * second - (moved + vel[1, j] * first))
+            out[s, j] = diff * second - (moved + vel[1, j] * first)
         return carry
 
     lax.fori_loop(0, count, species, 0)
@@ -189,6 +186,9 @@
             pltpu.VMEM((rows + 8, depth, width), jnp.float32),
         ],
         compiler_params=pltpu.CompilerParams(vmem_limit_bytes=32 * MIB),
+        cost_estimate=pl.CostEstimate(
+            flops=10**9, bytes_accessed=10**7, transcendentals=0
+        ),
         name="along_xy",
     )(y, *rest)
 
@@ -286,8 +286,8 @@
     outer = lax.ppermute(outer, gy, cross(16))
     xlow = lax.ppermute(xs, gx, up)
     xhigh = lax.ppermute(xs, gx, [(target, source) for source, target in up])
-    base = along_z(y, vel, za, zb)
-    updated = along_xy(y, vel, base, outer, inner, xlow, xhigh)
+    base = along_xy(y, vel, outer, inner, xlow, xhigh)
+    updated = along_z(y, vel, base, za, zb)
     mine, other = gram_blocks(exchange(updated.reshape(4, species * rows * depth // 4, width), gx))
     mine = mine + lax.ppermute(other, "core", swap)
     plane = ("gx", "x")

time: 144 us -> 145 us (level)
  starting transfers between devices: 55.3 us -> 49.7 us
  blocking collectives: 66.6 us -> 70.8 us
    ppermute x1, starting transfers between devices: 9.28 us -> 3.84 us  [shards(): mine = mine + lax.ppermute(other, 'core', swap)]
    all_to_all x5, blocking collectives: 66.6 us -> 70.8 us  [exchange(): return lax.all_to_all(pieces, axes, split_axis=0, concat_axis=0, tiled=True)]
  transfers between devices with their start and end apart: 8 -> 8, of which waited for: 3 -> 3; matrix products, arithmetic and copies ran while one was open for 0% -> 0% of each run, Pallas kernels for 1% -> 2%
where the time goes in v7:
time: 145 us; the launch traced here: 144 us
  blocking collectives  70.8 us (49%)
  starting transfers between devices  49.7 us (34%)
  Pallas kernels  10.4 us (7%)
  waiting for transfers between devices  8.77 us (6%)
  local copies, waits for them, and re-layouts  3.45 us (2%)
    all_to_all x5, blocking collectives, exchange(): return lax.all_to_all(pieces, axes, split_axis=0, concat_axis=0, tiled=True)  70.8 us
    ppermute x1, starting transfers between devices, shards(): inner = lax.ppermute(inner, 'core', swap)  11.1 us
    ppermute x1, starting transfers between devices, shards(): zb = lax.ppermute(zb, gz, cross(8))  8.25 us
    ppermute x1, starting transfers between devices, shards(): za = lax.ppermute(za, 'zhi', swap)  7.94 us
    ppermute x1, starting transfers between devices, shards(): other = lax.ppermute(mine, 'core', swap)  7.11 us
    ppermute x1, waiting for transfers between devices, shards(): zb = lax.ppermute(zb, gz, cross(8))  6.29 us
    ppermute x1, starting transfers between devices, shards(): outer = lax.ppermute(outer, gy, cross(16))  4.94 us
    ppermute x1, starting transfers between devices, shards(): xhigh = lax.ppermute(xs, gx, [(target, source) for source, target in up])  4.64 us
  transfers between devices with their start and end apart: 8, of which 3 were waited for; matrix products, arithmetic and copies ran while one was open for 0% of the time, Pallas kernels for 2%

profile of v7, /device:TPU:1, one launch (start us, length us, event | category | flops | bytes accessed | tf_op | source)
XLA Modules:
  0.0 144.1 jit_solution(699871389594167831)
XLA Ops:
  0.6 0.0 copy-start
  0.6 1.4 copy-done
  2.0 0.0 copy-start.1
  2.0 0.8 pack.1
  2.8 4.9 %collective-permute-start = (f32[4,4,96,128]{3,2,1,0:T(8,128)S(1)}, f32[4,4,96,128]{3,2,1,0:T(8,128)S(1)}, u32[]{:S(2)}, u32[]{:S(2)}) collective-permute-start(f32[4,4,96,128]{3,2,1,0:T(8,128)S(1)} %get-tuple-element.9), channel_id=1, source_target_pairs={{0,120},{8,16},{16,8},{24,32},{32,24},{40,48},{48,40},{56,64},{64,... | collective-permute-start | bytes 2359304 | tf_op jit(solution)/shard_map/ppermute | solution.py:286
  7.8 11.1 %collective-permute-start.1 = (f32[4,4,96,128]{3,2,1,0:T(8,128)S(1)}, f32[4,4,96,128]{3,2,1,0:T(8,128)S(1)}, u32[]{:S(2)}, u32[]{:S(2)}) collective-permute-start(f32[4,4,96,128]{3,2,1,0:T(8,128)S(1)} %get-tuple-element.10), channel_id=1, source_target_pairs={{0,8},{8,0},{1,9},{9,1},{2,10},{10,2},{3,11},{11,3},{4,12},{12,4},... | collective-permute-start | bytes 2359304 | tf_op jit(solution)/shard_map/ppermute | solution.py:285
  18.9 4.6 %collective-permute-start.3 = (f32[4,8,8,128]{3,2,1,0:T(8,128)S(1)}, f32[4,8,8,128]{3,2,1,0:T(8,128)S(1)}, u32[]{:S(2)}, u32[]{:S(2)}) collective-permute-start(f32[4,8,8,128]{3,2,1,0:T(8,128)S(1)} %get-tuple-element.11), channel_id=1, source_target_pairs={{128,0},{256,128},{384,256},{0,384},{129,1},{257,129},{385,257},{1... | collective-permute-start | bytes 393224 | tf_op jit(solution)/shard_map/ppermute | solution.py:288
  23.5 1.9 %collective-permute-start.2 = (f32[4,8,8,128]{3,2,1,0:T(8,128)S(1)}, f32[4,8,8,128]{3,2,1,0:T(8,128)S(1)}, u32[]{:S(2)}, u32[]{:S(2)}) collective-permute-start(f32[4,8,8,128]{3,2,1,0:T(8,128)S(1)} %get-tuple-element.11), channel_id=1, source_target_pairs={{0,128},{128,256},{256,384},{384,0},{1,129},{129,257},{257,385},{3... | collective-permute-start | bytes 393224 | tf_op jit(solution)/shard_map/ppermute | solution.py:287
  25.4 7.9 %collective-permute-start.4 = (f32[4,4,8,128]{3,2,1,0:T(8,128)S(1)}, f32[4,4,8,128]{3,2,1,0:T(8,128)S(1)}, u32[]{:S(2)}, u32[]{:S(2)}) collective-permute-start(f32[4,4,8,128]{3,2,1,0:T(8,128)S(1)} %get-tuple-element.12), channel_id=1, source_target_pairs={{0,1},{1,0},{2,3},{3,2},{4,5},{5,4},{6,7},{7,6},{8,9},{9,8},{10,11... | collective-permute-start | bytes 196616 | tf_op jit(solution)/shard_map/ppermute | solution.py:283
  33.4 0.0 collective-permute-done.3.xhigh
  33.4 8.3 %collective-permute-start.5 = (f32[4,4,8,128]{3,2,1,0:T(8,128)S(1)}, f32[4,4,8,128]{3,2,1,0:T(8,128)S(1)}, u32[]{:S(2)}, u32[]{:S(2)}) collective-permute-start(f32[4,4,8,128]{3,2,1,0:T(8,128)S(1)} %get-tuple-element.13), channel_id=1, source_target_pairs={{0,7},{1,2},{2,1},{3,4},{4,3},{5,6},{6,5},{7,0},{8,15},{9,10},{10,... | collective-permute-start | bytes 196616 | tf_op jit(solution)/shard_map/ppermute | solution.py:284
  41.7 0.0 collective-permute-done.2.xlow
  41.7 0.0 collective-permute-done.outer
  41.7 0.0 collective-permute-done.1.inner
  41.7 0.0 copy-done.1
  41.7 0.0 copy-start.2
  41.7 1.3 copy-done.2
  43.0 3.2 %along_xy.1.base = f32[4,8,96,128]{3,2,1,0:T(8,128)S(1)} custom-call(f32[4,8,96,128]{3,2,1,0:T(8,128)S(1)} %copy-done.1, f32[3,8,96,128]{3,2,1,0:T(8,128)S(1)} %copy-done.2, f32[4,4,96,128]{3,2,1,0:T(8,128)S(1)} %collective-permute-done.outer, f32[4,4,96,128]{3,2,1,0:T(8,128)S(1)} %collective-permute-done.1.inner, ...), custom_call_target="tpu_custom_call" | custom-call | flops 1000000000 | bytes 10000000 | tf_op jit(solution)/shard_map/along_xy/pallas_call | solution.py:178
  46.2 0.0 collective-permute-done.4.za
  46.2 6.3 %collective-permute-done.5.zb = f32[4,4,8,128]{3,2,1,0:T(8,128)S(1)} collective-permute-done((f32[4,4,8,128]{3,2,1,0:T(8,128)S(1)}, f32[4,4,8,128]{3,2,1,0:T(8,128)S(1)}, u32[]{:S(2)}, u32[]{:S(2)}) %collective-permute-start.5) | collective-permute-done | bytes 65568 | tf_op jit(solution)/shard_map/ppermute | solution.py:284
  52.5 3.1 %along_z.1 = f32[4,8,96,128]{3,2,1,0:T(8,128)} custom-call(f32[4,8,96,128]{3,2,1,0:T(8,128)S(1)} %copy-done.1, f32[3,8,96,128]{3,2,1,0:T(8,128)S(1)} %copy-done.2, f32[4,8,96,128]{3,2,1,0:T(8,128)S(1)} %along_xy.1.base, f32[4,4,8,128]{3,2,1,0:T(8,128)S(1)} %collective-permute-done.4.za, f32[4,4,8,128]{3,2,1,0:T(8,128)S(1)} %collective-permute-done.5.zb), custom_call_target="tpu_custom_call" | custom-call | tf_op jit(solution)/shard_map/along_z/pallas_call | solution.py:128
  55.6 23.8 %all_to_all.25.lines = f32[4,768,128]{2,1,0:T(8,128)S(1)} all-to-all(f32[4,768,128]{2,1,0:T(8,128)} %bitcast.3), channel_id=1, replica_groups=mesh['gx'=4,'zpair'=2,'znear'=4,'core'=2,'x'=4,'zhi'=2] {'gx'}, dimensions={0} | all-to-all | bytes 3145728 | tf_op jit(solution)/shard_map/all_to_all | solution.py:266
  79.4 1.5 %gram.1 = (f32[640,128]{1,0:T(8,128)S(1)}, f32[640,128]{1,0:T(8,128)S(1)}) custom-call(f32[4,768,128]{2,1,0:T(8,128)S(1)} %all_to_all.25.lines), custom_call_target="tpu_custom_call" | custom-call | tf_op jit(solution)/shard_map/gram/pallas_call | solution.py:214
  80.8 3.8 %collective-permute-start.6 = (f32[640,128]{1,0:T(8,128)S(1)}, f32[640,128]{1,0:T(8,128)S(1)}, u32[]{:S(2)}, u32[]{:S(2)}) collective-permute-start(f32[640,128]{1,0:T(8,128)S(1)} %get-tuple-element.15), channel_id=1, source_target_pairs={{0,8},{8,0},{1,9},{9,1},{2,10},{10,2},{3,11},{11,3},{4,12},{12,4},... | collective-permute-start | bytes 983048 | tf_op jit(solution)/shard_map/ppermute | solution.py:292
  84.7 1.2 collective-permute-done.6
  86.0 11.6 %all_to_all.26 = f32[16,40,128]{2,1,0:T(8,128)S(1)} all-to-all(f32[16,40,128]{2,1,0:T(8,128)S(1)} %bitcast.6), channel_id=1, replica_groups=mesh['gx'=4,'zpair'=2,'znear'=4,'core'=2,'x'=4,'zhi'=2] {'gx','x'}, dimensions={0} | all-to-all | bytes 655360 | tf_op jit(solution)/shard_map/all_to_all | solution.py:266
  97.6 7.0 %all_to_all.27 = f32[4,40,128]{2,1,0:T(8,128)S(1)} all-to-all(f32[4,40,128]{2,1,0:T(8,128)S(1)} %broadcast_in_dim.9), channel_id=1, replica_groups=mesh['gx'=4,'zpair'=2,'znear'=4,'core'=2,'x'=4,'zhi'=2] {'znear'}, dimensions={0} | all-to-all | bytes 163840 | tf_op jit(solution)/shard_map/all_to_all | solution.py:266
  104.6 17.6 %all_to_all.28 = f32[4,40,128]{2,1,0:T(8,128)S(1)} all-to-all(f32[4,40,128]{2,1,0:T(8,128)S(1)} %broadcast_in_dim.10), channel_id=1, replica_groups=mesh['gx'=4,'zpair'=2,'znear'=4,'core'=2,'x'=4,'zhi'=2] {'zpair','zhi'}, dimensions={0} | all-to-all | bytes 163840 | tf_op jit(solution)/shard_map/all_to_all | solution.py:266
  122.3 10.8 %all_to_all.29 = f32[16,40,128]{2,1,0:T(8,128)S(1)} all-to-all(f32[16,40,128]{2,1,0:T(8,128)S(1)} %broadcast_in_dim.11), channel_id=1, replica_groups=mesh['gx'=4,'zpair'=2,'znear'=4,'core'=2,'x'=4,'zhi'=2] {'gx','x'}, dimensions={0} | all-to-all | bytes 655360 | tf_op jit(solution)/shard_map/all_to_all | solution.py:266
  133.1 0.0 copy-start.3
  133.1 7.1 %collective-permute-start.7 = (f32[640,128]{1,0:T(8,128)S(1)}, f32[640,128]{1,0:T(8,128)S(1)}, u32[]{:S(2)}, u32[]{:S(2)}) collective-permute-start(f32[640,128]{1,0:T(8,128)S(1)} %bitcast.4), channel_id=1, source_target_pairs={{0,8},{8,0},{1,9},{9,1},{2,10},{10,2},{3,11},{11,3},{4,12},{12,4},... | collective-permute-start | bytes 983048 | tf_op jit(solution)/shard_map/ppermute | solution.py:298
  140.2 1.2 collective-permute-done.7.other
  141.5 0.0 copy-done.3
  141.5 0.0 copy-start.4
  141.5 0.7 copy-done.4
  142.2 1.9 %gram_rows.1 = f32[128,512]{1,0:T(8,128)} custom-call(f32[640,128]{1,0:T(8,128)} %bitcast.5, f32[640,128]{1,0:T(8,128)} %copy-done.4), custom_call_target="tpu_custom_call" | custom-call | tf_op jit(solution)/shard_map/gram_rows/pallas_call | solution.py:252
  (7 shorter events, 0.1 us)
Async XLA Ops:
  0.6 1.4 copy-start
  2.0 39.6 %copy-start.1 = (f32[4,8,96,128]{3,2,1,0:T(8,128)S(1)}, f32[4,8,96,128]{3,2,1,0:T(8,128)}, u32[]{:S(2)}) copy-start(f32[4,8,96,128]{3,2,1,0:T(8,128)} %y.5) | copy-start | bytes 4718596
  2.8 38.8 %collective-permute-start = (f32[4,4,96,128]{3,2,1,0:T(8,128)S(1)}, f32[4,4,96,128]{3,2,1,0:T(8,128)S(1)}, u32[]{:S(2)}, u32[]{:S(2)}) collective-permute-start(f32[4,4,96,128]{3,2,1,0:T(8,128)S(1)} %get-tuple-element.9), channel_id=1, source_target_pairs={{0,120},{8,16},{16,8},{24,32},{32,24},{40,48},{48,40},{56,64},{64,... | collective-permute-start | bytes 2359304 | tf_op jit(solution)/shard_map/ppermute | solution.py:286
  7.8 33.9 %collective-permute-start.1 = (f32[4,4,96,128]{3,2,1,0:T(8,128)S(1)}, f32[4,4,96,128]{3,2,1,0:T(8,128)S(1)}, u32[]{:S(2)}, u32[]{:S(2)}) collective-permute-start(f32[4,4,96,128]{3,2,1,0:T(8,128)S(1)} %get-tuple-element.10), channel_id=1, source_target_pairs={{0,8},{8,0},{1,9},{9,1},{2,10},{10,2},{3,11},{11,3},{4,12},{12,4},... | collective-permute-start | bytes 2359304 | tf_op jit(solution)/shard_map/ppermute | solution.py:285
  18.9 14.5 %collective-permute-start.3 = (f32[4,8,8,128]{3,2,1,0:T(8,128)S(1)}, f32[4,8,8,128]{3,2,1,0:T(8,128)S(1)}, u32[]{:S(2)}, u32[]{:S(2)}) collective-permute-start(f32[4,8,8,128]{3,2,1,0:T(8,128)S(1)} %get-tuple-element.11), channel_id=1, source_target_pairs={{128,0},{256,128},{384,256},{0,384},{129,1},{257,129},{385,257},{1... | collective-permute-start | bytes 393224 | tf_op jit(solution)/shard_map/ppermute | solution.py:288
  23.5 18.1 %collective-permute-start.2 = (f32[4,8,8,128]{3,2,1,0:T(8,128)S(1)}, f32[4,8,8,128]{3,2,1,0:T(8,128)S(1)}, u32[]{:S(2)}, u32[]{:S(2)}) collective-permute-start(f32[4,8,8,128]{3,2,1,0:T(8,128)S(1)} %get-tuple-element.11), channel_id=1, source_target_pairs={{0,128},{128,256},{256,384},{384,0},{1,129},{129,257},{257,385},{3... | collective-permute-start | bytes 393224 | tf_op jit(solution)/shard_map/ppermute | solution.py:287
  25.4 20.7 %collective-permute-start.4 = (f32[4,4,8,128]{3,2,1,0:T(8,128)S(1)}, f32[4,4,8,128]{3,2,1,0:T(8,128)S(1)}, u32[]{:S(2)}, u32[]{:S(2)}) collective-permute-start(f32[4,4,8,128]{3,2,1,0:T(8,128)S(1)} %get-tuple-element.12), channel_id=1, source_target_pairs={{0,1},{1,0},{2,3},{3,2},{4,5},{5,4},{6,7},{7,6},{8,9},{9,8},{10,11... | collective-permute-start | bytes 196616 | tf_op jit(solution)/shard_map/ppermute | solution.py:283
  33.4 19.1 %collective-permute-start.5 = (f32[4,4,8,128]{3,2,1,0:T(8,128)S(1)}, f32[4,4,8,128]{3,2,1,0:T(8,128)S(1)}, u32[]{:S(2)}, u32[]{:S(2)}) collective-permute-start(f32[4,4,8,128]{3,2,1,0:T(8,128)S(1)} %get-tuple-element.13), channel_id=1, source_target_pairs={{0,7},{1,2},{2,1},{3,4},{4,3},{5,6},{6,5},{7,0},{8,15},{9,10},{10,... | collective-permute-start | bytes 196616 | tf_op jit(solution)/shard_map/ppermute | solution.py:284
  41.7 1.3 copy-start.2
  80.8 5.1 %collective-permute-start.6 = (f32[640,128]{1,0:T(8,128)S(1)}, f32[640,128]{1,0:T(8,128)S(1)}, u32[]{:S(2)}, u32[]{:S(2)}) collective-permute-start(f32[640,128]{1,0:T(8,128)S(1)} %get-tuple-element.15), channel_id=1, source_target_pairs={{0,8},{8,0},{1,9},{9,1},{2,10},{10,2},{3,11},{11,3},{4,12},{12,4},... | collective-permute-start | bytes 983048 | tf_op jit(solution)/shard_map/ppermute | solution.py:292
  133.1 8.4 %copy-start.3 = (f32[16,40,128]{2,1,0:T(8,128)}, f32[16,40,128]{2,1,0:T(8,128)S(1)}, u32[]{:S(2)}) copy-start(f32[16,40,128]{2,1,0:T(8,128)S(1)} %all_to_all.29) | copy-start | bytes 983044
  133.1 8.3 %collective-permute-start.7 = (f32[640,128]{1,0:T(8,128)S(1)}, f32[640,128]{1,0:T(8,128)S(1)}, u32[]{:S(2)}, u32[]{:S(2)}) collective-permute-start(f32[640,128]{1,0:T(8,128)S(1)} %bitcast.4), channel_id=1, source_target_pairs={{0,8},{8,0},{1,9},{9,1},{2,10},{10,2},{3,11},{11,3},{4,12},{12,4},... | collective-permute-start | bytes 983048 | tf_op jit(solution)/shard_map/ppermute | solution.py:298
  141.5 0.7 copy-start.4

commit v8 on v7

--- a/solution.py
+++ b/solution.py
@@ -44,19 +44,20 @@
     return lax.broadcasted_iota(jnp.int32, (8, 128), 1)
 
 
-def pack_body(y, inner, outer, za, zb, xs):
+def pack_body(y, inner, outer, keep, xs):
     count, rows, depth, width = y.shape
     core, half = lax.axis_index("core"), lax.axis_index("zhi")
     lane = lanes()
 
     def species(s, carry):
-        inner[s] = y[s, pl.ds(4 * (1 - core), 4)]
+        swap = 4 * depth
+        inner[s, 0:swap] = y[s, pl.ds(4 * (1 - core), 4)].reshape(swap, width)
         outer[s] = y[s, pl.ds(4 * core, 4)]
         for j in range(rows):
             low, high = y[s, j, 0:4], y[s, j, depth - 4 :]
-            at = 4 * (j % 2)
-            za[s, j // 2, at : at + 4] = jnp.where(half == 0, high, low)
-            zb[s, j // 2, at : at + 4] = jnp.where(half == 0, low, high)
+            at = 4 * j
+            keep[s, at : at + 4] = jnp.where(half == core, high, low)
+            inner[s, swap + at : swap + at + 4] = jnp.where(half == core, low, high)
             packed = jnp.zeros((8, width), jnp.float32)
             for g in range(depth // 8):
                 turned = pltpu.roll(y[s, j, 8 * g : 8 * g + 8], 8 * g + 4, 1)
@@ -72,13 +73,13 @@
 
 def pack(y):
     count, rows, depth, width = y.shape
-    shapes = [(count, 4, depth, width)] * 2 + [(count, rows // 2, 8, width)] * 2
-    shapes = shapes + [(count, rows, 8, width)]
+    shapes = [(count, 4 * depth + 4 * rows, width), (count, 4, depth, width)]
+    shapes = shapes + [(count, 4 * rows, width), (count, rows, 8, width)]
     return pl.pallas_call(
         pack_body,
         out_shape=[jax.ShapeDtypeStruct(shape, jnp.float32) for shape in shapes],
         in_specs=[VMEM],
-        out_specs=[VMEM] * 5,
+        out_specs=[VMEM] * 4,
         compiler_params=pltpu.CompilerParams(vmem_limit_bytes=24 * MIB),
         name="pack",
     )(y)
@@ -93,9 +94,9 @@
     return diff, nu
 
 
-def along_z_body(y, vel, base, za, zb, out, rate, pad):
+def along_z_body(y, vel, base, direct, carried, out, rate, pad):
     count, rows, depth, width = y.shape
-    half = lax.axis_index("zhi")
+    apart = lax.axis_index("zhi") != lax.axis_index("core")
     for j in range(rows):
         heat = 1.0 + 3.0 * y[2, j]
         rate[j] = y[0, j] * y[1, j] * jnp.exp(-3.0 / heat)
@@ -103,11 +104,11 @@
     def species(s, carry):
         diff, nu = factors(s, count)
         for j in range(rows):
-            at = 4 * (j % 2)
-            fa, fb = za[s, j // 2, at : at + 4], zb[s, j // 2, at : at + 4]
-            pad[j, 4:8] = jnp.where(half == 0, fb, fa)
+            at = 4 * j
+            fa, fb = direct[0, s, at : at + 4], carried[s, at : at + 4]
+            pad[j, 4:8] = jnp.where(apart, fa, fb)
             pad[j, 8 : 8 + depth] = y[s, j]
-            pad[j, 8 + depth : 12 + depth] = jnp.where(half == 0, fa, fb)
+            pad[j, 8 + depth : 12 + depth] = jnp.where(apart, fb, fa)
         for j in range(rows):
             centre = y[s, j]
             first = None
@@ -147,7 +148,7 @@
 
     def species(s, carry):
         diff, _ = factors(s, count)
-        pad[pl.ds(12 * (1 - core), 4)] = inner[s]
+        pad[pl.ds(12 * (1 - core), 4)] = inner[s, 0 : 4 * depth].reshape(4, depth, width)
         pad[pl.ds(12 * core, 4)] = outer[s]
         pad[4 : 4 + rows] = y[s]
         for j in range(rows):
@@ -273,21 +274,23 @@
 def shards(y, vel):
     species, rows, depth, width = y.shape
     gy, gz, gx = ("zpair", "znear", "core"), ("x", "zhi"), ("gx",)
-    inner, outer, za, zb, xs = pack(y)
+    inner, outer, keep, xs = pack(y)
 
     def cross(count):
         return [(i, (i + 1) % count if i % 2 else (i - 1) % count) for i in range(count)]
 
     up = [(i, (i + 1) % 4) for i in range(4)]
     swap = [(0, 1), (1, 0)]
-    za = lax.ppermute(za, "zhi", swap)
-    zb = lax.ppermute(zb, gz, cross(8))
+    outer = lax.ppermute(outer, gy, cross(16))
     inner = lax.ppermute(inner, "core", swap)
-    outer = lax.ppermute(outer, gy, cross(16))
     xlow = lax.ppermute(xs, gx, up)
     xhigh = lax.ppermute(xs, gx, [(target, source) for source, target in up])
+    pairs = [(i, i ^ 1) for i in range(8)] + [(8 + i, 8 + j) for i, j in cross(8)]
+    faces = jnp.stack([keep, inner[:, 4 * depth :]])
+    faces = lax.ppermute(faces, ("core",) + gz, pairs)
+    carried = lax.ppermute(faces[1], "core", swap)
     base = along_xy(y, vel, outer, inner, xlow, xhigh)
-    updated = along_z(y, vel, base, za, zb)
+    updated = along_z(y, vel, base, faces, carried)
     mine, other = gram_blocks(exchange(updated.reshape(4, species * rows * depth // 4, width), gx))
     mine = mine + lax.ppermute(other, "core", swap)
     plane = ("gx", "x")

time: 145 us -> 151 us (1.041)
  waiting for transfers between devices: 8.77 us -> 14.3 us
    ppermute x2, waiting for transfers between devices: 6.29 us -> 11.8 us  [the longest x1 11.8 us: shards(): faces = lax.ppermute(faces, ('core',) + gz, pairs)]
    ppermute x2, starting transfers between devices: 16.2 us -> 21.6 us  [the longest x1 12.9 us: shards(): faces = lax.ppermute(faces, ('core',) + gz, pairs)]
    ppermute x1, starting transfers between devices: 4.94 us -> 1.92 us  [shards(): outer = lax.ppermute(outer, gy, cross(16))]
    ppermute x1, starting transfers between devices: 11.1 us -> 8.79 us  [shards(): inner = lax.ppermute(inner, 'core', swap)]
  transfers between devices with their start and end apart: 8 -> 8, of which waited for: 3 -> 4; matrix products, arithmetic and copies ran while one was open for 0% -> 0% of each run, Pallas kernels for 2% -> 2%
where the time goes in v8:
time: 151 us; the launch traced here: 150 us
  blocking collectives  71.7 us (47%)
  starting transfers between devices  49.2 us (33%)
  waiting for transfers between devices  14.3 us (9%)
  Pallas kernels  10.5 us (7%)
  local copies, waits for them, and re-layouts  3.46 us (2%)
    all_to_all x5, blocking collectives, exchange(): return lax.all_to_all(pieces, axes, split_axis=0, concat_axis=0, tiled=True)  71.7 us
    ppermute x1, starting transfers between devices, shards(): faces = lax.ppermute(faces, ('core',) + gz, pairs)  12.9 us
    ppermute x1, waiting for transfers between devices, shards(): faces = lax.ppermute(faces, ('core',) + gz, pairs)  11.8 us
    ppermute x1, starting transfers between devices, shards(): inner = lax.ppermute(inner, 'core', swap)  8.79 us
    ppermute x1, starting transfers between devices, shards(): carried = lax.ppermute(faces[1], 'core', swap)  8.72 us
    ppermute x1, starting transfers between devices, shards(): other = lax.ppermute(mine, 'core', swap)  7.35 us
    ppermute x1, starting transfers between devices, shards(): xhigh = lax.ppermute(xs, gx, [(target, source) for source, target in up])  4.64 us
    unnamed x10, local copies, waits for them, and re-layouts  3.41 us
  transfers between devices with their start and end apart: 8, of which 4 were waited for; matrix products, arithmetic and copies ran while one was open for 0% of the time, Pallas kernels for 2%

profile of v8, /device:TPU:1, one launch (start us, length us, event | category | flops | bytes accessed | tf_op | source)
XLA Modules:
  0.0 150.1 jit_solution(12333565683196417679)
XLA Ops:
  0.6 0.0 copy-start
  0.6 1.4 copy-done
  2.0 0.0 copy-start.1
  2.0 0.8 pack.1
  2.8 8.8 %collective-permute-start.1 = (f32[4,416,128]{2,1,0:T(8,128)S(1)}, f32[4,416,128]{2,1,0:T(8,128)S(1)}, u32[]{:S(2)}, u32[]{:S(2)}) collective-permute-start(f32[4,416,128]{2,1,0:T(8,128)S(1)} %get-tuple-element.9), channel_id=1, source_target_pairs={{0,8},{8,0},{1,9},{9,1},{2,10},{10,2},{3,11},{11,3},{4,12},{12,4},... | collective-permute-start | bytes 2555912 | tf_op jit(solution)/shard_map/ppermute | solution.py:285
  11.6 1.9 %collective-permute-start = (f32[4,4,96,128]{3,2,1,0:T(8,128)S(1)}, f32[4,4,96,128]{3,2,1,0:T(8,128)S(1)}, u32[]{:S(2)}, u32[]{:S(2)}) collective-permute-start(f32[4,4,96,128]{3,2,1,0:T(8,128)S(1)} %get-tuple-element.8), channel_id=1, source_target_pairs={{0,120},{8,16},{16,8},{24,32},{32,24},{40,48},{48,40},{56,64},{64,... | collective-permute-start | bytes 2359304 | tf_op jit(solution)/shard_map/ppermute | solution.py:284
  13.6 0.1 collective-permute-done.1.inner
  13.6 12.9 %collective-permute-start.4 = (f32[2,4,32,128]{3,2,1,0:T(8,128)S(1)}, f32[2,4,32,128]{3,2,1,0:T(8,128)S(1)}, u32[]{:S(2)}, u32[]{:S(2)}) collective-permute-start(f32[2,4,32,128]{3,2,1,0:T(8,128)S(1)} %pad_maximum_fusion), channel_id=1, source_target_pairs={{0,1},{1,0},{2,3},{3,2},{4,5},{5,4},{6,7},{7,6},{8,15},{9,10},{10,... | collective-permute-start | bytes 393224 | tf_op jit(solution)/shard_map/ppermute | solution.py:290
  26.5 4.6 %collective-permute-start.3 = (f32[4,8,8,128]{3,2,1,0:T(8,128)S(1)}, f32[4,8,8,128]{3,2,1,0:T(8,128)S(1)}, u32[]{:S(2)}, u32[]{:S(2)}) collective-permute-start(f32[4,8,8,128]{3,2,1,0:T(8,128)S(1)} %get-tuple-element.10), channel_id=1, source_target_pairs={{128,0},{256,128},{384,256},{0,384},{129,1},{257,129},{385,257},{1... | collective-permute-start | bytes 393224 | tf_op jit(solution)/shard_map/ppermute | solution.py:287
  31.1 1.9 %collective-permute-start.2 = (f32[4,8,8,128]{3,2,1,0:T(8,128)S(1)}, f32[4,8,8,128]{3,2,1,0:T(8,128)S(1)}, u32[]{:S(2)}, u32[]{:S(2)}) collective-permute-start(f32[4,8,8,128]{3,2,1,0:T(8,128)S(1)} %get-tuple-element.10), channel_id=1, source_target_pairs={{0,128},{128,256},{256,384},{384,0},{1,129},{129,257},{257,385},{3... | collective-permute-start | bytes 393224 | tf_op jit(solution)/shard_map/ppermute | solution.py:286
  33.1 11.8 %collective-permute-done.4.direct = f32[2,4,32,128]{3,2,1,0:T(8,128)S(1)} collective-permute-done((f32[2,4,32,128]{3,2,1,0:T(8,128)S(1)}, f32[2,4,32,128]{3,2,1,0:T(8,128)S(1)}, u32[]{:S(2)}, u32[]{:S(2)}) %collective-permute-start.4) | collective-permute-done | bytes 131104 | tf_op jit(solution)/shard_map/ppermute | solution.py:290
  44.9 8.7 %collective-permute-start.5 = (f32[4,32,128]{2,1,0:T(8,128)S(1)}, f32[4,32,128]{2,1,0:T(8,128)S(1)}, u32[]{:S(2)}, u32[]{:S(2)}) collective-permute-start(f32[4,32,128]{2,1,0:T(8,128)S(1)} %slice_bitcast_fusion), channel_id=1, source_target_pairs={{0,8},{8,0},{1,9},{9,1},{2,10},{10,2},{3,11},{11,3},{4,12},{12,4},... | collective-permute-start | bytes 196616 | tf_op jit(solution)/shard_map/ppermute | solution.py:291
  53.6 0.0 collective-permute-done.3.xhigh
  53.6 0.0 collective-permute-done.2.xlow
  53.6 0.0 collective-permute-done.outer
  53.6 0.0 copy-done.1
  53.7 0.0 copy-start.2
  53.7 1.3 copy-done.2
  54.9 3.3 %along_xy.1.base = f32[4,8,96,128]{3,2,1,0:T(8,128)S(1)} custom-call(f32[4,8,96,128]{3,2,1,0:T(8,128)S(1)} %copy-done.1, f32[3,8,96,128]{3,2,1,0:T(8,128)S(1)} %copy-done.2, f32[4,4,96,128]{3,2,1,0:T(8,128)S(1)} %collective-permute-done.outer, f32[4,416,128]{2,1,0:T(8,128)S(1)} %collective-permute-done.1.inner, ...), custom_call_target="tpu_custom_call" | custom-call | flops 1000000000 | bytes 10000000 | tf_op jit(solution)/shard_map/along_xy/pallas_call | solution.py:179
  58.2 0.0 collective-permute-done.5.carried
  58.2 3.1 %along_z.1 = f32[4,8,96,128]{3,2,1,0:T(8,128)} custom-call(f32[4,8,96,128]{3,2,1,0:T(8,128)S(1)} %copy-done.1, f32[3,8,96,128]{3,2,1,0:T(8,128)S(1)} %copy-done.2, f32[4,8,96,128]{3,2,1,0:T(8,128)S(1)} %along_xy.1.base, f32[2,4,32,128]{3,2,1,0:T(8,128)S(1)} %collective-permute-done.4.direct, f32[4,32,128]{2,1,0:T(8,128)S(1)} %collective-permute-done.5.carried), custom_call_target="tpu_custom_call" | custom-call | tf_op jit(solution)/shard_map/along_z/pallas_call | solution.py:129
  61.3 25.0 %all_to_all.25.lines = f32[4,768,128]{2,1,0:T(8,128)S(1)} all-to-all(f32[4,768,128]{2,1,0:T(8,128)} %bitcast.9), channel_id=1, replica_groups=mesh['gx'=4,'zpair'=2,'znear'=4,'core'=2,'x'=4,'zhi'=2] {'gx'}, dimensions={0} | all-to-all | bytes 3145728 | tf_op jit(solution)/shard_map/all_to_all | solution.py:267
  86.4 1.5 gram.1
  87.8 3.0 %collective-permute-start.6 = (f32[640,128]{1,0:T(8,128)S(1)}, f32[640,128]{1,0:T(8,128)S(1)}, u32[]{:S(2)}, u32[]{:S(2)}) collective-permute-start(f32[640,128]{1,0:T(8,128)S(1)} %get-tuple-element.13), channel_id=1, source_target_pairs={{0,8},{8,0},{1,9},{9,1},{2,10},{10,2},{3,11},{11,3},{4,12},{12,4},... | collective-permute-start | bytes 983048 | tf_op jit(solution)/shard_map/ppermute | solution.py:295
  90.9 1.2 collective-permute-done.6
  92.2 13.4 %all_to_all.26 = f32[16,40,128]{2,1,0:T(8,128)S(1)} all-to-all(f32[16,40,128]{2,1,0:T(8,128)S(1)} %bitcast.12), channel_id=1, replica_groups=mesh['gx'=4,'zpair'=2,'znear'=4,'core'=2,'x'=4,'zhi'=2] {'gx','x'}, dimensions={0} | all-to-all | bytes 655360 | tf_op jit(solution)/shard_map/all_to_all | solution.py:267
  105.6 7.0 %all_to_all.27 = f32[4,40,128]{2,1,0:T(8,128)S(1)} all-to-all(f32[4,40,128]{2,1,0:T(8,128)S(1)} %broadcast_in_dim.9), channel_id=1, replica_groups=mesh['gx'=4,'zpair'=2,'znear'=4,'core'=2,'x'=4,'zhi'=2] {'znear'}, dimensions={0} | all-to-all | bytes 163840 | tf_op jit(solution)/shard_map/all_to_all | solution.py:267
  112.6 15.7 %all_to_all.28 = f32[4,40,128]{2,1,0:T(8,128)S(1)} all-to-all(f32[4,40,128]{2,1,0:T(8,128)S(1)} %broadcast_in_dim.10), channel_id=1, replica_groups=mesh['gx'=4,'zpair'=2,'znear'=4,'core'=2,'x'=4,'zhi'=2] {'zpair','zhi'}, dimensions={0} | all-to-all | bytes 163840 | tf_op jit(solution)/shard_map/all_to_all | solution.py:267
  128.4 10.5 %all_to_all.29 = f32[16,40,128]{2,1,0:T(8,128)S(1)} all-to-all(f32[16,40,128]{2,1,0:T(8,128)S(1)} %broadcast_in_dim.11), channel_id=1, replica_groups=mesh['gx'=4,'zpair'=2,'znear'=4,'core'=2,'x'=4,'zhi'=2] {'gx','x'}, dimensions={0} | all-to-all | bytes 655360 | tf_op jit(solution)/shard_map/all_to_all | solution.py:267
  138.9 0.0 copy-start.3
  138.9 7.3 %collective-permute-start.7 = (f32[640,128]{1,0:T(8,128)S(1)}, f32[640,128]{1,0:T(8,128)S(1)}, u32[]{:S(2)}, u32[]{:S(2)}) collective-permute-start(f32[640,128]{1,0:T(8,128)S(1)} %bitcast.10), channel_id=1, source_target_pairs={{0,8},{8,0},{1,9},{9,1},{2,10},{10,2},{3,11},{11,3},{4,12},{12,4},... | collective-permute-start | bytes 983048 | tf_op jit(solution)/shard_map/ppermute | solution.py:301
  146.3 1.2 collective-permute-done.7.other
  147.5 0.0 copy-done.3
  147.5 0.0 copy-start.4
  147.5 0.7 copy-done.4
  148.2 1.9 %gram_rows.1 = f32[128,512]{1,0:T(8,128)} custom-call(f32[640,128]{1,0:T(8,128)} %bitcast.11, f32[640,128]{1,0:T(8,128)} %copy-done.4), custom_call_target="tpu_custom_call" | custom-call | tf_op jit(solution)/shard_map/gram_rows/pallas_call | solution.py:253
  (10 shorter events, 0.1 us)
Async XLA Ops:
  0.6 1.4 copy-start
  2.0 51.6 %copy-start.1 = (f32[4,8,96,128]{3,2,1,0:T(8,128)S(1)}, f32[4,8,96,128]{3,2,1,0:T(8,128)}, u32[]{:S(2)}) copy-start(f32[4,8,96,128]{3,2,1,0:T(8,128)} %y.5) | copy-start | bytes 4718596
  2.8 10.8 %collective-permute-start.1 = (f32[4,416,128]{2,1,0:T(8,128)S(1)}, f32[4,416,128]{2,1,0:T(8,128)S(1)}, u32[]{:S(2)}, u32[]{:S(2)}) collective-permute-start(f32[4,416,128]{2,1,0:T(8,128)S(1)} %get-tuple-element.9), channel_id=1, source_target_pairs={{0,8},{8,0},{1,9},{9,1},{2,10},{10,2},{3,11},{11,3},{4,12},{12,4},... | collective-permute-start | bytes 2555912 | tf_op jit(solution)/shard_map/ppermute | solution.py:285
  11.6 42.0 %collective-permute-start = (f32[4,4,96,128]{3,2,1,0:T(8,128)S(1)}, f32[4,4,96,128]{3,2,1,0:T(8,128)S(1)}, u32[]{:S(2)}, u32[]{:S(2)}) collective-permute-start(f32[4,4,96,128]{3,2,1,0:T(8,128)S(1)} %get-tuple-element.8), channel_id=1, source_target_pairs={{0,120},{8,16},{16,8},{24,32},{32,24},{40,48},{48,40},{56,64},{64,... | collective-permute-start | bytes 2359304 | tf_op jit(solution)/shard_map/ppermute | solution.py:284
  13.6 31.3 %collective-permute-start.4 = (f32[2,4,32,128]{3,2,1,0:T(8,128)S(1)}, f32[2,4,32,128]{3,2,1,0:T(8,128)S(1)}, u32[]{:S(2)}, u32[]{:S(2)}) collective-permute-start(f32[2,4,32,128]{3,2,1,0:T(8,128)S(1)} %pad_maximum_fusion), channel_id=1, source_target_pairs={{0,1},{1,0},{2,3},{3,2},{4,5},{5,4},{6,7},{7,6},{8,15},{9,10},{10,... | collective-permute-start | bytes 393224 | tf_op jit(solution)/shard_map/ppermute | solution.py:290
  26.5 27.1 %collective-permute-start.3 = (f32[4,8,8,128]{3,2,1,0:T(8,128)S(1)}, f32[4,8,8,128]{3,2,1,0:T(8,128)S(1)}, u32[]{:S(2)}, u32[]{:S(2)}) collective-permute-start(f32[4,8,8,128]{3,2,1,0:T(8,128)S(1)} %get-tuple-element.10), channel_id=1, source_target_pairs={{128,0},{256,128},{384,256},{0,384},{129,1},{257,129},{385,257},{1... | collective-permute-start | bytes 393224 | tf_op jit(solution)/shard_map/ppermute | solution.py:287
  31.1 22.5 %collective-permute-start.2 = (f32[4,8,8,128]{3,2,1,0:T(8,128)S(1)}, f32[4,8,8,128]{3,2,1,0:T(8,128)S(1)}, u32[]{:S(2)}, u32[]{:S(2)}) collective-permute-start(f32[4,8,8,128]{3,2,1,0:T(8,128)S(1)} %get-tuple-element.10), channel_id=1, source_target_pairs={{0,128},{128,256},{256,384},{384,0},{1,129},{129,257},{257,385},{3... | collective-permute-start | bytes 393224 | tf_op jit(solution)/shard_map/ppermute | solution.py:286
  44.9 13.4 %collective-permute-start.5 = (f32[4,32,128]{2,1,0:T(8,128)S(1)}, f32[4,32,128]{2,1,0:T(8,128)S(1)}, u32[]{:S(2)}, u32[]{:S(2)}) collective-permute-start(f32[4,32,128]{2,1,0:T(8,128)S(1)} %slice_bitcast_fusion), channel_id=1, source_target_pairs={{0,8},{8,0},{1,9},{9,1},{2,10},{10,2},{3,11},{11,3},{4,12},{12,4},... | collective-permute-start | bytes 196616 | tf_op jit(solution)/shard_map/ppermute | solution.py:291
  53.7 1.3 copy-start.2
  87.8 4.3 %collective-permute-start.6 = (f32[640,128]{1,0:T(8,128)S(1)}, f32[640,128]{1,0:T(8,128)S(1)}, u32[]{:S(2)}, u32[]{:S(2)}) collective-permute-start(f32[640,128]{1,0:T(8,128)S(1)} %get-tuple-element.13), channel_id=1, source_target_pairs={{0,8},{8,0},{1,9},{9,1},{2,10},{10,2},{3,11},{11,3},{4,12},{12,4},... | collective-permute-start | bytes 983048 | tf_op jit(solution)/shard_map/ppermute | solution.py:295
  138.9 8.6 %copy-start.3 = (f32[16,40,128]{2,1,0:T(8,128)}, f32[16,40,128]{2,1,0:T(8,128)S(1)}, u32[]{:S(2)}) copy-start(f32[16,40,128]{2,1,0:T(8,128)S(1)} %all_to_all.29) | copy-start | bytes 983044
  138.9 8.6 %collective-permute-start.7 = (f32[640,128]{1,0:T(8,128)S(1)}, f32[640,128]{1,0:T(8,128)S(1)}, u32[]{:S(2)}, u32[]{:S(2)}) collective-permute-start(f32[640,128]{1,0:T(8,128)S(1)} %bitcast.10), channel_id=1, source_target_pairs={{0,8},{8,0},{1,9},{9,1},{2,10},{10,2},{3,11},{11,3},{4,12},{12,4},... | collective-permute-start | bytes 983048 | tf_op jit(solution)/shard_map/ppermute | solution.py:301
  147.5 0.7 copy-start.4

commit v9 on v6

--- a/solution.py
+++ b/solution.py
@@ -79,7 +79,7 @@
         out_shape=[jax.ShapeDtypeStruct(shape, jnp.float32) for shape in shapes],
         in_specs=[VMEM],
         out_specs=[VMEM] * 5,
-        compiler_params=pltpu.CompilerParams(vmem_limit_bytes=24 * MIB),
+        compiler_params=pltpu.CompilerParams(vmem_limit_bytes=14 * MIB),
         name="pack",
     )(y)
 
@@ -134,7 +134,7 @@
             pltpu.VMEM((rows, depth, width), jnp.float32),
             pltpu.VMEM((rows, depth + 16, width), jnp.float32),
         ],
-        compiler_params=pltpu.CompilerParams(vmem_limit_bytes=24 * MIB),
+        compiler_params=pltpu.CompilerParams(vmem_limit_bytes=14 * MIB),
         cost_estimate=pl.CostEstimate(
             flops=10**9, bytes_accessed=10**7, transcendentals=0
         ),
@@ -142,7 +142,7 @@
     )(y, *rest)
 
 
-def along_xy_body(y, vel, base, outer, inner, xlow, xhigh, out, side, dx, pad):
+def along_xy_body(y, vel, base, outer, inner, xlow, xhigh, result, side, dx, pad, out, sems):
     count, rows, depth, width = y.shape
     core = lax.axis_index("core")
     below = lanes() % 8 < 4
@@ -171,9 +171,12 @@
                 second = second + C2[k] * (ahead + behind)
             moved = (0.25 * vel[0, j]) * dx[j * depth : (j + 1) * depth, :width]
             out[s, j] = base[s, j] + (diff * second - (moved + vel[1, j] * first))
+        pltpu.make_async_copy(out.at[s], result.at[s], sems.at[s]).start()
         return carry
 
     lax.fori_loop(0, count, species, 0)
+    for s in range(count):
+        pltpu.make_async_copy(out.at[s], result.at[s], sems.at[s]).wait()
 
 
 def along_xy(y, *rest):
@@ -182,13 +185,15 @@
         along_xy_body,
         out_shape=jax.ShapeDtypeStruct(y.shape, jnp.float32),
         in_specs=[VMEM] * (1 + len(rest)),
-        out_specs=VMEM,
+        out_specs=pl.BlockSpec(memory_space=pl.ANY),
         scratch_shapes=[
             pltpu.VMEM((rows * depth, width), jnp.float32),
             pltpu.VMEM((rows * depth, 2 * width), jnp.float32),
             pltpu.VMEM((rows + 8, depth, width), jnp.float32),
+            pltpu.VMEM(y.shape, jnp.float32),
+            pltpu.SemaphoreType.DMA((y.shape[0],)),
         ],
-        compiler_params=pltpu.CompilerParams(vmem_limit_bytes=32 * MIB),
+        compiler_params=pltpu.CompilerParams(vmem_limit_bytes=16 * MIB),
         name="along_xy",
     )(y, *rest)
 
@@ -216,7 +221,7 @@
         out_shape=[jax.ShapeDtypeStruct((len(PAIRS) * 64, 128), jnp.float32)] * 2,
         in_specs=[VMEM],
         out_specs=[VMEM] * 2,
-        compiler_params=pltpu.CompilerParams(vmem_limit_bytes=40 * MIB),
+        compiler_params=pltpu.CompilerParams(vmem_limit_bytes=16 * MIB),
         name="gram",
     )(lines)
 
@@ -258,6 +263,7 @@
             pltpu.VMEM((4, 128, 128), jnp.float32),
             pltpu.SemaphoreType.DMA((4,)),
         ],
+        compiler_params=pltpu.CompilerParams(vmem_limit_bytes=8 * MIB),
         name="gram_rows",
     )(mine, other)
 

time: 144 us -> 142 us (0.986)
  no operation moved by 1% of the time
where the time goes in v9:
time: 142 us
  blocking collectives  66.8 us (47%)
  starting transfers between devices  54.9 us (39%)
  Pallas kernels  9.63 us (7%)
  waiting for transfers between devices  8.07 us (6%)
  local copies, waits for them, and re-layouts  1.45 us (1%)
    all_to_all x5, blocking collectives, exchange(): return lax.all_to_all(pieces, axes, split_axis=0, concat_axis=0, tiled=True)  66.8 us
    ppermute x1, starting transfers between devices, shards(): inner = lax.ppermute(inner, 'core', swap)  11.1 us
    ppermute x1, starting transfers between devices, shards(): mine = mine + lax.ppermute(other, 'core', swap)  8.96 us
    ppermute x1, starting transfers between devices, shards(): zb = lax.ppermute(zb, gz, cross(8))  8.25 us
    ppermute x1, starting transfers between devices, shards(): za = lax.ppermute(za, 'zhi', swap)  7.94 us
    ppermute x1, starting transfers between devices, shards(): other = lax.ppermute(mine, 'core', swap)  7.08 us
    ppermute x1, waiting for transfers between devices, shards(): zb = lax.ppermute(zb, gz, cross(8))  5.59 us
    ppermute x1, starting transfers between devices, shards(): outer = lax.ppermute(outer, gy, cross(16))  4.94 us
  transfers between devices with their start and end apart: 8, of which 3 were waited for; matrix products, arithmetic and copies ran while one was open for 0% of the time, Pallas kernels for 1%

profile of v9, /device:TPU:1, one launch (start us, length us, event | category | flops | bytes accessed | tf_op | source)
XLA Modules:
  0.0 141.8 jit_solution(3357037073102985458)
XLA Ops:
  0.6 0.0 copy-start
  0.6 1.4 copy-done
  2.0 0.0 copy-start.2
  2.0 0.8 pack.1
  2.8 4.9 %collective-permute-start.2 = (f32[4,4,96,128]{3,2,1,0:T(8,128)S(1)}, f32[4,4,96,128]{3,2,1,0:T(8,128)S(1)}, u32[]{:S(2)}, u32[]{:S(2)}) collective-permute-start(f32[4,4,96,128]{3,2,1,0:T(8,128)S(1)} %get-tuple-element.11), channel_id=1, source_target_pairs={{0,120},{8,16},{16,8},{24,32},{32,24},{40,48},{48,40},{56,64},{64,... | collective-permute-start | bytes 2359304 | tf_op jit(solution)/shard_map/ppermute | solution.py:292
  7.8 11.1 %collective-permute-start.3 = (f32[4,4,96,128]{3,2,1,0:T(8,128)S(1)}, f32[4,4,96,128]{3,2,1,0:T(8,128)S(1)}, u32[]{:S(2)}, u32[]{:S(2)}) collective-permute-start(f32[4,4,96,128]{3,2,1,0:T(8,128)S(1)} %get-tuple-element.12), channel_id=1, source_target_pairs={{0,8},{8,0},{1,9},{9,1},{2,10},{10,2},{3,11},{11,3},{4,12},{12,4},... | collective-permute-start | bytes 2359304 | tf_op jit(solution)/shard_map/ppermute | solution.py:291
  18.9 7.9 %collective-permute-start = (f32[4,4,8,128]{3,2,1,0:T(8,128)S(1)}, f32[4,4,8,128]{3,2,1,0:T(8,128)S(1)}, u32[]{:S(2)}, u32[]{:S(2)}) collective-permute-start(f32[4,4,8,128]{3,2,1,0:T(8,128)S(1)} %get-tuple-element.9), channel_id=1, source_target_pairs={{0,1},{1,0},{2,3},{3,2},{4,5},{5,4},{6,7},{7,6},{8,9},{9,8},{10,11... | collective-permute-start | bytes 196616 | tf_op jit(solution)/shard_map/ppermute | solution.py:289
  26.8 8.3 %collective-permute-start.1 = (f32[4,4,8,128]{3,2,1,0:T(8,128)S(1)}, f32[4,4,8,128]{3,2,1,0:T(8,128)S(1)}, u32[]{:S(2)}, u32[]{:S(2)}) collective-permute-start(f32[4,4,8,128]{3,2,1,0:T(8,128)S(1)} %get-tuple-element.10), channel_id=1, source_target_pairs={{0,7},{1,2},{2,1},{3,4},{4,3},{5,6},{6,5},{7,0},{8,15},{9,10},{10,... | collective-permute-start | bytes 196616 | tf_op jit(solution)/shard_map/ppermute | solution.py:290
  35.1 0.0 copy-start.1
  35.1 4.8 %collective-permute-start.5 = (f32[4,8,8,128]{3,2,1,0:T(8,128)S(1)}, f32[4,8,8,128]{3,2,1,0:T(8,128)S(1)}, u32[]{:S(2)}, u32[]{:S(2)}) collective-permute-start(f32[4,8,8,128]{3,2,1,0:T(8,128)S(1)} %get-tuple-element.13), channel_id=1, source_target_pairs={{128,0},{256,128},{384,256},{0,384},{129,1},{257,129},{385,257},{1... | collective-permute-start | bytes 393224 | tf_op jit(solution)/shard_map/ppermute | solution.py:294
  39.9 0.0 collective-permute-done.za
  39.9 1.9 %collective-permute-start.4 = (f32[4,8,8,128]{3,2,1,0:T(8,128)S(1)}, f32[4,8,8,128]{3,2,1,0:T(8,128)S(1)}, u32[]{:S(2)}, u32[]{:S(2)}) collective-permute-start(f32[4,8,8,128]{3,2,1,0:T(8,128)S(1)} %get-tuple-element.13), channel_id=1, source_target_pairs={{0,128},{128,256},{256,384},{384,0},{1,129},{129,257},{257,385},{3... | collective-permute-start | bytes 393224 | tf_op jit(solution)/shard_map/ppermute | solution.py:293
  41.8 5.6 %collective-permute-done.1.zb = f32[4,4,8,128]{3,2,1,0:T(8,128)S(1)} collective-permute-done((f32[4,4,8,128]{3,2,1,0:T(8,128)S(1)}, f32[4,4,8,128]{3,2,1,0:T(8,128)S(1)}, u32[]{:S(2)}, u32[]{:S(2)}) %collective-permute-start.1) | collective-permute-done | bytes 65568 | tf_op jit(solution)/shard_map/ppermute | solution.py:290
  47.4 0.0 copy-done.2
  47.4 1.9 %along_z.1.base = f32[4,8,96,128]{3,2,1,0:T(8,128)S(1)} custom-call(f32[4,8,96,128]{3,2,1,0:T(8,128)S(1)} %copy-done, f32[3,8,96,128]{3,2,1,0:T(8,128)S(1)} %copy-done.2, f32[4,4,8,128]{3,2,1,0:T(8,128)S(1)} %collective-permute-done.za, f32[4,4,8,128]{3,2,1,0:T(8,128)S(1)} %collective-permute-done.1.zb), custom_call_target="tpu_custom_call" | custom-call | flops 1000000000 | bytes 10000000 | tf_op jit(solution)/shard_map/along_z/pallas_call | solution.py:128
  49.3 0.0 collective-permute-done.5.xhigh
  49.3 0.0 collective-permute-done.4.xlow
  49.3 0.0 collective-permute-done.2.outer
  49.3 0.0 collective-permute-done.3.inner
  49.3 0.0 copy-done.1
  49.3 4.1 %along_xy.1 = f32[4,8,96,128]{3,2,1,0:T(8,128)} custom-call(f32[4,8,96,128]{3,2,1,0:T(8,128)S(1)} %copy-done.1, f32[3,8,96,128]{3,2,1,0:T(8,128)S(1)} %copy-done.2, f32[4,8,96,128]{3,2,1,0:T(8,128)S(1)} %along_z.1.base, f32[4,4,96,128]{3,2,1,0:T(8,128)S(1)} %collective-permute-done.2.outer, f32[4,4,96,128]{3,2,1,0:T(8,128)S(1)} %collective-permute-done.3.inner, ...), custom_call_target="tpu_custom_call" | custom-call | tf_op jit(solution)/shard_map/along_xy/pallas_call | solution.py:184
  53.4 18.8 %all_to_all.25.lines = f32[4,768,128]{2,1,0:T(8,128)S(1)} all-to-all(f32[4,768,128]{2,1,0:T(8,128)} %bitcast.5), channel_id=1, replica_groups=mesh['gx'=4,'zpair'=2,'znear'=4,'core'=2,'x'=4,'zhi'=2] {'gx'}, dimensions={0} | all-to-all | bytes 3145728 | tf_op jit(solution)/shard_map/all_to_all | solution.py:272
  72.2 1.4 %gram.1 = (f32[640,128]{1,0:T(8,128)S(1)}, f32[640,128]{1,0:T(8,128)S(1)}) custom-call(f32[4,768,128]{2,1,0:T(8,128)S(1)} %all_to_all.25.lines), custom_call_target="tpu_custom_call" | custom-call | tf_op jit(solution)/shard_map/gram/pallas_call | solution.py:219
  73.7 9.0 %collective-permute-start.6 = (f32[640,128]{1,0:T(8,128)S(1)}, f32[640,128]{1,0:T(8,128)S(1)}, u32[]{:S(2)}, u32[]{:S(2)}) collective-permute-start(f32[640,128]{1,0:T(8,128)S(1)} %get-tuple-element.15), channel_id=1, source_target_pairs={{0,8},{8,0},{1,9},{9,1},{2,10},{10,2},{3,11},{11,3},{4,12},{12,4},... | collective-permute-start | bytes 983048 | tf_op jit(solution)/shard_map/ppermute | solution.py:298
  82.7 1.2 collective-permute-done.6
  83.9 11.6 %all_to_all.26 = f32[16,40,128]{2,1,0:T(8,128)S(1)} all-to-all(f32[16,40,128]{2,1,0:T(8,128)S(1)} %bitcast.6), channel_id=1, replica_groups=mesh['gx'=4,'zpair'=2,'znear'=4,'core'=2,'x'=4,'zhi'=2] {'gx','x'}, dimensions={0} | all-to-all | bytes 655360 | tf_op jit(solution)/shard_map/all_to_all | solution.py:272
  95.6 7.1 %all_to_all.27 = f32[4,40,128]{2,1,0:T(8,128)S(1)} all-to-all(f32[4,40,128]{2,1,0:T(8,128)S(1)} %broadcast_in_dim.9), channel_id=1, replica_groups=mesh['gx'=4,'zpair'=2,'znear'=4,'core'=2,'x'=4,'zhi'=2] {'znear'}, dimensions={0} | all-to-all | bytes 163840 | tf_op jit(solution)/shard_map/all_to_all | solution.py:272
  102.7 18.4 %all_to_all.28 = f32[4,40,128]{2,1,0:T(8,128)S(1)} all-to-all(f32[4,40,128]{2,1,0:T(8,128)S(1)} %broadcast_in_dim.10), channel_id=1, replica_groups=mesh['gx'=4,'zpair'=2,'znear'=4,'core'=2,'x'=4,'zhi'=2] {'zpair','zhi'}, dimensions={0} | all-to-all | bytes 163840 | tf_op jit(solution)/shard_map/all_to_all | solution.py:272
  121.1 10.9 %all_to_all.29 = f32[16,40,128]{2,1,0:T(8,128)S(1)} all-to-all(f32[16,40,128]{2,1,0:T(8,128)S(1)} %broadcast_in_dim.11), channel_id=1, replica_groups=mesh['gx'=4,'zpair'=2,'znear'=4,'core'=2,'x'=4,'zhi'=2] {'gx','x'}, dimensions={0} | all-to-all | bytes 655360 | tf_op jit(solution)/shard_map/all_to_all | solution.py:272
  132.1 7.1 %collective-permute-start.7 = (f32[640,128]{1,0:T(8,128)S(1)}, f32[640,128]{1,0:T(8,128)S(1)}, u32[]{:S(2)}, u32[]{:S(2)}) collective-permute-start(f32[640,128]{1,0:T(8,128)S(1)} %bitcast.3), channel_id=1, source_target_pairs={{0,8},{8,0},{1,9},{9,1},{2,10},{10,2},{3,11},{11,3},{4,12},{12,4},... | collective-permute-start | bytes 983048 | tf_op jit(solution)/shard_map/ppermute | solution.py:304
  139.2 1.2 collective-permute-done.7.other
  140.4 1.4 %gram_rows.1 = f32[128,512]{1,0:T(8,128)} custom-call(f32[640,128]{1,0:T(8,128)S(1)} %bitcast.4, f32[640,128]{1,0:T(8,128)S(1)} %collective-permute-done.7.other), custom_call_target="tpu_custom_call" | custom-call | tf_op jit(solution)/shard_map/gram_rows/pallas_call | solution.py:257
  (7 shorter events, 0.1 us)
Async XLA Ops:
  0.6 1.4 copy-start
  2.0 45.3 %copy-start.2 = (f32[3,8,96,128]{3,2,1,0:T(8,128)S(1)}, f32[3,8,96,128]{3,2,1,0:T(8,128)}, u32[]{:S(2)}) copy-start(f32[3,8,96,128]{3,2,1,0:T(8,128)} %vel.3) | copy-start | bytes 3538948
  2.8 46.4 %collective-permute-start.2 = (f32[4,4,96,128]{3,2,1,0:T(8,128)S(1)}, f32[4,4,96,128]{3,2,1,0:T(8,128)S(1)}, u32[]{:S(2)}, u32[]{:S(2)}) collective-permute-start(f32[4,4,96,128]{3,2,1,0:T(8,128)S(1)} %get-tuple-element.11), channel_id=1, source_target_pairs={{0,120},{8,16},{16,8},{24,32},{32,24},{40,48},{48,40},{56,64},{64,... | collective-permute-start | bytes 2359304 | tf_op jit(solution)/shard_map/ppermute | solution.py:292
  7.8 41.5 %collective-permute-start.3 = (f32[4,4,96,128]{3,2,1,0:T(8,128)S(1)}, f32[4,4,96,128]{3,2,1,0:T(8,128)S(1)}, u32[]{:S(2)}, u32[]{:S(2)}) collective-permute-start(f32[4,4,96,128]{3,2,1,0:T(8,128)S(1)} %get-tuple-element.12), channel_id=1, source_target_pairs={{0,8},{8,0},{1,9},{9,1},{2,10},{10,2},{3,11},{11,3},{4,12},{12,4},... | collective-permute-start | bytes 2359304 | tf_op jit(solution)/shard_map/ppermute | solution.py:291
  18.9 21.0 %collective-permute-start = (f32[4,4,8,128]{3,2,1,0:T(8,128)S(1)}, f32[4,4,8,128]{3,2,1,0:T(8,128)S(1)}, u32[]{:S(2)}, u32[]{:S(2)}) collective-permute-start(f32[4,4,8,128]{3,2,1,0:T(8,128)S(1)} %get-tuple-element.9), channel_id=1, source_target_pairs={{0,1},{1,0},{2,3},{3,2},{4,5},{5,4},{6,7},{7,6},{8,9},{9,8},{10,11... | collective-permute-start | bytes 196616 | tf_op jit(solution)/shard_map/ppermute | solution.py:289
  26.8 20.6 %collective-permute-start.1 = (f32[4,4,8,128]{3,2,1,0:T(8,128)S(1)}, f32[4,4,8,128]{3,2,1,0:T(8,128)S(1)}, u32[]{:S(2)}, u32[]{:S(2)}) collective-permute-start(f32[4,4,8,128]{3,2,1,0:T(8,128)S(1)} %get-tuple-element.10), channel_id=1, source_target_pairs={{0,7},{1,2},{2,1},{3,4},{4,3},{5,6},{6,5},{7,0},{8,15},{9,10},{10,... | collective-permute-start | bytes 196616 | tf_op jit(solution)/shard_map/ppermute | solution.py:290
  35.1 14.2 %copy-start.1 = (f32[4,8,96,128]{3,2,1,0:T(8,128)S(1)}, f32[4,8,96,128]{3,2,1,0:T(8,128)}, u32[]{:S(2)}) copy-start(f32[4,8,96,128]{3,2,1,0:T(8,128)} %y.5) | copy-start | bytes 4718596
  35.1 14.2 %collective-permute-start.5 = (f32[4,8,8,128]{3,2,1,0:T(8,128)S(1)}, f32[4,8,8,128]{3,2,1,0:T(8,128)S(1)}, u32[]{:S(2)}, u32[]{:S(2)}) collective-permute-start(f32[4,8,8,128]{3,2,1,0:T(8,128)S(1)} %get-tuple-element.13), channel_id=1, source_target_pairs={{128,0},{256,128},{384,256},{0,384},{129,1},{257,129},{385,257},{1... | collective-permute-start | bytes 393224 | tf_op jit(solution)/shard_map/ppermute | solution.py:294
  39.9 9.4 %collective-permute-start.4 = (f32[4,8,8,128]{3,2,1,0:T(8,128)S(1)}, f32[4,8,8,128]{3,2,1,0:T(8,128)S(1)}, u32[]{:S(2)}, u32[]{:S(2)}) collective-permute-start(f32[4,8,8,128]{3,2,1,0:T(8,128)S(1)} %get-tuple-element.13), channel_id=1, source_target_pairs={{0,128},{128,256},{256,384},{384,0},{1,129},{129,257},{257,385},{3... | collective-permute-start | bytes 393224 | tf_op jit(solution)/shard_map/ppermute | solution.py:293
  73.7 10.2 %collective-permute-start.6 = (f32[640,128]{1,0:T(8,128)S(1)}, f32[640,128]{1,0:T(8,128)S(1)}, u32[]{:S(2)}, u32[]{:S(2)}) collective-permute-start(f32[640,128]{1,0:T(8,128)S(1)} %get-tuple-element.15), channel_id=1, source_target_pairs={{0,8},{8,0},{1,9},{9,1},{2,10},{10,2},{3,11},{11,3},{4,12},{12,4},... | collective-permute-start | bytes 983048 | tf_op jit(solution)/shard_map/ppermute | solution.py:298
  132.1 8.3 %collective-permute-start.7 = (f32[640,128]{1,0:T(8,128)S(1)}, f32[640,128]{1,0:T(8,128)S(1)}, u32[]{:S(2)}, u32[]{:S(2)}) collective-permute-start(f32[640,128]{1,0:T(8,128)S(1)} %bitcast.3), channel_id=1, source_target_pairs={{0,8},{8,0},{1,9},{9,1},{2,10},{10,2},{3,11},{11,3},{4,12},{12,4},... | collective-permute-start | bytes 983048 | tf_op jit(solution)/shard_map/ppermute | solution.py:304

commit v10 on v9

--- a/solution.py
+++ b/solution.py
@@ -93,12 +93,25 @@
     return diff, nu
 
 
-def along_z_body(y, vel, za, zb, out, rate, pad):
+def rates_body(y, out):
+    heat = 1.0 + 3.0 * y[2]
+    out[...] = y[0] * y[1] * jnp.exp(-3.0 / heat)
+
+
+def rates(y):
+    return pl.pallas_call(
+        rates_body,
+        out_shape=jax.ShapeDtypeStruct(y.shape[1:], jnp.float32),
+        in_specs=[VMEM],
+        out_specs=VMEM,
+        compiler_params=pltpu.CompilerParams(vmem_limit_bytes=14 * MIB),
+        name="rates",
+    )(y)
+
+
+def along_z_body(y, vel, rate, za, zb, out, pad):
     count, rows, depth, width = y.shape
     half = lax.axis_index("zhi")
-    for j in range(rows):
-        heat = 1.0 + 3.0 * y[2, j]
-        rate[j] = y[0, j] * y[1, j] * jnp.exp(-3.0 / heat)
 
     def species(s, carry):
         diff, nu = factors(s, count)
@@ -131,7 +144,6 @@
         in_specs=[VMEM] * (1 + len(rest)),
         out_specs=VMEM,
         scratch_shapes=[
-            pltpu.VMEM((rows, depth, width), jnp.float32),
             pltpu.VMEM((rows, depth + 16, width), jnp.float32),
         ],
         compiler_params=pltpu.CompilerParams(vmem_limit_bytes=14 * MIB),
@@ -292,7 +304,7 @@
     outer = lax.ppermute(outer, gy, cross(16))
     xlow = lax.ppermute(xs, gx, up)
     xhigh = lax.ppermute(xs, gx, [(target, source) for source, target in up])
-    base = along_z(y, vel, za, zb)
+    base = along_z(y, vel, rates(y), za, zb)
     updated = along_xy(y, vel, base, outer, inner, xlow, xhigh)
     mine, other = gram_blocks(exchange(updated.reshape(4, species * rows * depth // 4, width), gx))
     mine = mine + lax.ppermute(other, "core", swap)

time: 142 us -> 142 us (level)
  no operation moved by 1% of the time
where the time goes in v10:
time: 142 us
  blocking collectives  66.5 us (47%)
  starting transfers between devices  55.2 us (39%)
  Pallas kernels  9.63 us (7%)
  waiting for transfers between devices  8.08 us (6%)
  local copies, waits for them, and re-layouts  1.45 us (1%)
    all_to_all x5, blocking collectives, exchange(): return lax.all_to_all(pieces, axes, split_axis=0, concat_axis=0, tiled=True)  66.5 us
    ppermute x1, starting transfers between devices, shards(): inner = lax.ppermute(inner, 'core', swap)  11.1 us
    ppermute x1, starting transfers between devices, shards(): mine = mine + lax.ppermute(other, 'core', swap)  9.37 us
    ppermute x1, starting transfers between devices, shards(): zb = lax.ppermute(zb, gz, cross(8))  8.25 us
    ppermute x1, starting transfers between devices, shards(): za = lax.ppermute(za, 'zhi', swap)  7.94 us
    ppermute x1, starting transfers between devices, shards(): other = lax.ppermute(mine, 'core', swap)  7.08 us
    ppermute x1, waiting for transfers between devices, shards(): zb = lax.ppermute(zb, gz, cross(8))  5.59 us
    ppermute x1, starting transfers between devices, shards(): outer = lax.ppermute(outer, gy, cross(16))  4.94 us
  transfers between devices with their start and end apart: 8, of which 3 were waited for; matrix products, arithmetic and copies ran while one was open for 0% of the time, Pallas kernels for 1%

profile of v10, /device:TPU:1, one launch (start us, length us, event | category | flops | bytes accessed | tf_op | source)
XLA Modules:
  0.0 141.8 jit_solution(8657277032858639150)
XLA Ops:
  0.6 0.0 copy-start
  0.6 1.4 copy-done
  2.0 0.0 copy-start.2
  2.0 0.8 pack.1
  2.8 4.9 %collective-permute-start.2 = (f32[4,4,96,128]{3,2,1,0:T(8,128)S(1)}, f32[4,4,96,128]{3,2,1,0:T(8,128)S(1)}, u32[]{:S(2)}, u32[]{:S(2)}) collective-permute-start(f32[4,4,96,128]{3,2,1,0:T(8,128)S(1)} %get-tuple-element.11), channel_id=1, source_target_pairs={{0,120},{8,16},{16,8},{24,32},{32,24},{40,48},{48,40},{56,64},{64,... | collective-permute-start | bytes 2359304 | tf_op jit(solution)/shard_map/ppermute | solution.py:304
  7.8 11.1 %collective-permute-start.3 = (f32[4,4,96,128]{3,2,1,0:T(8,128)S(1)}, f32[4,4,96,128]{3,2,1,0:T(8,128)S(1)}, u32[]{:S(2)}, u32[]{:S(2)}) collective-permute-start(f32[4,4,96,128]{3,2,1,0:T(8,128)S(1)} %get-tuple-element.12), channel_id=1, source_target_pairs={{0,8},{8,0},{1,9},{9,1},{2,10},{10,2},{3,11},{11,3},{4,12},{12,4},... | collective-permute-start | bytes 2359304 | tf_op jit(solution)/shard_map/ppermute | solution.py:303
  18.9 7.9 %collective-permute-start = (f32[4,4,8,128]{3,2,1,0:T(8,128)S(1)}, f32[4,4,8,128]{3,2,1,0:T(8,128)S(1)}, u32[]{:S(2)}, u32[]{:S(2)}) collective-permute-start(f32[4,4,8,128]{3,2,1,0:T(8,128)S(1)} %get-tuple-element.9), channel_id=1, source_target_pairs={{0,1},{1,0},{2,3},{3,2},{4,5},{5,4},{6,7},{7,6},{8,9},{9,8},{10,11... | collective-permute-start | bytes 196616 | tf_op jit(solution)/shard_map/ppermute | solution.py:301
  26.8 8.3 %collective-permute-start.1 = (f32[4,4,8,128]{3,2,1,0:T(8,128)S(1)}, f32[4,4,8,128]{3,2,1,0:T(8,128)S(1)}, u32[]{:S(2)}, u32[]{:S(2)}) collective-permute-start(f32[4,4,8,128]{3,2,1,0:T(8,128)S(1)} %get-tuple-element.10), channel_id=1, source_target_pairs={{0,7},{1,2},{2,1},{3,4},{4,3},{5,6},{6,5},{7,0},{8,15},{9,10},{10,... | collective-permute-start | bytes 196616 | tf_op jit(solution)/shard_map/ppermute | solution.py:302
  35.1 4.6 %collective-permute-start.5 = (f32[4,8,8,128]{3,2,1,0:T(8,128)S(1)}, f32[4,8,8,128]{3,2,1,0:T(8,128)S(1)}, u32[]{:S(2)}, u32[]{:S(2)}) collective-permute-start(f32[4,8,8,128]{3,2,1,0:T(8,128)S(1)} %get-tuple-element.13), channel_id=1, source_target_pairs={{128,0},{256,128},{384,256},{0,384},{129,1},{257,129},{385,257},{1... | collective-permute-start | bytes 393224 | tf_op jit(solution)/shard_map/ppermute | solution.py:306
  39.7 0.0 collective-permute-done.za
  39.7 1.9 %collective-permute-start.4 = (f32[4,8,8,128]{3,2,1,0:T(8,128)S(1)}, f32[4,8,8,128]{3,2,1,0:T(8,128)S(1)}, u32[]{:S(2)}, u32[]{:S(2)}) collective-permute-start(f32[4,8,8,128]{3,2,1,0:T(8,128)S(1)} %get-tuple-element.13), channel_id=1, source_target_pairs={{0,128},{128,256},{256,384},{384,0},{1,129},{129,257},{257,385},{3... | collective-permute-start | bytes 393224 | tf_op jit(solution)/shard_map/ppermute | solution.py:305
  41.7 0.1 rates.1.rate
  41.8 0.0 copy-start.1
  41.8 5.6 %collective-permute-done.1.zb = f32[4,4,8,128]{3,2,1,0:T(8,128)S(1)} collective-permute-done((f32[4,4,8,128]{3,2,1,0:T(8,128)S(1)}, f32[4,4,8,128]{3,2,1,0:T(8,128)S(1)}, u32[]{:S(2)}, u32[]{:S(2)}) %collective-permute-start.1) | collective-permute-done | bytes 65568 | tf_op jit(solution)/shard_map/ppermute | solution.py:302
  47.4 0.0 copy-done.2
  47.4 1.7 %along_z.1.base = f32[4,8,96,128]{3,2,1,0:T(8,128)S(1)} custom-call(f32[4,8,96,128]{3,2,1,0:T(8,128)S(1)} %copy-done, f32[3,8,96,128]{3,2,1,0:T(8,128)S(1)} %copy-done.2, f32[8,96,128]{2,1,0:T(8,128)S(1)} %rates.1.rate, f32[4,4,8,128]{3,2,1,0:T(8,128)S(1)} %collective-permute-done.za, f32[4,4,8,128]{3,2,1,0:T(8,128)S(1)} %collective-permute-done.1.zb), custom_call_target="tpu_custom_call" | custom-call | flops 1000000000 | bytes 10000000 | tf_op jit(solution)/shard_map/along_z/pallas_call | solution.py:141
  49.1 0.0 collective-permute-done.5.xhigh
  49.2 0.0 collective-permute-done.4.xlow
  49.2 0.0 collective-permute-done.2.outer
  49.2 0.0 collective-permute-done.3.inner
  49.2 0.0 copy-done.1
  49.2 4.1 %along_xy.1 = f32[4,8,96,128]{3,2,1,0:T(8,128)} custom-call(f32[4,8,96,128]{3,2,1,0:T(8,128)S(1)} %copy-done.1, f32[3,8,96,128]{3,2,1,0:T(8,128)S(1)} %copy-done.2, f32[4,8,96,128]{3,2,1,0:T(8,128)S(1)} %along_z.1.base, f32[4,4,96,128]{3,2,1,0:T(8,128)S(1)} %collective-permute-done.2.outer, f32[4,4,96,128]{3,2,1,0:T(8,128)S(1)} %collective-permute-done.3.inner, ...), custom_call_target="tpu_custom_call" | custom-call | tf_op jit(solution)/shard_map/along_xy/pallas_call | solution.py:196
  53.3 18.4 %all_to_all.25.lines = f32[4,768,128]{2,1,0:T(8,128)S(1)} all-to-all(f32[4,768,128]{2,1,0:T(8,128)} %bitcast.5), channel_id=1, replica_groups=mesh['gx'=4,'zpair'=2,'znear'=4,'core'=2,'x'=4,'zhi'=2] {'gx'}, dimensions={0} | all-to-all | bytes 3145728 | tf_op jit(solution)/shard_map/all_to_all | solution.py:284
  71.7 1.5 %gram.1 = (f32[640,128]{1,0:T(8,128)S(1)}, f32[640,128]{1,0:T(8,128)S(1)}) custom-call(f32[4,768,128]{2,1,0:T(8,128)S(1)} %all_to_all.25.lines), custom_call_target="tpu_custom_call" | custom-call | tf_op jit(solution)/shard_map/gram/pallas_call | solution.py:231
  73.2 9.4 %collective-permute-start.6 = (f32[640,128]{1,0:T(8,128)S(1)}, f32[640,128]{1,0:T(8,128)S(1)}, u32[]{:S(2)}, u32[]{:S(2)}) collective-permute-start(f32[640,128]{1,0:T(8,128)S(1)} %get-tuple-element.15), channel_id=1, source_target_pairs={{0,8},{8,0},{1,9},{9,1},{2,10},{10,2},{3,11},{11,3},{4,12},{12,4},... | collective-permute-start | bytes 983048 | tf_op jit(solution)/shard_map/ppermute | solution.py:310
  82.6 1.2 collective-permute-done.6
  83.8 11.6 %all_to_all.26 = f32[16,40,128]{2,1,0:T(8,128)S(1)} all-to-all(f32[16,40,128]{2,1,0:T(8,128)S(1)} %bitcast.6), channel_id=1, replica_groups=mesh['gx'=4,'zpair'=2,'znear'=4,'core'=2,'x'=4,'zhi'=2] {'gx','x'}, dimensions={0} | all-to-all | bytes 655360 | tf_op jit(solution)/shard_map/all_to_all | solution.py:284
  95.5 7.1 %all_to_all.27 = f32[4,40,128]{2,1,0:T(8,128)S(1)} all-to-all(f32[4,40,128]{2,1,0:T(8,128)S(1)} %broadcast_in_dim.9), channel_id=1, replica_groups=mesh['gx'=4,'zpair'=2,'znear'=4,'core'=2,'x'=4,'zhi'=2] {'znear'}, dimensions={0} | all-to-all | bytes 163840 | tf_op jit(solution)/shard_map/all_to_all | solution.py:284
  102.6 18.5 %all_to_all.28 = f32[4,40,128]{2,1,0:T(8,128)S(1)} all-to-all(f32[4,40,128]{2,1,0:T(8,128)S(1)} %broadcast_in_dim.10), channel_id=1, replica_groups=mesh['gx'=4,'zpair'=2,'znear'=4,'core'=2,'x'=4,'zhi'=2] {'zpair','zhi'}, dimensions={0} | all-to-all | bytes 163840 | tf_op jit(solution)/shard_map/all_to_all | solution.py:284
  121.1 10.9 %all_to_all.29 = f32[16,40,128]{2,1,0:T(8,128)S(1)} all-to-all(f32[16,40,128]{2,1,0:T(8,128)S(1)} %broadcast_in_dim.11), channel_id=1, replica_groups=mesh['gx'=4,'zpair'=2,'znear'=4,'core'=2,'x'=4,'zhi'=2] {'gx','x'}, dimensions={0} | all-to-all | bytes 655360 | tf_op jit(solution)/shard_map/all_to_all | solution.py:284
  132.1 7.1 %collective-permute-start.7 = (f32[640,128]{1,0:T(8,128)S(1)}, f32[640,128]{1,0:T(8,128)S(1)}, u32[]{:S(2)}, u32[]{:S(2)}) collective-permute-start(f32[640,128]{1,0:T(8,128)S(1)} %bitcast.3), channel_id=1, source_target_pairs={{0,8},{8,0},{1,9},{9,1},{2,10},{10,2},{3,11},{11,3},{4,12},{12,4},... | collective-permute-start | bytes 983048 | tf_op jit(solution)/shard_map/ppermute | solution.py:316
  139.2 1.2 collective-permute-done.7.other
  140.4 1.4 %gram_rows.1 = f32[128,512]{1,0:T(8,128)} custom-call(f32[640,128]{1,0:T(8,128)S(1)} %bitcast.4, f32[640,128]{1,0:T(8,128)S(1)} %collective-permute-done.7.other), custom_call_target="tpu_custom_call" | custom-call | tf_op jit(solution)/shard_map/gram_rows/pallas_call | solution.py:269
  (7 shorter events, 0.1 us)
Async XLA Ops:
  0.6 1.4 copy-start
  2.0 45.3 %copy-start.2 = (f32[3,8,96,128]{3,2,1,0:T(8,128)S(1)}, f32[3,8,96,128]{3,2,1,0:T(8,128)}, u32[]{:S(2)}) copy-start(f32[3,8,96,128]{3,2,1,0:T(8,128)} %vel.3) | copy-start | bytes 3538948
  2.8 46.3 %collective-permute-start.2 = (f32[4,4,96,128]{3,2,1,0:T(8,128)S(1)}, f32[4,4,96,128]{3,2,1,0:T(8,128)S(1)}, u32[]{:S(2)}, u32[]{:S(2)}) collective-permute-start(f32[4,4,96,128]{3,2,1,0:T(8,128)S(1)} %get-tuple-element.11), channel_id=1, source_target_pairs={{0,120},{8,16},{16,8},{24,32},{32,24},{40,48},{48,40},{56,64},{64,... | collective-permute-start | bytes 2359304 | tf_op jit(solution)/shard_map/ppermute | solution.py:304
  7.8 41.4 %collective-permute-start.3 = (f32[4,4,96,128]{3,2,1,0:T(8,128)S(1)}, f32[4,4,96,128]{3,2,1,0:T(8,128)S(1)}, u32[]{:S(2)}, u32[]{:S(2)}) collective-permute-start(f32[4,4,96,128]{3,2,1,0:T(8,128)S(1)} %get-tuple-element.12), channel_id=1, source_target_pairs={{0,8},{8,0},{1,9},{9,1},{2,10},{10,2},{3,11},{11,3},{4,12},{12,4},... | collective-permute-start | bytes 2359304 | tf_op jit(solution)/shard_map/ppermute | solution.py:303
  18.9 20.9 %collective-permute-start = (f32[4,4,8,128]{3,2,1,0:T(8,128)S(1)}, f32[4,4,8,128]{3,2,1,0:T(8,128)S(1)}, u32[]{:S(2)}, u32[]{:S(2)}) collective-permute-start(f32[4,4,8,128]{3,2,1,0:T(8,128)S(1)} %get-tuple-element.9), channel_id=1, source_target_pairs={{0,1},{1,0},{2,3},{3,2},{4,5},{5,4},{6,7},{7,6},{8,9},{9,8},{10,11... | collective-permute-start | bytes 196616 | tf_op jit(solution)/shard_map/ppermute | solution.py:301
  26.8 20.6 %collective-permute-start.1 = (f32[4,4,8,128]{3,2,1,0:T(8,128)S(1)}, f32[4,4,8,128]{3,2,1,0:T(8,128)S(1)}, u32[]{:S(2)}, u32[]{:S(2)}) collective-permute-start(f32[4,4,8,128]{3,2,1,0:T(8,128)S(1)} %get-tuple-element.10), channel_id=1, source_target_pairs={{0,7},{1,2},{2,1},{3,4},{4,3},{5,6},{6,5},{7,0},{8,15},{9,10},{10,... | collective-permute-start | bytes 196616 | tf_op jit(solution)/shard_map/ppermute | solution.py:302
  35.1 14.1 %collective-permute-start.5 = (f32[4,8,8,128]{3,2,1,0:T(8,128)S(1)}, f32[4,8,8,128]{3,2,1,0:T(8,128)S(1)}, u32[]{:S(2)}, u32[]{:S(2)}) collective-permute-start(f32[4,8,8,128]{3,2,1,0:T(8,128)S(1)} %get-tuple-element.13), channel_id=1, source_target_pairs={{128,0},{256,128},{384,256},{0,384},{129,1},{257,129},{385,257},{1... | collective-permute-start | bytes 393224 | tf_op jit(solution)/shard_map/ppermute | solution.py:306
  39.7 9.4 %collective-permute-start.4 = (f32[4,8,8,128]{3,2,1,0:T(8,128)S(1)}, f32[4,8,8,128]{3,2,1,0:T(8,128)S(1)}, u32[]{:S(2)}, u32[]{:S(2)}) collective-permute-start(f32[4,8,8,128]{3,2,1,0:T(8,128)S(1)} %get-tuple-element.13), channel_id=1, source_target_pairs={{0,128},{128,256},{256,384},{384,0},{1,129},{129,257},{257,385},{3... | collective-permute-start | bytes 393224 | tf_op jit(solution)/shard_map/ppermute | solution.py:305
  41.8 7.4 %copy-start.1 = (f32[4,8,96,128]{3,2,1,0:T(8,128)S(1)}, f32[4,8,96,128]{3,2,1,0:T(8,128)}, u32[]{:S(2)}) copy-start(f32[4,8,96,128]{3,2,1,0:T(8,128)} %y.7) | copy-start | bytes 4718596
  73.2 10.6 %collective-permute-start.6 = (f32[640,128]{1,0:T(8,128)S(1)}, f32[640,128]{1,0:T(8,128)S(1)}, u32[]{:S(2)}, u32[]{:S(2)}) collective-permute-start(f32[640,128]{1,0:T(8,128)S(1)} %get-tuple-element.15), channel_id=1, source_target_pairs={{0,8},{8,0},{1,9},{9,1},{2,10},{10,2},{3,11},{11,3},{4,12},{12,4},... | collective-permute-start | bytes 983048 | tf_op jit(solution)/shard_map/ppermute | solution.py:310
  132.1 8.3 %collective-permute-start.7 = (f32[640,128]{1,0:T(8,128)S(1)}, f32[640,128]{1,0:T(8,128)S(1)}, u32[]{:S(2)}, u32[]{:S(2)}) collective-permute-start(f32[640,128]{1,0:T(8,128)S(1)} %bitcast.3), channel_id=1, source_target_pairs={{0,8},{8,0},{1,9},{9,1},{2,10},{10,2},{3,11},{11,3},{4,12},{12,4},... | collective-permute-start | bytes 983048 | tf_op jit(solution)/shard_map/ppermute | solution.py:316
